TPU v7x, 32 devices: a whole 2x2x4 slice. The times are simulated.
32 devices in a mesh: ctx: 16 (over z, y, x), fsdp: 2 (over core).
Axes of the slice: x: 2, y: 2, z: 4, core: 2. Of those that a mesh axis runs over, the one named last changes fastest.
Arguments:
- hidden_in: bfloat16 [2, 2048, 2048], P('fsdp', 'ctx'), may hold values from -6 to 6
- block_map: int32 [2, 32], P('fsdp'), may hold values from 0 to 31, as said below
- query_weight: bfloat16 [2048, 2048], P(('ctx', 'fsdp')), may hold values from -0.125 to 0.125
- key_weight: bfloat16 [2048, 1024], P(('ctx', 'fsdp')), may hold values from -0.125 to 0.125
- value_weight: bfloat16 [2048, 1024], P(('ctx', 'fsdp')), may hold values from -0.125 to 0.125
- out_weight: bfloat16 [2048, 2048], P(('ctx', 'fsdp')), may hold values from -0.5 to 0.5
- gate_weight: bfloat16 [2048, 6144], P(('ctx', 'fsdp')), may hold values from -0.125 to 0.125
- up_weight: bfloat16 [2048, 6144], P(('ctx', 'fsdp')), may hold values from -0.125 to 0.125
- down_weight: bfloat16 [2048, 6144], P(('ctx', 'fsdp')), may hold values from -0.109375 to 0.109375
- attention_norm_gain: bfloat16 [2048], P(('ctx', 'fsdp')), may hold values from 0.25 to 1.75
- feedforward_gain: bfloat16 [2048], P(('ctx', 'fsdp')), may hold values from 0.25 to 1.75
- query_gain: bfloat16 [128], replicated, may hold values from 1 to 2
- key_gain: bfloat16 [128], replicated, may hold values from 1 to 2
- output_grad: bfloat16 [2, 2048, 2048], P('fsdp', 'ctx'), may hold values from -6 to 6
Outputs:
- layer_out: bfloat16 [2, 2048, 2048], P('fsdp', 'ctx')
- input_grad: bfloat16 [2, 2048, 2048], P('fsdp', 'ctx')
- query_weight_grad: float32 [2048, 2048], P(('ctx', 'fsdp'))
- key_weight_grad: float32 [2048, 1024], P(('ctx', 'fsdp'))
- value_weight_grad: float32 [2048, 1024], P(('ctx', 'fsdp'))
- out_weight_grad: float32 [2048, 2048], P(('ctx', 'fsdp'))
- gate_weight_grad: float32 [2048, 6144], P(('ctx', 'fsdp'))
- up_weight_grad: float32 [2048, 6144], P(('ctx', 'fsdp'))
- down_weight_grad: float32 [2048, 6144], P(('ctx', 'fsdp'))
- attention_norm_gain_grad: float32 [2048], P(('ctx', 'fsdp'))
- feedforward_gain_grad: float32 [2048], P(('ctx', 'fsdp'))
- query_gain_grad: float32 [128], replicated
- key_gain_grad: float32 [128], replicated
Inputs may be any that keep to these rules, and one draw needn't show every extreme that they name: `block_map`: in each row, entries 2 d and 2 d + 1 are the blocks stored on ctx device d: a block c below 16, then 32 - 1 - c; every block appears once in a row.
All inputs are finite; a program needn't handle non-finite values.
Results may differ from a plain program's by a relative error of at most 0.017.
Values may be sent and summed in bfloat16 or wider, within the bound.
A program may use at most 704 MiB of HBM per device.

v0:
```python
import jax
import jax.numpy as jnp
from jax import lax
from jax.sharding import PartitionSpec as P

epsilon = 1e-06
rotary_base = 1000000.0
masked_score = -1e30


def norm_rows(values, gain):
    scale_row = lax.rsqrt(jnp.mean(values * values, axis=-1, keepdims=True) + epsilon)
    unit_rows = values * scale_row
    return (unit_rows * gain, unit_rows, scale_row)


def norm_back(grad_rows, unit_rows, scale_row, gain):
    weighted = grad_rows * gain
    inner_mean = jnp.mean(weighted * unit_rows, axis=-1, keepdims=True)
    return (scale_row * (weighted - unit_rows * inner_mean), grad_rows * unit_rows)


def rope_tables(positions, width):
    half_width = width // 2
    frequency = rotary_base ** (-(jnp.arange(half_width, dtype=jnp.float32) * 2.0 / width))
    angles = positions.astype(jnp.float32)[:, None] * frequency[None, :]
    angles = jnp.concatenate([angles, angles], axis=-1)
    return (jnp.cos(angles)[:, None, :], jnp.sin(angles)[:, None, :])


def rotate(values, cosine, sine_table):
    half_width = values.shape[-1] // 2
    turned = jnp.concatenate([-values[..., half_width:], values[..., :half_width]], axis=-1)
    return values * cosine + turned * sine_table


def rotate_back(grads, cosine, sine_table):
    half_width = grads.shape[-1] // 2
    shifted = grads * sine_table
    turned = jnp.concatenate([shifted[..., half_width:], -shifted[..., :half_width]], axis=-1)
    return grads * cosine + turned


def multiply(left, right):
    return jnp.dot(left, right, preferred_element_type=jnp.float32)


def multiply_trans(left, right):
    return lax.dot_general(
        left, right, (((1,), (1,)), ((), ())), preferred_element_type=jnp.float32
    )


def outer_rows(left, right):
    return lax.dot_general(
        left, right, (((0,), (0,)), ((), ())), preferred_element_type=jnp.float32
    )


def fetch_attention(query_weight, key_weight, value_weight, out_weight, attention_norm_gain):
    return (
        lax.all_gather(query_weight, ("ctx", "fsdp"), axis=0, tiled=True),
        lax.all_gather(key_weight, ("ctx", "fsdp"), axis=0, tiled=True),
        lax.all_gather(value_weight, ("ctx", "fsdp"), axis=0, tiled=True),
        lax.all_gather(out_weight, ("ctx", "fsdp"), axis=0, tiled=True),
        lax.all_gather(attention_norm_gain, ("ctx", "fsdp"), axis=0, tiled=True),
    )


def fetch_feedforward(gate_weight, up_weight, down_weight, feedforward_gain):
    return (
        lax.all_gather(gate_weight, ("ctx", "fsdp"), axis=0, tiled=True),
        lax.all_gather(up_weight, ("ctx", "fsdp"), axis=0, tiled=True),
        lax.all_gather(down_weight, ("ctx", "fsdp"), axis=0, tiled=True),
        lax.all_gather(feedforward_gain, ("ctx", "fsdp"), axis=0, tiled=True),
    )


def block_scores(queries, query_pos, key_block, pos_block, factor):
    scores = (
        jnp.einsum("rkgd,tkd->kgrt", queries, key_block, preferred_element_type=jnp.float32)
        * factor
    )
    allowed = pos_block[None, :] <= query_pos[:, None]
    return jnp.where(allowed[None, None], scores, masked_score)


def split_blocks(key_rows, value_rows, key_pos):
    key_count = key_rows.shape[0]
    block_size = min(512, key_count)
    block_count = key_count // block_size
    return (
        key_rows.reshape(block_count, block_size, key_rows.shape[1], key_rows.shape[2]),
        value_rows.reshape(block_count, block_size, value_rows.shape[1], value_rows.shape[2]),
        key_pos.reshape(block_count, block_size),
    )


def attend(queries, query_pos, key_rows, value_rows, key_pos):
    factor = queries.shape[-1] ** (-0.5)
    key_blocks, value_blocks, pos_blocks = split_blocks(key_rows, value_rows, key_pos)
    stat_shape = (queries.shape[1], queries.shape[2], queries.shape[0])

    def row_stats(running, pieces):
        row_best, summed = running
        scores = block_scores(queries, query_pos, pieces[0], pieces[1], factor)
        new_best = jnp.maximum(row_best, jnp.max(scores, axis=-1))
        summed = summed * jnp.exp(row_best - new_best) + jnp.sum(
            jnp.exp(scores - new_best[..., None]), axis=-1
        )
        return ((new_best, summed), None)

    initial = (jnp.full(stat_shape, masked_score, jnp.float32), jnp.zeros(stat_shape, jnp.float32))
    (row_best, summed), unused = lax.scan(row_stats, initial, (key_blocks, pos_blocks))

    def mix_values(accumulated, pieces):
        scores = block_scores(queries, query_pos, pieces[0], pieces[2], factor)
        weights = (jnp.exp(scores - row_best[..., None]) / summed[..., None]).astype(jnp.bfloat16)
        return (
            accumulated
            + jnp.einsum("kgrt,tkd->rkgd", weights, pieces[1], preferred_element_type=jnp.float32),
            None,
        )

    attended, unused = lax.scan(
        mix_values, jnp.zeros(queries.shape, jnp.float32), (key_blocks, value_blocks, pos_blocks)
    )
    return (attended, row_best, summed)


def attend_back(
    queries, query_pos, key_rows, value_rows, key_pos, grad_out, row_delta, row_best, summed
):
    factor = queries.shape[-1] ** (-0.5)
    key_blocks, value_blocks, pos_blocks = split_blocks(key_rows, value_rows, key_pos)

    def back_block(accumulated, pieces):
        key_block, value_block, pos_block = pieces
        scores = block_scores(queries, query_pos, key_block, pos_block, factor)
        probabilities = jnp.exp(scores - row_best[..., None]) / summed[..., None]
        weights = probabilities.astype(jnp.bfloat16)
        grad_probs = jnp.einsum(
            "rkgd,tkd->kgrt", grad_out, value_block, preferred_element_type=jnp.float32
        )
        grad_scores = (probabilities * (grad_probs - row_delta[..., None])).astype(jnp.bfloat16)
        accumulated = accumulated + jnp.einsum(
            "kgrt,tkd->rkgd", grad_scores, key_block, preferred_element_type=jnp.float32
        )
        grad_keys = jnp.einsum(
            "kgrt,rkgd->tkd", grad_scores, queries, preferred_element_type=jnp.float32
        )
        grad_values = jnp.einsum(
            "kgrt,rkgd->tkd", weights, grad_out, preferred_element_type=jnp.float32
        )
        return (accumulated, (grad_keys, grad_values))

    grad_queries, (grad_keys, grad_values) = lax.scan(
        back_block, jnp.zeros(queries.shape, jnp.float32), (key_blocks, value_blocks, pos_blocks)
    )
    return (
        grad_queries * factor,
        grad_keys.reshape(key_rows.shape) * factor,
        grad_values.reshape(value_rows.shape),
    )


def attention_forward(queries, query_pos, all_keys, all_values, key_pos):
    return attend(queries, query_pos, all_keys, all_values, key_pos)


def attention_backward(
    queries, query_pos, all_keys, all_values, key_pos, grad_out, row_delta, row_best, summed
):
    return attend_back(
        queries, query_pos, all_keys, all_values, key_pos, grad_out, row_delta, row_best, summed
    )


def local(
    hidden_in,
    block_map,
    query_weight,
    key_weight,
    value_weight,
    out_weight,
    gate_weight,
    up_weight,
    down_weight,
    attention_norm_gain,
    feedforward_gain,
    query_gain,
    key_gain,
    output_grad,
):
    hidden = hidden_in[0]
    row_count = hidden.shape[0]
    piece_rows = row_count // 2
    head_width = query_gain.shape[0]
    query_heads = query_weight.shape[1] // head_width
    key_heads = key_weight.shape[1] // head_width
    group_size = query_heads // key_heads
    hidden_units = gate_weight.shape[1]
    device_index = lax.axis_index("ctx")
    map_row = block_map[0]
    own_blocks = lax.dynamic_slice_in_dim(map_row, 2 * device_index, 2)
    offsets = jnp.arange(piece_rows, dtype=jnp.int32)
    query_pos = (own_blocks[:, None] * piece_rows + offsets[None, :]).reshape(row_count)
    key_pos = (map_row[:, None] * piece_rows + offsets[None, :]).reshape(-1)
    cosine, sine_table = rope_tables(query_pos, head_width)
    full_query, full_key, full_value, full_out, full_attention_gain = fetch_attention(
        query_weight, key_weight, value_weight, out_weight, attention_norm_gain
    )
    hidden_float = hidden.astype(jnp.float32)
    normed_float, unit_one, scale_one = norm_rows(
        hidden_float, full_attention_gain.astype(jnp.float32)
    )
    normed = normed_float.astype(jnp.bfloat16)
    query_lin = multiply(normed, full_query).reshape(row_count, query_heads, head_width)
    key_lin = multiply(normed, full_key).reshape(row_count, key_heads, head_width)
    value_rows = (
        multiply(normed, full_value).astype(jnp.bfloat16).reshape(row_count, key_heads, head_width)
    )
    query_gain_float = query_gain.astype(jnp.float32)
    key_gain_float = key_gain.astype(jnp.float32)
    query_normed, query_unit, query_scale = norm_rows(query_lin, query_gain_float)
    queries = (
        rotate(query_normed, cosine, sine_table)
        .astype(jnp.bfloat16)
        .reshape(row_count, key_heads, group_size, head_width)
    )
    key_normed, key_unit, key_scale = norm_rows(key_lin, key_gain_float)
    key_rows = rotate(key_normed, cosine, sine_table).astype(jnp.bfloat16)
    all_keys, all_values = (
        lax.all_gather(key_rows, "ctx", axis=0, tiled=True),
        lax.all_gather(value_rows, "ctx", axis=0, tiled=True),
    )
    attended, row_best, summed = attention_forward(
        queries, query_pos, all_keys, all_values, key_pos
    )
    attended_low = attended.reshape(row_count, query_heads * head_width).astype(jnp.bfloat16)
    residual = hidden_float + multiply_trans(attended_low, full_out)
    full_gate, full_up, full_down, full_mlp_gain = fetch_feedforward(
        gate_weight, up_weight, down_weight, feedforward_gain
    )
    normed_mlp_float, unit_two, scale_two = norm_rows(residual, full_mlp_gain.astype(jnp.float32))
    normed_mlp = normed_mlp_float.astype(jnp.bfloat16)
    gate_lin = multiply(normed_mlp, full_gate)
    up_lin = multiply(normed_mlp, full_up)
    sigmoid_gate = jax.nn.sigmoid(gate_lin)
    silu_gate = gate_lin * sigmoid_gate
    activation = (silu_gate * up_lin).astype(jnp.bfloat16)
    output = (residual + multiply_trans(activation, full_down)).astype(jnp.bfloat16)
    full_gate, full_up, full_down, full_mlp_gain = fetch_feedforward(
        gate_weight, up_weight, down_weight, feedforward_gain
    )
    grad_rows = output_grad[0]
    grad_act = multiply(grad_rows, full_down)
    grad_gate = (grad_act * up_lin * sigmoid_gate * (1.0 + gate_lin * (1.0 - sigmoid_gate))).astype(
        jnp.bfloat16
    )
    grad_up = (grad_act * silu_gate).astype(jnp.bfloat16)
    grad_normed_mlp = multiply_trans(grad_gate, full_gate) + multiply_trans(grad_up, full_up)
    grad_residual_norm, gain_terms_two = norm_back(
        grad_normed_mlp, unit_two, scale_two, full_mlp_gain.astype(jnp.float32)
    )
    grad_residual = grad_rows.astype(jnp.float32) + grad_residual_norm
    feed_sums = lax.psum_scatter(
        jnp.concatenate(
            [
                outer_rows(normed_mlp, grad_gate),
                outer_rows(normed_mlp, grad_up),
                outer_rows(grad_rows, activation),
            ],
            axis=1,
        ),
        ("ctx", "fsdp"),
        scatter_dimension=0,
        tiled=True,
    )
    gate_grad = feed_sums[:, :hidden_units]
    up_grad = feed_sums[:, hidden_units : 2 * hidden_units]
    down_grad = feed_sums[:, 2 * hidden_units :]
    full_query, full_key, full_value, full_out, full_attention_gain = fetch_attention(
        query_weight, key_weight, value_weight, out_weight, attention_norm_gain
    )
    grad_residual_low = grad_residual.astype(jnp.bfloat16)
    out_grad_own = outer_rows(grad_residual_low, attended_low)
    grad_attended = (
        multiply(grad_residual_low, full_out)
        .astype(jnp.bfloat16)
        .reshape(row_count, key_heads, group_size, head_width)
    )
    row_delta = jnp.moveaxis(jnp.sum(grad_attended.astype(jnp.float32) * attended, axis=-1), 0, -1)
    grad_queries, grad_keys_all, grad_values_all = attention_backward(
        queries,
        query_pos,
        all_keys,
        all_values,
        key_pos,
        grad_attended,
        row_delta,
        row_best,
        summed,
    )
    grad_keys, grad_values = (
        lax.psum_scatter(grad_keys_all, "ctx", scatter_dimension=0, tiled=True),
        lax.psum_scatter(grad_values_all, "ctx", scatter_dimension=0, tiled=True),
    )
    grad_values_low = grad_values.astype(jnp.bfloat16).reshape(row_count, key_heads * head_width)
    grad_query_rot = rotate_back(
        grad_queries.reshape(row_count, query_heads, head_width), cosine, sine_table
    )
    grad_query_lin, query_gain_terms = norm_back(
        grad_query_rot, query_unit, query_scale, query_gain_float
    )
    grad_key_rot = rotate_back(grad_keys, cosine, sine_table)
    grad_key_lin, key_gain_terms = norm_back(grad_key_rot, key_unit, key_scale, key_gain_float)
    grad_query_low = grad_query_lin.reshape(row_count, query_heads * head_width).astype(
        jnp.bfloat16
    )
    grad_key_low = grad_key_lin.reshape(row_count, key_heads * head_width).astype(jnp.bfloat16)
    query_grad_own = outer_rows(normed, grad_query_low)
    key_grad_own = outer_rows(normed, grad_key_low)
    value_grad_own = outer_rows(normed, grad_values_low)
    grad_normed = (
        multiply_trans(grad_query_low, full_query)
        + multiply_trans(grad_key_low, full_key)
        + multiply_trans(grad_values_low, full_value)
    )
    grad_hidden_norm, gain_terms_one = norm_back(
        grad_normed, unit_one, scale_one, full_attention_gain.astype(jnp.float32)
    )
    input_grad = (grad_residual + grad_hidden_norm).astype(jnp.bfloat16)
    attention_sums = (
        lax.psum_scatter(query_grad_own, ("ctx", "fsdp"), scatter_dimension=0, tiled=True),
        lax.psum_scatter(key_grad_own, ("ctx", "fsdp"), scatter_dimension=0, tiled=True),
        lax.psum_scatter(value_grad_own, ("ctx", "fsdp"), scatter_dimension=0, tiled=True),
        lax.psum_scatter(out_grad_own, ("ctx", "fsdp"), scatter_dimension=0, tiled=True),
        lax.psum_scatter(
            jnp.sum(gain_terms_one, axis=0), ("ctx", "fsdp"), scatter_dimension=0, tiled=True
        ),
        lax.psum_scatter(
            jnp.sum(gain_terms_two, axis=0), ("ctx", "fsdp"), scatter_dimension=0, tiled=True
        ),
    )
    head_sums = lax.psum(
        (jnp.sum(query_gain_terms, axis=(0, 1)), jnp.sum(key_gain_terms, axis=(0, 1))),
        ("ctx", "fsdp"),
    )
    return (
        output[None],
        input_grad[None],
        attention_sums[0],
        attention_sums[1],
        attention_sums[2],
        attention_sums[3],
        gate_grad,
        up_grad,
        down_grad,
        attention_sums[4],
        attention_sums[5],
        head_sums[0],
        head_sums[1],
    )


def solution(mesh):
    placed = (
        P("fsdp", "ctx", None),
        P("fsdp", None),
        P(("ctx", "fsdp"), None),
        P(("ctx", "fsdp"), None),
        P(("ctx", "fsdp"), None),
        P(("ctx", "fsdp"), None),
        P(("ctx", "fsdp"), None),
        P(("ctx", "fsdp"), None),
        P(("ctx", "fsdp"), None),
        P(("ctx", "fsdp")),
        P(("ctx", "fsdp")),
        P(),
        P(),
        P("fsdp", "ctx", None),
    )
    return jax.shard_map(
        local,
        mesh=mesh,
        in_specs=placed,
        out_specs=(
            P("fsdp", "ctx", None),
            P("fsdp", "ctx", None),
            P(("ctx", "fsdp"), None),
            P(("ctx", "fsdp"), None),
            P(("ctx", "fsdp"), None),
            P(("ctx", "fsdp"), None),
            P(("ctx", "fsdp"), None),
            P(("ctx", "fsdp"), None),
            P(("ctx", "fsdp"), None),
            P(("ctx", "fsdp")),
            P(("ctx", "fsdp")),
            P(),
            P(),
        ),
        check_vma=False,
    )
```

profile of v0, /device:TPU:0, one launch (start us, length us, event | category | flops | bytes accessed | tf_op | source)
XLA Modules:
  0.0 3341.9 jit_solution(16327627066163136442)
XLA Ops:
  11.9 42.2 %all-reduce.5 = (bf16[2048]{0:T(1024)(128)(2,1)S(1)}, bf16[2048]{0:T(1024)(128)(2,1)S(1)}) all-reduce(bf16[2048]{0:T(1024)(128)(2,1)S(1)} %dynamic-update-slice, bf16[2048]{0:T(1024)(128)(2,1)S(1)} %dynamic-update-slice.1), channel_id=1, replica_groups=mesh['ctx'=16,'fsdp'=2] {'ctx','fsdp'}, use_global_device_ids=true, to_apply=%add | all-reduce | flops 4096 | bytes 16384
  55.8 19.8 all-gather.14.cloned.1.call-done
  75.7 6.6 copy.62
  88.1 51.0 %all-gather.10.cloned.1.call-done = bf16[2048,1024]{1,0:T(8,128)(2,1)} async-done(((bf16[64,1024]{1,0:T(8,128)(2,1)}), bf16[2048,1024]{1,0:T(8,128)(2,1)}) %all-gather.10.cloned.1.call-update) | async-done | bytes 4194320 | tf_op jit(solution)/shard_map/all_gather | solution.py:64
  146.4 83.8 %all-gather.16.cloned.1.call-done = bf16[2048,8,128]{0,2,1:T(8,128)(2,1)} async-done(((bf16[128,8,128]{0,2,1:T(8,128)(2,1)}), bf16[2048,8,128]{0,2,1:T(8,128)(2,1)}) %all-gather.16.cloned.1.call-update) | async-done | bytes 4194320 | tf_op jit(solution)/shard_map/all_gather | solution.py:234
  230.2 7.8 reshape.383
  238.0 7.8 copy.67
  245.9 62.8 %all-gather.18.cloned.1.call-done = bf16[2048,2048]{1,0:T(8,128)(2,1)} async-done(((bf16[64,2048]{1,0:T(8,128)(2,1)}), bf16[2048,2048]{1,0:T(8,128)(2,1)}) %all-gather.18.cloned.1.call-update) | async-done | bytes 8388624 | tf_op jit(solution)/shard_map/all_gather | solution.py:62
  308.7 12.3 copy.63
  321.0 5.9 multiply_reduce_fusion.6
  328.2 12.9 while.39
  341.1 45.5 %all-gather.12.cloned.1.call-done = bf16[2048,8,128]{2,1,0:T(8,128)(2,1)} async-done(((bf16[128,8,128]{2,1,0:T(8,128)(2,1)}), bf16[2048,8,128]{2,1,0:T(8,128)(2,1)}) %all-gather.12.cloned.1.call-update) | async-done | bytes 4194320 | tf_op jit(solution)/shard_map/all_gather | solution.py:235
  386.6 29.7 while.40
  396.8 4.4 fusion.176
  418.4 47.1 %all-gather.20.cloned.1.call-done = bf16[2048,2048]{1,0:T(8,128)(2,1)} async-done(((bf16[64,2048]{1,0:T(8,128)(2,1)}), bf16[2048,2048]{1,0:T(8,128)(2,1)}) %all-gather.20.cloned.1.call-update) | async-done | bytes 8388624 | tf_op jit(solution)/shard_map/all_gather | solution.py:65
  465.5 6.5 multiply_reduce_fusion.5
  472.3 149.4 %all-gather.24.cloned.1.call-done = bf16[2048,6144]{1,0:T(8,128)(2,1)} async-done(((bf16[64,6144]{1,0:T(8,128)(2,1)}), bf16[2048,6144]{1,0:T(8,128)(2,1)}) %all-gather.24.cloned.1.call-update) | async-done | bytes 25165840 | tf_op jit(solution)/shard_map/all_gather | solution.py:73
  621.7 13.3 fusion.105
  634.9 142.4 %all-gather.22.cloned.1.call-done = bf16[2048,6144]{1,0:T(8,128)(2,1)} async-done(((bf16[64,6144]{1,0:T(8,128)(2,1)}), bf16[2048,6144]{1,0:T(8,128)(2,1)}) %all-gather.22.cloned.1.call-update) | async-done | bytes 25165840 | tf_op jit(solution)/shard_map/all_gather | solution.py:72
  777.4 13.3 fusion.104
  790.6 142.5 %all-gather.26.cloned.1.call-done = bf16[2048,6144]{1,0:T(8,128)(2,1)} async-done(((bf16[64,6144]{1,0:T(8,128)(2,1)}), bf16[2048,6144]{1,0:T(8,128)(2,1)}) %all-gather.26.cloned.1.call-update) | async-done | bytes 25165840 | tf_op jit(solution)/shard_map/all_gather | solution.py:74
  933.1 14.9 multiply_convert_fusion
  948.0 14.7 fusion.106
  962.7 15.2 multiply_reduce_fusion.1
  980.6 4.7 convolution_convert_fusion
  988.4 48.0 %while.41 = (s32[]{:T(128)}, f32[128,8,2,128]{0,3,2,1:T(8,128)S(1)}, f32[4,512,8,128]{3,1,2,0:T(8,128)}, f32[4,512,8,128]{3,2,1,0:T(8,128)}, bf16[4,512,8,128]{3...) while((s32[]{:T(128)}, ...), condition=%wide.region_13.14_spmd.clone, body=%wide.region_12.13_spmd.clone.sunk | while | flops 1351155840 | bytes 36864192 | solution.py:157
  1037.5 7.9 broadcast_multiply_fusion
  1045.3 10.3 copy.74
  1055.6 10.9 mul.427
  1067.9 19.8 fusion.109
  1087.7 21.3 fusion.108
  1109.0 19.7 convolution_bitcast_fusion.1
  1128.7 98.3 %pad_maximum_fusion = f32[2048,18432]{1,0:T(8,128)} fusion(f32[2048,6144]{1,0:T(8,128)} %convolution_bitcast_fusion.1, f32[2048,6144]{1,0:T(8,128)} %fusion.109, f32[2048,6144]{1,0:T(8,128)} %fusion.108), kind=kLoop, calls=%fused_computation.60 | loop fusion | flops 75497472 | bytes 301989888 | tf_op jit(solution)/shard_map/concatenate | solution.py:268
  1228.2 4.6 fusion.81
  1232.9 162.3 %reduce-scatter.8.cloned.1.call-done = f32[128,8,128]{0,2,1:T(8,128)} async-done(((f32[2048,8,128]{0,2,1:T(8,128)}), f32[128,8,128]{0,2,1:T(8,128)}) %reduce-scatter.8.cloned.1.call-update) | async-done | bytes 524304 | tf_op jit(solution)/shard_map/reduce_scatter | solution.py:306
  1397.8 4.6 fusion.83
  1403.7 9.7 fusion.89
  1416.2 10.9 fusion.79
  1427.2 9.0 fusion.107
  1436.1 17.1 fusion.48
  1453.2 5.1 convolution_add_fusion.1
  1460.3 43.0 %all-reduce.4 = (f32[2048]{0:T(1024)S(1)}, f32[2048]{0:T(1024)S(1)}, f32[128]{0:T(128)}, f32[128]{0:T(128)}) all-reduce(f32[2048]{0:T(1024)S(1)} %get-tuple-element.369, f32[2048]{0:T(1024)S(1)} %copy-done.33, f32[128]{0:T(128)S(1)} %get-tuple-element.365, ...), channel_id=9, replica_groups=mesh['ctx'=16,'fsdp'=2] {'ctx','fsdp'}, use_global_device_ids=true, to_apply=%region_25.26.clone | all-reduce | flops 4352 | bytes 34816
  1505.6 1162.2 %reduce-scatter.20.cloned.1.call-done = f32[64,18432]{1,0:T(8,128)} async-done(((f32[2048,18432]{1,0:T(8,128)}), f32[64,18432]{1,0:T(8,128)}) %reduce-scatter.20.cloned.1.call-update) | async-done | bytes 4718608 | tf_op jit(solution)/shard_map/reduce_scatter | solution.py:267
  2667.9 4.6 fusion.101
  2672.5 146.1 %reduce-scatter.16.cloned.1.call-done = f32[64,1024]{1,0:T(8,128)} async-done(((f32[2048,1024]{1,0:T(8,128)}), f32[64,1024]{1,0:T(8,128)}) %reduce-scatter.16.cloned.1.call-update) | async-done | bytes 262160 | tf_op jit(solution)/shard_map/reduce_scatter | solution.py:337
  2818.6 147.5 %reduce-scatter.14.cloned.1.call-done = f32[64,1024]{1,0:T(8,128)} async-done(((f32[2048,1024]{1,0:T(8,128)}), f32[64,1024]{1,0:T(8,128)}) %reduce-scatter.14.cloned.1.call-update) | async-done | bytes 262160 | tf_op jit(solution)/shard_map/reduce_scatter | solution.py:336
  2966.1 181.5 %reduce-scatter.18.cloned.1.call-done = f32[64,2048]{1,0:T(8,128)} async-done(((f32[2048,2048]{1,0:T(8,128)}), f32[64,2048]{1,0:T(8,128)}) %reduce-scatter.18.cloned.1.call-update) | async-done | bytes 524304 | tf_op jit(solution)/shard_map/reduce_scatter | solution.py:338
  3147.7 187.4 %reduce-scatter.12.cloned.1.call-done = f32[64,2048]{1,0:T(8,128)} async-done(((f32[2048,2048]{1,0:T(8,128)}), f32[64,2048]{1,0:T(8,128)}) %reduce-scatter.12.cloned.1.call-update) | async-done | bytes 524304 | tf_op jit(solution)/shard_map/reduce_scatter | solution.py:335
  (287 shorter events, 128.6 us)
Async XLA Ops:
  7.2 68.5 %all-gather.14.cloned.1.call-start = ((), (), s32[]{:S(2)}) async-start(), calls=%async_computation.9 | async-start | bytes 4325376 | tf_op jit(solution)/shard_map/all_gather | solution.py:63
  7.9 131.2 %all-gather.10.cloned.1.call-start = ((), (), s32[]{:S(2)}) async-start(), calls=%async_computation.7 | async-start | bytes 4325376 | tf_op jit(solution)/shard_map/all_gather | solution.py:64
  8.7 221.5 %all-gather.16.cloned.1.call-start = ((), (), s32[]{:S(2)}) async-start(), calls=%async_computation.10 | async-start | bytes 4456448 | tf_op jit(solution)/shard_map/all_gather | solution.py:234
  9.4 76.6 %copy-start.34 = (f32[128]{0:T(128)}, f32[128]{0:T(128)S(1)}, u32[]{:S(2)}) copy-start(f32[128]{0:T(128)S(1)} %convert_element_type.128) | copy-start | bytes 1540
  54.2 266.8 %copy-start.25 = (f32[2048]{0:T(1024)}, f32[2048]{0:T(1024)S(1)}, u32[]{:S(2)}) copy-start(f32[2048]{0:T(1024)S(1)} %convert_element_type.122) | copy-start | bytes 24580
  54.5 272.7 %copy-start.21 = (f32[128,128]{0,1:T(8,128)}, f32[128,128]{0,1:T(8,128)S(1)}, u32[]{:S(2)}) copy-start(f32[128,128]{0,1:T(8,128)S(1)} %get-tuple-element.455) | copy-start | bytes 196612
  54.5 272.7 %copy-start.23 = (f32[128,128]{0,1:T(8,128)}, f32[128,128]{0,1:T(8,128)S(1)}, u32[]{:S(2)}) copy-start(f32[128,128]{0,1:T(8,128)S(1)} %get-tuple-element.456) | copy-start | bytes 196612
  55.8 265.2 %copy-start.31 = (f32[128]{0:T(128)}, f32[128]{0:T(128)S(1)}, u32[]{:S(2)}) copy-start(f32[128]{0:T(128)S(1)} %add_rsqrt_fusion.3) | copy-start | bytes 1540
  75.7 6.6 copy-start
  85.8 56.3 %copy-start.29 = (f32[128,8]{0,1:T(8,128)}, f32[128,8]{0,1:T(8,128)S(1)}, u32[]{:S(2)}) copy-start(f32[128,8]{0,1:T(8,128)S(1)} %add_rsqrt_fusion.1) | copy-start | bytes 12292
  87.5 221.2 %all-gather.18.cloned.1.call-start = ((), (), s32[]{:S(2)}) async-start(), calls=%async_computation.11 | async-start | bytes 8650752 | tf_op jit(solution)/shard_map/all_gather | solution.py:62
  88.0 57.9 %copy-start.38 = (bf16[128]{0:T(256)(128)(2,1)S(1)}, bf16[128]{0:T(256)(128)(2,1)}, u32[]{:S(2)}) copy-start(bf16[128]{0:T(256)(128)(2,1)} %param.31) | copy-start | bytes 772
  88.1 57.9 %copy-start.39 = (s32[1,32]{1,0:T(1,128)S(1)}, s32[1,32]{1,0:T(1,128)}, u32[]{:S(2)}) copy-start(s32[1,32]{1,0:T(1,128)} %param.21) | copy-start | bytes 388
  88.1 298.5 %all-gather.12.cloned.1.call-start = ((), (), s32[]{:S(2)}) async-start(), calls=%async_computation.8 | async-start | bytes 4456448 | tf_op jit(solution)/shard_map/all_gather | solution.py:235
  142.9 322.7 %all-gather.20.cloned.1.call-start = ((), (), s32[]{:S(2)}) async-start(), calls=%async_computation.12 | async-start | bytes 8650752 | tf_op jit(solution)/shard_map/all_gather | solution.py:65
  143.5 478.2 %all-gather.24.cloned.1.call-start = ((), (), s32[]{:S(2)}) async-start(), calls=%async_computation.14 | async-start | bytes 25952256 | tf_op jit(solution)/shard_map/all_gather | solution.py:73
  144.2 633.1 %all-gather.22.cloned.1.call-start = ((), (), s32[]{:S(2)}) async-start(), calls=%async_computation.13 | async-start | bytes 25952256 | tf_op jit(solution)/shard_map/all_gather | solution.py:72
  145.0 788.1 %all-gather.26.cloned.1.call-start = ((), (), s32[]{:S(2)}) async-start(), calls=%async_computation.15 | async-start | bytes 25952256 | tf_op jit(solution)/shard_map/all_gather | solution.py:74
  145.7 1081.4 %reduce-scatter.10.cloned.1.call-start = ((), (), s32[]{:S(2)}) async-start(), calls=%async_computation.17 | async-start | bytes 8912896 | tf_op jit(solution)/shard_map/reduce_scatter | solution.py:307
  146.0 181.3 %copy-start.36 = (f32[128]{0:T(128)}, f32[128]{0:T(128)S(1)}, u32[]{:S(2)}) copy-start(f32[128]{0:T(128)S(1)} %convert_element_type.132) | copy-start | bytes 1540
  472.1 505.8 %copy-start.6 = (f32[128,2048]{1,0:T(8,128)}, f32[128,2048]{1,0:T(8,128)S(1)}, u32[]{:S(2)}) copy-start(f32[128,2048]{1,0:T(8,128)S(1)} %get-tuple-element.462) | copy-start | bytes 3145732
  1037.5 357.8 %reduce-scatter.8.cloned.1.call-start = ((), (), s32[]{:S(2)}) async-start(), calls=%async_computation.16 | async-start | bytes 8912896 | tf_op jit(solution)/shard_map/reduce_scatter | solution.py:306
  1066.5 1.4 copy-start.16
  1066.5 1601.3 %reduce-scatter.20.cloned.1.call-start = ((), (), s32[]{:S(2)}) async-start(), calls=%async_computation.22 | async-start | bytes 155713536 | tf_op jit(solution)/shard_map/reduce_scatter | solution.py:267
  1087.7 21.3 copy-start.14
  1087.7 21.3 copy-start.20
  1226.9 1.3 copy-start.32
  1227.0 1591.6 %reduce-scatter.16.cloned.1.call-start = ((), (), s32[]{:S(2)}) async-start(), calls=%async_computation.20 | async-start | bytes 8650752 | tf_op jit(solution)/shard_map/reduce_scatter | solution.py:337
  1232.8 162.4 %copy-start.24 = (f32[128,128]{0,1:T(8,128)S(1)}, f32[128,128]{0,1:T(8,128)}, u32[]{:S(2)}) copy-start(f32[128,128]{0,1:T(8,128)} %copy-done.23) | copy-start | bytes 196612
  1232.8 163.5 %copy-start.13 = (f32[128,8,128]{0,2,1:T(8,128)S(1)}, f32[128,8,128]{0,2,1:T(8,128)}, u32[]{:S(2)}) copy-start(f32[128,8,128]{0,2,1:T(8,128)} %copy-done.12) | copy-start | bytes 1572868
  1232.8 163.5 %copy-start.22 = (f32[128,128]{0,1:T(8,128)S(1)}, f32[128,128]{0,1:T(8,128)}, u32[]{:S(2)}) copy-start(f32[128,128]{0,1:T(8,128)} %copy-done.21) | copy-start | bytes 196612
  1232.8 163.5 %copy-start.30 = (f32[128,8]{0,1:T(8,128)S(1)}, f32[128,8]{0,1:T(8,128)}, u32[]{:S(2)}) copy-start(f32[128,8]{0,1:T(8,128)} %copy-done.29) | copy-start | bytes 12292
  1232.8 163.5 %copy-start.35 = (f32[128]{0:T(128)S(1)}, f32[128]{0:T(128)}, u32[]{:S(2)}) copy-start(f32[128]{0:T(128)} %copy-done.34) | copy-start | bytes 1540
  1232.9 1733.3 %reduce-scatter.14.cloned.1.call-start = ((), (), s32[]{:S(2)}) async-start(), calls=%async_computation.19 | async-start | bytes 8650752 | tf_op jit(solution)/shard_map/reduce_scatter | solution.py:336
  1397.8 4.6 copy-start.19
  1402.4 1.4 copy-start.18
  1402.4 1745.3 %reduce-scatter.18.cloned.1.call-start = ((), (), s32[]{:S(2)}) async-start(), calls=%async_computation.21 | async-start | bytes 17301504 | tf_op jit(solution)/shard_map/reduce_scatter | solution.py:338
  1413.5 1.4 copy-start.3
  1413.5 1.9 copy-start.5
  1413.5 1.9 copy-start.28
  1413.5 1.9 copy-start.37
  1413.5 1921.6 %reduce-scatter.12.cloned.1.call-start = ((), (), s32[]{:S(2)}) async-start(), calls=%async_computation.18 | async-start | bytes 17301504 | tf_op jit(solution)/shard_map/reduce_scatter | solution.py:335
  1416.2 10.9 copy-start.17
  1427.1 9.0 copy-start.7
  1427.2 9.0 copy-start.15
  1453.2 5.3 copy-start.11
  1458.6 1.7 copy-start.33
  1458.6 45.9 %copy-start.10 = (f32[128,2048]{1,0:T(8,128)S(1)}, f32[128,2048]{1,0:T(8,128)}, u32[]{:S(2)}) copy-start(f32[128,2048]{1,0:T(8,128)} %copy-done.8) | copy-start | bytes 3145732
  (8 other events, 8.5 us)
Sparse Core Ops, SparseCore 0:
  10.9 64.7 all-gather.13
  78.5 60.5 all-gather.9
  142.4 87.7 all-gather.15
  232.9 75.7 all-gather.17
  311.9 74.6 all-gather.11
  389.3 76.1 all-gather.19
  468.4 153.2 all-gather.23
  624.5 152.7 all-gather.21
  780.2 152.7 all-gather.25
  1036.6 175.9 reduce-scatter.9
  1215.0 180.2 reduce-scatter.7
  1401.5 1266.2 reduce-scatter.19
  2670.8 147.7 reduce-scatter.15
  2821.4 144.6 reduce-scatter.13
  2968.9 178.6 reduce-scatter.17
  3150.5 184.5 reduce-scatter.11
where the time goes:
time: 3350 us; the launch traced here: 3340 us
  waiting for transfers between devices  2740 us (82%)
  matrix products  275 us (8%)
  other arithmetic  128 us (4%)
  local copies, waits for them, and re-layouts  101 us (3%)
  blocking collectives  85.2 us (3%)
    reduce_scatter x1, waiting for transfers between devices, local(): lax.psum_scatter(jnp.concatenate([outer_rows(normed_mlp, grad_gate), oute...  1160 us
    reduce_scatter x1, waiting for transfers between devices, local(): lax.psum_scatter(query_grad_own, ('ctx', 'fsdp'), scatter_dimension=0, ti...  187 us
    reduce_scatter x1, waiting for transfers between devices, local(): lax.psum_scatter(out_grad_own, ('ctx', 'fsdp'), scatter_dimension=0, tile...  182 us
    reduce_scatter x1, waiting for transfers between devices, local(): lax.psum_scatter(grad_keys_all, 'ctx', scatter_dimension=0, tiled=True)  162 us
    all_gather x1, waiting for transfers between devices, fetch_feedforward(): lax.all_gather(up_weight, ('ctx', 'fsdp'), axis=0, tiled=True)  149 us
    reduce_scatter x1, waiting for transfers between devices, local(): lax.psum_scatter(key_grad_own, ('ctx', 'fsdp'), scatter_dimension=0, tile...  148 us
    reduce_scatter x1, waiting for transfers between devices, local(): lax.psum_scatter(value_grad_own, ('ctx', 'fsdp'), scatter_dimension=0, ti...  146 us
    all_gather x1, waiting for transfers between devices, fetch_feedforward(): lax.all_gather(down_weight, ('ctx', 'fsdp'), axis=0, tiled=True)  142 us
  transfers between devices with their start and end apart: 16, of which 15 were waited for; matrix products, arithmetic and copies ran while one was open for 12% of the time, Pallas kernels for 0%

commit v1 on v0

v1 whole, which is shorter than its diff:
```python
import jax
import jax.numpy as jnp
from jax import lax
from jax.sharding import Mesh, PartitionSpec as P

epsilon = 1e-06
rotary_base = 1000000.0
masked_score = -1e30
parts = 4
bf16 = jnp.bfloat16
f32 = jnp.float32


def unit_rows(values):
    scale_row = lax.rsqrt(jnp.mean(values * values, axis=-1, keepdims=True) + epsilon)
    return values * scale_row, scale_row


def norm_back(weighted, unit, scale_row):
    inner_mean = jnp.mean(weighted * unit, axis=-1, keepdims=True)
    return scale_row * (weighted - unit * inner_mean)


def rope_tables(positions, width):
    half_width = width // 2
    frequency = rotary_base ** (-(jnp.arange(half_width, dtype=f32) * 2.0 / width))
    angles = positions.astype(f32)[:, None] * frequency[None, :]
    angles = jnp.concatenate([angles, angles], axis=-1)
    return jnp.cos(angles)[:, None, :], jnp.sin(angles)[:, None, :]


def rotate(values, cosine, sine_table):
    half_width = values.shape[-1] // 2
    turned = jnp.concatenate([-values[..., half_width:], values[..., :half_width]], axis=-1)
    return values * cosine + turned * sine_table


def rotate_back(grads, cosine, sine_table):
    half_width = grads.shape[-1] // 2
    shifted = grads * sine_table
    turned = jnp.concatenate([shifted[..., half_width:], -shifted[..., :half_width]], axis=-1)
    return grads * cosine + turned


def multiply(left, right):
    return jnp.dot(left, right, preferred_element_type=f32)


def multiply_trans(left, right):
    return lax.dot_general(left, right, (((1,), (1,)), ((), ())), preferred_element_type=f32)


def outer_rows(left, right):
    return lax.dot_general(left, right, (((0,), (0,)), ((), ())), preferred_element_type=f32)


def block_scores(queries, query_pos, key_block, pos_block, factor):
    scores = (
        jnp.einsum("rkgd,tkd->kgrt", queries, key_block, preferred_element_type=f32) * factor
    )
    allowed = pos_block[None, :] <= query_pos[:, None]
    return jnp.where(allowed[None, None], scores, masked_score)


def split_blocks(key_rows, value_rows, key_pos):
    key_count = key_rows.shape[0]
    block_size = min(512, key_count)
    block_count = key_count // block_size
    return (
        key_rows.reshape(block_count, block_size, key_rows.shape[1], key_rows.shape[2]),
        value_rows.reshape(block_count, block_size, value_rows.shape[1], value_rows.shape[2]),
        key_pos.reshape(block_count, block_size),
    )


def attend(queries, query_pos, key_rows, value_rows, key_pos):
    factor = queries.shape[-1] ** (-0.5)
    key_blocks, value_blocks, pos_blocks = split_blocks(key_rows, value_rows, key_pos)
    stat_shape = (queries.shape[1], queries.shape[2], queries.shape[0])

    def row_stats(running, pieces):
        row_best, summed = running
        scores = block_scores(queries, query_pos, pieces[0], pieces[1], factor)
        new_best = jnp.maximum(row_best, jnp.max(scores, axis=-1))
        summed = summed * jnp.exp(row_best - new_best) + jnp.sum(
            jnp.exp(scores - new_best[..., None]), axis=-1
        )
        return ((new_best, summed), None)

    initial = (jnp.full(stat_shape, masked_score, f32), jnp.zeros(stat_shape, f32))
    (row_best, summed), unused = lax.scan(row_stats, initial, (key_blocks, pos_blocks))

    def mix_values(accumulated, pieces):
        scores = block_scores(queries, query_pos, pieces[0], pieces[2], factor)
        weights = (jnp.exp(scores - row_best[..., None]) / summed[..., None]).astype(bf16)
        return (
            accumulated
            + jnp.einsum("kgrt,tkd->rkgd", weights, pieces[1], preferred_element_type=f32),
            None,
        )

    attended, unused = lax.scan(
        mix_values, jnp.zeros(queries.shape, f32), (key_blocks, value_blocks, pos_blocks)
    )
    return attended, row_best, summed


def attend_back(
    queries, query_pos, key_rows, value_rows, key_pos, grad_out, row_delta, row_best, summed
):
    factor = queries.shape[-1] ** (-0.5)
    key_blocks, value_blocks, pos_blocks = split_blocks(key_rows, value_rows, key_pos)

    def back_block(accumulated, pieces):
        key_block, value_block, pos_block = pieces
        scores = block_scores(queries, query_pos, key_block, pos_block, factor)
        probabilities = jnp.exp(scores - row_best[..., None]) / summed[..., None]
        weights = probabilities.astype(bf16)
        grad_probs = jnp.einsum("rkgd,tkd->kgrt", grad_out, value_block, preferred_element_type=f32)
        grad_scores = (probabilities * (grad_probs - row_delta[..., None])).astype(bf16)
        accumulated = accumulated + jnp.einsum(
            "kgrt,tkd->rkgd", grad_scores, key_block, preferred_element_type=f32
        )
        grad_keys = jnp.einsum("kgrt,rkgd->tkd", grad_scores, queries, preferred_element_type=f32)
        grad_values = jnp.einsum("kgrt,rkgd->tkd", weights, grad_out, preferred_element_type=f32)
        return (accumulated, (grad_keys, grad_values))

    grad_queries, (grad_keys, grad_values) = lax.scan(
        back_block, jnp.zeros(queries.shape, f32), (key_blocks, value_blocks, pos_blocks)
    )
    return (
        grad_queries * factor,
        grad_keys.reshape(key_rows.shape) * factor,
        grad_values.reshape(value_rows.shape),
    )


def gather_z(rows):
    return lax.all_gather(rows, "z", axis=0, tiled=True)


def scatter_sum_z(partial_rows):
    count = partial_rows.shape[0] // parts
    pieces = partial_rows.astype(bf16).reshape(parts, count, partial_rows.shape[1])
    pieces = lax.all_to_all(pieces, "z", 0, 0, tiled=True)
    return jnp.sum(pieces.astype(f32), axis=0)


def columns_of(weight):
    rows, columns = weight.shape
    return weight.reshape(rows, parts, columns // parts).transpose(1, 0, 2)


def fetch_columns(slices):
    pieces = lax.all_to_all(slices, "z", 0, 0, tiled=True)
    pieces = pieces.reshape(parts * pieces.shape[1], pieces.shape[2])
    return lax.all_gather(pieces, ("p", "c"), axis=0, tiled=True)


def return_columns(grads):
    summed = lax.psum_scatter(grads.astype(bf16), ("p", "c"), scatter_dimension=0, tiled=True)
    pieces = summed.reshape(parts, summed.shape[0] // parts, summed.shape[1])
    return lax.all_to_all(pieces, "z", 0, 0, tiled=True)


def spread(pieces):
    return pieces.astype(f32).transpose(1, 0, 2).reshape(pieces.shape[1], -1)


def make_local(plane):
    def shuffle(values, shard):
        rows = values.shape[0]
        return values.reshape(rows, parts, plane, shard).transpose(0, 2, 1, 3).reshape(rows, -1)

    def unshuffle(values, shard):
        rows = values.shape[0]
        return values.reshape(rows, plane, parts, shard).transpose(0, 2, 1, 3).reshape(rows, -1)

    def local(
        hidden_in,
        block_map,
        query_weight,
        key_weight,
        value_weight,
        out_weight,
        gate_weight,
        up_weight,
        down_weight,
        attention_norm_gain,
        feedforward_gain,
        query_gain,
        key_gain,
        output_grad,
    ):
        shard = query_weight.shape[0]
        row_count = hidden_in.shape[1]
        piece_rows = row_count // 2
        head_width = query_gain.shape[0]
        query_heads = query_weight.shape[1] // head_width // parts
        key_heads = key_weight.shape[1] // head_width // parts
        group_size = query_heads // key_heads
        query_width = query_heads * head_width
        key_width = key_heads * head_width
        hidden_units = gate_weight.shape[1] // parts
        z_index = lax.axis_index("z")
        p_index = lax.axis_index("p")
        p_count = plane // lax.axis_size("c")

        hidden_own = shuffle(hidden_in[0], shard)
        grad_own = shuffle(output_grad[0], shard)

        gains = jnp.stack([attention_norm_gain, feedforward_gain], axis=1)
        gains = jnp.pad(gains, ((0, 0), (0, 128 - gains.shape[1])))
        attention_slices = jnp.concatenate(
            [
                columns_of(query_weight),
                columns_of(key_weight),
                columns_of(value_weight),
                columns_of(out_weight),
                jnp.broadcast_to(gains[None], (parts,) + gains.shape),
            ],
            axis=2,
        )
        attention_columns = fetch_columns(attention_slices)
        hidden = gather_z(hidden_own).astype(f32)
        gate_columns = fetch_columns(columns_of(gate_weight))
        up_columns = fetch_columns(columns_of(up_weight))
        down_columns = fetch_columns(columns_of(down_weight))
        grad_rows = gather_z(grad_own)

        ends = [query_width, query_width + key_width, query_width + 2 * key_width]
        ends.append(ends[-1] + query_width)
        projection = attention_columns[:, : ends[2]]
        out_columns = attention_columns[:, ends[2] : ends[3]]
        gains = attention_columns[:, ends[3] : ends[3] + 2].astype(f32).T
        first_gain, second_gain = gains[0], gains[1]

        blocks = block_map[0].reshape(parts, p_count, 2)
        offsets = jnp.arange(piece_rows, dtype=jnp.int32)
        all_pos = blocks.transpose(1, 0, 2)[..., None] * piece_rows + offsets
        all_pos = all_pos.reshape(p_count, parts * row_count)
        query_pos = lax.dynamic_index_in_dim(all_pos, p_index, 0, keepdims=False)
        key_pos = all_pos.reshape(-1)
        cosine, sine_table = rope_tables(query_pos, head_width)
        tokens = parts * row_count

        unit_one, scale_one = unit_rows(hidden)
        normed = (unit_one * first_gain).astype(bf16)
        lin = multiply(normed, projection)
        query_lin = lin[:, : ends[0]].reshape(tokens, query_heads, head_width)
        key_lin = lin[:, ends[0] : ends[1]].reshape(tokens, key_heads, head_width)
        value_rows = lin[:, ends[1] :].astype(bf16).reshape(tokens, key_heads, head_width)
        query_gain_float = query_gain.astype(f32)
        key_gain_float = key_gain.astype(f32)
        query_unit, query_scale = unit_rows(query_lin)
        queries = rotate(query_unit * query_gain_float, cosine, sine_table).astype(bf16)
        queries = queries.reshape(tokens, key_heads, group_size, head_width)
        key_unit, key_scale = unit_rows(key_lin)
        key_rows = rotate(key_unit * key_gain_float, cosine, sine_table).astype(bf16)
        both = lax.all_gather(
            jnp.concatenate([key_rows, value_rows], axis=1), "p", axis=0, tiled=True
        )
        all_keys, all_values = both[:, :key_heads], both[:, key_heads:]
        attended, row_best, summed = attend(queries, query_pos, all_keys, all_values, key_pos)
        attended_low = attended.reshape(tokens, query_width).astype(bf16)

        own_residual = hidden_own.astype(f32) + scatter_sum_z(
            multiply_trans(attended_low, out_columns)
        )
        unit_two, scale_two = unit_rows(own_residual)
        normed_mlp = gather_z((unit_two * second_gain).astype(bf16))
        gate_lin = multiply(normed_mlp, gate_columns)
        up_lin = multiply(normed_mlp, up_columns)
        sigmoid_gate = jax.nn.sigmoid(gate_lin)
        silu_gate = gate_lin * sigmoid_gate
        activation = (silu_gate * up_lin).astype(bf16)
        output = own_residual + scatter_sum_z(multiply_trans(activation, down_columns))
        output = unshuffle(output.astype(bf16), shard)

        down_pieces = return_columns(outer_rows(grad_rows, activation))
        grad_act = multiply(grad_rows, down_columns)
        grad_gate = (
            grad_act * up_lin * sigmoid_gate * (1.0 + gate_lin * (1.0 - sigmoid_gate))
        ).astype(bf16)
        grad_up = (grad_act * silu_gate).astype(bf16)
        grad_normed_mlp = scatter_sum_z(
            multiply_trans(grad_gate, gate_columns) + multiply_trans(grad_up, up_columns)
        )
        gate_pieces = return_columns(outer_rows(normed_mlp, grad_gate))
        up_pieces = return_columns(outer_rows(normed_mlp, grad_up))
        second_gain_sum = jnp.sum(grad_normed_mlp * unit_two, axis=0)
        grad_residual = grad_own.astype(f32) + norm_back(
            grad_normed_mlp * second_gain, unit_two, scale_two
        )
        grad_residual_low = gather_z(grad_residual.astype(bf16))
        grad_attended = multiply(grad_residual_low, out_columns).astype(bf16)
        grad_attended = grad_attended.reshape(tokens, key_heads, group_size, head_width)
        out_own = outer_rows(grad_residual_low, attended_low)
        row_delta = jnp.moveaxis(jnp.sum(grad_attended.astype(f32) * attended, axis=-1), 0, -1)
        grad_queries, grad_keys_all, grad_values_all = attend_back(
            queries,
            query_pos,
            all_keys,
            all_values,
            key_pos,
            grad_attended,
            row_delta,
            row_best,
            summed,
        )
        both = jnp.concatenate([grad_keys_all, grad_values_all], axis=1).astype(bf16)
        both = both.reshape(p_count, tokens, 2 * key_width)
        both = lax.all_to_all(both, "p", 0, 0, tiled=True)
        both = jnp.sum(both.astype(f32), axis=0).reshape(tokens, 2 * key_heads, head_width)
        grad_keys, grad_values = both[:, :key_heads], both[:, key_heads:]
        grad_query_rot = rotate_back(
            grad_queries.reshape(tokens, query_heads, head_width), cosine, sine_table
        )
        grad_key_rot = rotate_back(grad_keys, cosine, sine_table)
        query_gain_sum = jnp.sum(grad_query_rot * query_unit, axis=(0, 1))
        key_gain_sum = jnp.sum(grad_key_rot * key_unit, axis=(0, 1))
        grad_query_lin = norm_back(grad_query_rot * query_gain_float, query_unit, query_scale)
        grad_key_lin = norm_back(grad_key_rot * key_gain_float, key_unit, key_scale)
        grad_lin = jnp.concatenate(
            [
                grad_query_lin.reshape(tokens, query_width).astype(bf16),
                grad_key_lin.reshape(tokens, key_width).astype(bf16),
                grad_values.reshape(tokens, key_width).astype(bf16),
            ],
            axis=1,
        )
        grad_normed = scatter_sum_z(multiply_trans(grad_lin, projection))
        unit_own, scale_own = unit_rows(hidden_own.astype(f32))
        first_gain_sum = jnp.sum(grad_normed * unit_own, axis=0)
        grad_hidden = grad_residual + norm_back(grad_normed * first_gain, unit_own, scale_own)
        input_grad = unshuffle(grad_hidden.astype(bf16), shard)
        attention_pieces = return_columns(
            jnp.concatenate([outer_rows(normed, grad_lin), out_own], axis=1)
        )
        gain_sums = lax.psum_scatter(
            jnp.stack([first_gain_sum, second_gain_sum], axis=1).reshape(plane, parts, shard, 2),
            ("p", "c"),
            scatter_dimension=0,
            tiled=True,
        )
        gain_sums = lax.psum_scatter(gain_sums[0], "z", scatter_dimension=0, tiled=True)[0]
        head_sums = lax.psum(jnp.stack([query_gain_sum, key_gain_sum]), ("z", "p", "c"))
        return (
            output[None],
            input_grad[None],
            spread(attention_pieces[:, :, : ends[0]]),
            spread(attention_pieces[:, :, ends[0] : ends[1]]),
            spread(attention_pieces[:, :, ends[1] : ends[2]]),
            spread(attention_pieces[:, :, ends[2] :]),
            spread(gate_pieces),
            spread(up_pieces),
            spread(down_pieces),
            gain_sums[:, 0],
            gain_sums[:, 1],
            head_sums[0],
            head_sums[1],
        )

    return local


def solution(mesh):
    ctx_count, core_count = mesh.shape["ctx"], mesh.shape["fsdp"]
    plane = ctx_count // parts
    fine_mesh = Mesh(mesh.devices.reshape(parts, plane, core_count), ("z", "p", "c"))
    token_spec = P("c", ("z", "p"), None)
    weight_spec = P(("z", "p", "c"), None)
    gain_spec = P(("z", "p", "c"))
    return jax.shard_map(
        make_local(plane * core_count),
        mesh=fine_mesh,
        in_specs=(
            (token_spec, P("c", None)) + (weight_spec,) * 7 + (gain_spec,) * 2 + (P(), P(), token_spec)
        ),
        out_specs=(token_spec,) * 2 + (weight_spec,) * 7 + (gain_spec,) * 2 + (P(), P()),
        check_vma=False,
    )
```

time: 3350 us -> 990 us (0.30)
  waiting for transfers between devices: 2740 us -> 373 us
  blocking collectives: 85.2 us -> 212 us
  matrix products: 275 us -> 161 us
  other arithmetic: 128 us -> 74.6 us
  starting transfers between devices: 0.98 us -> 45.4 us
    reduce_scatter x7 -> x4, waiting for transfers between devices: 1990 us -> 17.8 us  [return_columns(): lax.psum_scatter(grads.astype(bf16), ('p', 'c'), scatter_dimension=0, til...]
    all_gather x9, waiting for transfers between devices: 744 us -> 174 us  [the longest x4 112 us: fetch_columns(): return lax.all_gather(pieces, ('p', 'c'), axis=0, tiled=True)]
    all_to_all x0 -> x10, waiting for transfers between devices: none -> 180 us  [the longest x4 116 us: scatter_sum_z(): pieces = lax.all_to_all(pieces, 'z', 0, 0, tiled=True)]
    all_to_all x0 -> x3, blocking collectives: none -> 115 us  [fetch_columns(): pieces = lax.all_to_all(slices, 'z', 0, 0, tiled=True)]
    concatenate x1 -> x4, other arithmetic: 98.3 us -> 10.1 us  [the longest x1 5.32 us: local(): jnp.concatenate([outer_rows(normed, grad_lin), out_own], axis=1)]
    psum x0 -> x1, blocking collectives: none -> 62 us  [local(): lax.psum(jnp.stack([query_gain_sum, key_gain_sum]), ('z', 'p', 'c'))]
    dot_general x7 -> x5, matrix products: 90.5 us -> 28.7 us  [outer_rows(): lax.dot_general(left, right, (((0,), (0,)), ((), ())), preferred_element_...]
    unnamed x2, blocking collectives: 85.2 us -> 35.3 us
  transfers between devices with their start and end apart: 16 -> 23, of which waited for: 15 -> 15; matrix products, arithmetic and copies ran while one was open for 12% -> 28% of each run, Pallas kernels for 0% -> 0%
where the time goes in v1:
time: 990 us; the launch traced here: 979 us
  waiting for transfers between devices  373 us (38%)
  blocking collectives  212 us (21%)
  matrix products  161 us (16%)
  local copies, waits for them, and re-layouts  97.1 us (10%)
  other arithmetic  74.6 us (8%)
  starting transfers between devices  45.4 us (5%)
  between operations  15.4 us (2%)
    all_to_all x4, waiting for transfers between devices, scatter_sum_z(): pieces = lax.all_to_all(pieces, 'z', 0, 0, tiled=True)  116 us
    all_to_all x3, blocking collectives, fetch_columns(): pieces = lax.all_to_all(slices, 'z', 0, 0, tiled=True)  115 us
    all_gather x4, waiting for transfers between devices, fetch_columns(): return lax.all_gather(pieces, ('p', 'c'), axis=0, tiled=True)  112 us
    psum x1, blocking collectives, local(): lax.psum(jnp.stack([query_gain_sum, key_gain_sum]), ('z', 'p', 'c'))  62 us
    all_gather x4, waiting for transfers between devices, gather_z(): return lax.all_gather(rows, 'z', axis=0, tiled=True)  59 us
    dot_general x5, matrix products, multiply(): return jnp.dot(left, right, preferred_element_type=f32)  36.6 us
    unnamed x2, blocking collectives  35.3 us
    all_to_all x4, waiting for transfers between devices, return_columns(): return lax.all_to_all(pieces, 'z', 0, 0, tiled=True)  33.2 us
  transfers between devices with their start and end apart: 23, of which 15 were waited for; matrix products, arithmetic and copies ran while one was open for 28% of the time, Pallas kernels for 0%

profile of v1, /device:TPU:0, one launch (start us, length us, event | category | flops | bytes accessed | tf_op | source)
XLA Modules:
  0.0 979.3 jit_solution(11011505025411286727)
XLA Ops:
  11.9 47.5 %all_to_all.65 = bf16[4,64,1664]{2,1,0:T(8,128)(2,1)} all-to-all(bf16[4,64,1664]{2,1,0:T(8,128)(2,1)S(1)} %copy.316), channel_id=1, replica_groups=mesh['z'=4,'p'=4,'c'=2] {'z'}, dimensions={0} | all-to-all | bytes 1703936 | tf_op jit(solution)/shard_map/all_to_all | solution.py:155
  61.9 11.8 %all-gather.10.cloned.1.call-done = bf16[512,2048]{0,1:T(8,128)(2,1)} async-done(((bf16[128,2048]{0,1:T(8,128)(2,1)}), bf16[512,2048]{0,1:T(8,128)(2,1)}) %all-gather.10.cloned.1.call-update) | async-done | bytes 2097168 | tf_op jit(solution)/shard_map/all_gather | solution.py:139
  75.8 48.3 %all-gather.12.cloned.1.call-done = bf16[2048,1664]{1,0:T(8,128)(2,1)} async-done(((bf16[256,1664]{1,0:T(8,128)(2,1)}), bf16[2048,1664]{1,0:T(8,128)(2,1)}) %all-gather.12.cloned.1.call-update) | async-done | bytes 6815760 | tf_op jit(solution)/shard_map/all_gather | solution.py:157
  126.3 4.7 fusion.54
  138.3 4.7 all-to-all-start.2
  145.0 18.6 %all-to-all-done.2 = bf16[4,64,1536]{2,1,0:T(8,128)(2,1)S(1)} async-done(((bf16[4,64,1536]{2,1,0:T(8,128)(2,1)}), bf16[4,64,1536]{2,1,0:T(8,128)(2,1)S(1)}, u32[]{:S(2)}, u32[]{:S(2)}) %all-to-all-start.2) | async-done | bytes 786464 | tf_op jit(solution)/shard_map/all_to_all | solution.py:155
  172.2 24.9 %while.39 = (s32[]{:T(128)}, f32[2,2,512]{2,1,0:T(2,128)S(1)}, f32[2,2,512]{2,1,0:T(2,128)S(1)}, s32[4,512]{1,0:T(4,128)S(1)}, s32[512]{0:T(512)S(1)}, /*index=5...) while((s32[]{:T(128)}, f32[2,2,512]{2,1,0:T(2,128)S(1)}, ...), condition=%wide.region_6.7_spmd.clone, body=%wide.region_3.6_spmd.clone.sunk | while | flops 276047872 | bytes 10076272 | solution.py:91
  197.2 15.4 %while.40 = (s32[]{:T(128)}, f32[512,2,2,128]{0,3,2,1:T(8,128)}, bf16[4,512,2,128]{3,1,0,2:T(8,128)(2,1)S(1)}, s32[4,512]{1,0:T(4,128)S(1)}, s32[512]{0:T(512)S(...) while((s32[]{:T(128)}, f32[512,2,2,128]{0,3,2,1:T(8,128)}, ...), condition=%wide.region_8.9_spmd.clone, body=%wide.region_7.8_spmd.clone.sunk | while | flops 542900224 | bytes 3695739 | solution.py:102
  204.4 4.0 fusion.166
  208.6 4.0 fusion.166
  214.7 4.5 convolution_convert_fusion.6
  219.2 4.8 all-to-all-start.1
  225.0 47.3 %all-to-all-done.1 = bf16[4,128,2048]{2,1,0:T(8,128)(2,1)} async-done(((bf16[4,128,2048]{2,1,0:T(8,128)(2,1)}), bf16[4,128,2048]{2,1,0:T(8,128)(2,1)}, u32[]{:S(2)}, u32[]{:S(2)}) %all-to-all-start.1) | async-done | bytes 2097184 | tf_op jit(solution)/shard_map/all_to_all | solution.py:145
  281.4 44.3 %all_to_all.66 = bf16[4,64,1536]{2,1,0:T(8,128)(2,1)} all-to-all(bf16[4,64,1536]{2,1,0:T(8,128)(2,1)S(1)} %copy.334), channel_id=1, replica_groups=mesh['z'=4,'p'=4,'c'=2] {'z'}, dimensions={0} | all-to-all | bytes 1572864 | tf_op jit(solution)/shard_map/all_to_all | solution.py:155
  334.4 22.9 %all_to_all.67 = bf16[4,64,1536]{2,1,0:T(8,128)(2,1)} all-to-all(bf16[4,64,1536]{2,1,0:T(8,128)(2,1)S(1)} %copy.335), channel_id=1, replica_groups=mesh['z'=4,'p'=4,'c'=2] {'z'}, dimensions={0} | all-to-all | bytes 1572864 | tf_op jit(solution)/shard_map/all_to_all | solution.py:155
  357.4 8.5 fusion.98
  365.9 17.8 %all-gather.20.cloned.1.call-done = bf16[2048,1536]{1,0:T(8,128)(2,1)} async-done(((bf16[256,1536]{1,0:T(8,128)(2,1)}), bf16[2048,1536]{1,0:T(8,128)(2,1)}) %all-gather.20.cloned.1.call-update) | async-done | bytes 6291472 | tf_op jit(solution)/shard_map/all_gather | solution.py:157
  383.7 8.6 fusion.99
  392.3 39.3 %all-gather.24.cloned.1.call-done = bf16[512,2048]{0,1:T(8,128)(2,1)} async-done(((bf16[128,2048]{0,1:T(8,128)(2,1)}), bf16[512,2048]{0,1:T(8,128)(2,1)}) %all-gather.24.cloned.1.call-update) | async-done | bytes 2097168 | tf_op jit(solution)/shard_map/all_gather | solution.py:139
  431.5 45.7 %all-gather.22.cloned.1.call-done = bf16[2048,1536]{1,0:T(8,128)(2,1)} async-done(((bf16[256,1536]{1,0:T(8,128)(2,1)}), bf16[2048,1536]{1,0:T(8,128)(2,1)}) %all-gather.22.cloned.1.call-update) | async-done | bytes 6291472 | tf_op jit(solution)/shard_map/all_gather | solution.py:157
  477.2 11.3 %multiply_convert_fusion = (bf16[512,1536]{1,0:T(8,128)(2,1)S(1)}, bf16[512,1536]{1,0:T(8,128)(2,1)S(1)}, bf16[512,1536]{1,0:T(8,128)(2,1)}) fusion(f32[512,1536]{1,0:T(8,128)} %fusion.98, f32[512,1536]{1,0:T(8,128)} %fusion.99, bf16[512,2048]{0,1:T(8,128)(2,1)} %all-gather.24.cloned.1.call-done, bf16[2048,1536]{1,0:T(8,128)(2,1)} %all-gather.22.cloned.1.call-done), kind=kOutput, calls=%fused_computation.77 | convolution fusion | flops 3233021952 | bytes 19398656 | tf_op jit(solution)/shard_map/dot_general | solution.py:46
  488.5 6.7 fusion.100
  495.3 4.7 add_convert_fusion
  500.0 4.6 all-to-all-start.6
  506.9 46.5 %all-to-all-done.6 = bf16[4,128,2048]{2,1,0:T(8,128)(2,1)} async-done(((bf16[4,128,2048]{2,1,0:T(8,128)(2,1)}), bf16[4,128,2048]{2,1,0:T(8,128)(2,1)}, u32[]{:S(2)}, u32[]{:S(2)}) %all-to-all-start.6) | async-done | bytes 2097184 | tf_op jit(solution)/shard_map/all_to_all | solution.py:145
  563.5 8.2 convolution_convert_fusion.2
  573.4 6.7 convolution_convert_fusion.1
  583.3 8.3 fusion.48
  591.6 8.1 convolution_convert_fusion.5
  599.7 8.0 all-gather.26.cloned.1.call-done
  611.5 42.6 %while.41 = (s32[]{:T(128)}, f32[512,2,2,128]{0,3,2,1:T(8,128)}, f32[4,512,2,128]{3,1,0,2:T(8,128)}, bf16[4,512,2,128]{3,1,0,2:T(8,128)(2,1)}, bf16[4,512,2,128]...) while((s32[]{:T(128)}, f32[512,2,2,128]{0,3,2,1:T(8,128)}, ...), condition=%wide.region_17.18_spmd.clone, body=%wide.region_16.17_spmd.clone.sunk | while | flops 1351352320 | bytes 59017940 | solution.py:128
  659.1 10.8 %copy.358 = bf16[2048,4,128]{2,1,0:T(4,128)(2,1)} copy(bf16[2048,4,128]{2,0,1:T(8,128)(2,1)S(1)} %pad_maximum_fusion.1) | data formatting | bytes 4194304 | tf_op jit(solution)/shard_map/concatenate | solution.py:311
  669.9 4.1 convert_element_type.187
  674.0 5.0 all-to-all-start.7
  696.2 12.2 %all-to-all-done.7 = bf16[4,512,512]{2,1,0:T(8,128)(2,1)} async-done(((bf16[4,512,512]{2,1,0:T(8,128)(2,1)}), bf16[4,512,512]{2,1,0:T(8,128)(2,1)}, u32[]{:S(2)}, u32[]{:S(2)}) %all-to-all-start.7) | async-done | bytes 2097184 | tf_op jit(solution)/shard_map/all_to_all | solution.py:313
  729.8 5.3 pad_maximum_fusion
  735.1 22.5 %all-to-all-done.5 = bf16[4,128,2048]{2,1,0:T(8,128)(2,1)S(1)} async-done(((bf16[4,128,2048]{2,1,0:T(8,128)(2,1)}), bf16[4,128,2048]{2,1,0:T(8,128)(2,1)S(1)}, u32[]{:S(2)}, u32[]{:S(2)}) %all-to-all-start.5) | async-done | bytes 2097184 | tf_op jit(solution)/shard_map/all_to_all | solution.py:145
  761.3 19.5 %all-to-all-done.10 = bf16[4,64,1536]{2,1,0:T(8,128)(2,1)S(1)} async-done(((bf16[4,64,1536]{2,1,0:T(8,128)(2,1)}), bf16[4,64,1536]{2,1,0:T(8,128)(2,1)S(1)}, u32[]{:S(2)}, u32[]{:S(2)}) %all-to-all-start.10) | async-done | bytes 786464 | tf_op jit(solution)/shard_map/all_to_all | solution.py:163
  780.8 4.2 all-to-all-start.11
  785.0 17.8 %reduce-scatter.11.cloned.1.call-done = bf16[256,1536]{0,1:T(8,128)(2,1)} async-done(((bf16[2048,1536]{0,1:T(8,128)(2,1)}), bf16[256,1536]{0,1:T(8,128)(2,1)}) %reduce-scatter.11.cloned.1.call-update) | async-done | bytes 786448 | tf_op jit(solution)/shard_map/reduce_scatter | solution.py:161
  805.1 4.8 all-to-all-start.12
  809.9 6.5 fusion.57
  816.4 13.7 %all-to-all-done.12 = bf16[4,64,1536]{2,1,0:T(8,128)(2,1)} async-done(((bf16[4,64,1536]{2,1,0:T(8,128)(2,1)}), bf16[4,64,1536]{2,1,0:T(8,128)(2,1)}, u32[]{:S(2)}, u32[]{:S(2)}) %all-to-all-start.12) | async-done | bytes 786464 | tf_op jit(solution)/shard_map/all_to_all | solution.py:163
  830.1 4.5 all-to-all-start.8
  839.7 62.0 %psum.7 = f32[2,128]{1,0:T(2,128)S(1)} all-reduce(f32[2,128]{1,0:T(2,128)S(1)} %pad_maximum_fusion.9), channel_id=1, replica_groups=mesh['z'=4,'p'=4,'c'=2] {'z','p','c'}, use_global_device_ids=true, to_apply=%region_33.34 | all-reduce | flops 256 | bytes 2048 | tf_op jit(solution)/shard_map/psum | solution.py:347
  919.0 4.2 all-to-all-start.9
  923.2 23.9 %all-reduce.1 = f32[8,4,64,2]{2,1,3,0:T(4,128)S(1)} all-reduce(f32[8,4,64,2]{2,1,3,0:T(4,128)S(1)} %copy.377), channel_id=6, replica_groups=mesh['z'=4,'p'=4,'c'=2] {'p','c'}, use_global_device_ids=true, to_apply=%region_29.30.clone | all-reduce | flops 4096 | bytes 32768
  954.7 11.4 %all-reduce.2 = f32[4,64,2]{1,2,0:T(2,128)S(1)} all-reduce(f32[4,64,2]{1,2,0:T(2,128)S(1)} %copy.378), channel_id=7, replica_groups=mesh['z'=4,'p'=4,'c'=2] {'z'}, use_global_device_ids=true, to_apply=%region_30.31.clone | all-reduce | flops 512 | bytes 4096
  (405 shorter events, 230.5 us)
Async XLA Ops:
  7.2 66.5 %all-gather.10.cloned.1.call-start = ((), (), s32[]{:S(2)}) async-start(), calls=%async_computation.17 | async-start | bytes 2621440 | tf_op jit(solution)/shard_map/all_gather | solution.py:139
  8.7 550.3 %copy-start.5 = (bf16[1,128,2048]{1,2,0:T(8,128)(2,1)}, bf16[1,128,2048]{1,2,0:T(8,128)(2,1)S(1)}, u32[]{:S(2)}) copy-start(bf16[1,128,2048]{1,2,0:T(8,128)(2,1)S(1)} %copy.313) | copy-start | bytes 1572868
  9.6 114.5 %all-gather.12.cloned.1.call-start = ((), (), s32[]{:S(2)}) async-start(), calls=%async_computation.18 | async-start | bytes 7667712 | tf_op jit(solution)/shard_map/all_gather | solution.py:157
  11.0 48.5 %copy-start.56 = (bf16[128]{0:T(256)(128)(2,1)S(1)}, bf16[128]{0:T(256)(128)(2,1)}, u32[]{:S(2)}) copy-start(bf16[128]{0:T(256)(128)(2,1)} %param.32) | copy-start | bytes 772
  11.0 48.5 %copy-start.57 = (s32[1,32]{1,0:T(1,128)S(1)}, s32[1,32]{1,0:T(1,128)}, u32[]{:S(2)}) copy-start(s32[1,32]{1,0:T(1,128)} %param.21) | copy-start | bytes 388
  59.5 111.0 %all-gather.14.cloned.1.call-start = ((), (), s32[]{:S(2)}) async-start(), calls=%async_computation.19 | async-start | bytes 2621440 | tf_op jit(solution)/shard_map/all_gather | solution.py:260
  59.5 74.2 %copy-start.48 = (f32[128]{0:T(128)}, f32[128]{0:T(128)S(1)}, u32[]{:S(2)}) copy-start(f32[128]{0:T(128)S(1)} %convert_element_type.162) | copy-start | bytes 1540
  61.9 81.4 %copy-start.17 = (f32[512,128]{1,0:T(8,128)}, f32[512,128]{1,0:T(8,128)S(1)}, u32[]{:S(2)}) copy-start(f32[512,128]{1,0:T(8,128)S(1)} %get-tuple-element.603) | copy-start | bytes 786436
  61.9 82.2 %copy-start.15 = (f32[512,128]{1,0:T(8,128)}, f32[512,128]{1,0:T(8,128)S(1)}, u32[]{:S(2)}) copy-start(f32[512,128]{1,0:T(8,128)S(1)} %get-tuple-element.602) | copy-start | bytes 786436
  75.8 55.2 %copy-start.50 = (f32[512]{0:T(512)}, f32[512]{0:T(512)S(1)}, u32[]{:S(2)}) copy-start(f32[512]{0:T(512)S(1)} %add_rsqrt_fusion.2) | copy-start | bytes 6148
  135.0 10.0 %copy-start.58 = (bf16[128]{0:T(256)(128)(2,1)S(1)}, bf16[128]{0:T(256)(128)(2,1)}, u32[]{:S(2)}) copy-start(bf16[128]{0:T(256)(128)(2,1)} %param.31) | copy-start | bytes 772
  138.3 26.2 %slice-start = ((f32[512,1024]{1,0:T(8,128)}), f32[512,512]{1,0:T(8,128)S(1)}, s32[]{:S(2)}) async-start(f32[512,1024]{1,0:T(8,128)} %copy-done.24), calls=%async_computation.30 | async-start | bytes 2097152 | tf_op jit(solution)/shard_map/slice | solution.py:250
  138.3 25.3 %all-to-all-start.2 = ((bf16[4,64,1536]{2,1,0:T(8,128)(2,1)}), bf16[4,64,1536]{2,1,0:T(8,128)(2,1)S(1)}, u32[]{:S(2)}, u32[]{:S(2)}) async-start(bf16[4,64,1536]{2,1,0:T(8,128)(2,1)} %copy.333), calls=%async_computation.2 | async-start | bytes 1572864 | tf_op jit(solution)/shard_map/all_to_all | solution.py:155
  143.1 214.3 %all-gather.18.cloned.1.call-start = ((), (), s32[]{:S(2)}) async-start(), calls=%async_computation.21 | async-start | bytes 7077888 | tf_op jit(solution)/shard_map/all_gather | solution.py:157
  212.6 6.6 copy-start.19
  219.2 53.1 %all-to-all-start.1 = ((bf16[4,128,2048]{2,1,0:T(8,128)(2,1)}), bf16[4,128,2048]{2,1,0:T(8,128)(2,1)}, u32[]{:S(2)}, u32[]{:S(2)}) async-start(bf16[4,128,2048]{2,1,0:T(8,128)(2,1)} %bitcast.414), calls=%async_computation.1 | async-start | bytes 4194304 | tf_op jit(solution)/shard_map/all_to_all | solution.py:145
  224.0 133.4 %all-gather.16.cloned.1.call-start = ((), (), s32[]{:S(2)}) async-start(), calls=%async_computation.20 | async-start | bytes 2621440 | tf_op jit(solution)/shard_map/all_gather | solution.py:139
  274.7 284.3 %copy-start.7 = (f32[128,2048]{0,1:T(8,128)}, f32[128,2048]{0,1:T(8,128)S(1)}, u32[]{:S(2)}) copy-start(f32[128,2048]{0,1:T(8,128)S(1)} %copy.330) | copy-start | bytes 3145732
  277.1 106.6 %all-gather.20.cloned.1.call-start = ((), (), s32[]{:S(2)}) async-start(), calls=%async_computation.22 | async-start | bytes 7077888 | tf_op jit(solution)/shard_map/all_gather | solution.py:157
  325.7 105.9 %all-gather.24.cloned.1.call-start = ((), (), s32[]{:S(2)}) async-start(), calls=%async_computation.24 | async-start | bytes 2621440 | tf_op jit(solution)/shard_map/all_gather | solution.py:139
  329.7 147.5 %all-gather.22.cloned.1.call-start = ((), (), s32[]{:S(2)}) async-start(), calls=%async_computation.23 | async-start | bytes 7077888 | tf_op jit(solution)/shard_map/all_gather | solution.py:157
  477.2 18.1 %slice-start.1 = ((s8[6291456]{0:T(1024)(128)(4,1)}), s8[4194304]{0:T(1024)(128)(4,1)S(1)}, s32[]{:S(2)}) async-start(s8[6291456]{0:T(1024)(128)(4,1)} %bitcast.442), calls=%async_computation.31 | async-start | bytes 8388608
  488.5 6.8 copy-start.62
  488.5 6.8 copy-start.61
  488.5 6.8 slice-start.2
  500.0 53.4 %all-to-all-start.6 = ((bf16[4,128,2048]{2,1,0:T(8,128)(2,1)}), bf16[4,128,2048]{2,1,0:T(8,128)(2,1)}, u32[]{:S(2)}, u32[]{:S(2)}) async-start(bf16[4,128,2048]{2,1,0:T(8,128)(2,1)} %bitcast.413), calls=%async_computation.6 | async-start | bytes 4194304 | tf_op jit(solution)/shard_map/all_to_all | solution.py:145
  504.6 103.1 %all-gather.26.cloned.1.call-start = ((), (), s32[]{:S(2)}) async-start(), calls=%async_computation.25 | async-start | bytes 2621440 | tf_op jit(solution)/shard_map/all_gather | solution.py:139
  563.5 194.2 %reduce-scatter.7.cloned.1.call-start = ((), (), s32[]{:S(2)}) async-start(), calls=%async_computation.27 | async-start | bytes 7077888 | tf_op jit(solution)/shard_map/reduce_scatter | solution.py:161
  571.8 189.5 %reduce-scatter.9.cloned.1.call-start = ((), (), s32[]{:S(2)}) async-start(), calls=%async_computation.28 | async-start | bytes 7077888 | tf_op jit(solution)/shard_map/reduce_scatter | solution.py:161
  580.1 222.7 %reduce-scatter.11.cloned.1.call-start = ((), (), s32[]{:S(2)}) async-start(), calls=%async_computation.29 | async-start | bytes 7077888 | tf_op jit(solution)/shard_map/reduce_scatter | solution.py:161
  591.6 16.1 %copy-start.29 = (f32[512,2,2,128]{0,3,2,1:T(8,128)S(1)}, f32[512,2,2,128]{0,3,2,1:T(8,128)}, u32[]{:S(2)}) copy-start(f32[512,2,2,128]{0,3,2,1:T(8,128)} %get-tuple-element.169) | copy-start | bytes 3145732
  674.0 34.4 %all-to-all-start.7 = ((bf16[4,512,512]{2,1,0:T(8,128)(2,1)}), bf16[4,512,512]{2,1,0:T(8,128)(2,1)}, u32[]{:S(2)}, u32[]{:S(2)}) async-start(bf16[4,512,512]{2,1,0:T(8,128)(2,1)} %convert_element_type.187), calls=%async_computation.7 | async-start | bytes 4194304 | tf_op jit(solution)/shard_map/all_to_all | solution.py:313
  708.4 49.2 %all-to-all-start.5 = ((bf16[4,128,2048]{2,1,0:T(8,128)(2,1)}), bf16[4,128,2048]{2,1,0:T(8,128)(2,1)S(1)}, u32[]{:S(2)}, u32[]{:S(2)}) async-start(bf16[4,128,2048]{2,1,0:T(8,128)(2,1)} %bitcast.411), calls=%async_computation.5 | async-start | bytes 4194304 | tf_op jit(solution)/shard_map/all_to_all | solution.py:145
  712.0 204.7 %reduce-scatter.5.cloned.1.call-start = ((), (), s32[]{:S(2)}) async-start(), calls=%async_computation.26 | async-start | bytes 7077888 | tf_op jit(solution)/shard_map/reduce_scatter | solution.py:161
  717.6 7.3 copy-start.10
  717.6 7.3 copy-start.43
  717.6 7.4 copy-start.49
  757.6 52.3 %copy-start.36 = (bf16[512,512]{1,0:T(8,128)(2,1)S(1)}, bf16[512,512]{1,0:T(8,128)(2,1)}, u32[]{:S(2)}) copy-start(bf16[512,512]{1,0:T(8,128)(2,1)} %fusion.78) | copy-start | bytes 1572868
  757.6 23.2 %all-to-all-start.10 = ((bf16[4,64,1536]{2,1,0:T(8,128)(2,1)}), bf16[4,64,1536]{2,1,0:T(8,128)(2,1)S(1)}, u32[]{:S(2)}, u32[]{:S(2)}) async-start(bf16[4,64,1536]{2,1,0:T(8,128)(2,1)} %bitcast.423), calls=%async_computation.12 | async-start | bytes 1572864 | tf_op jit(solution)/shard_map/all_to_all | solution.py:163
  780.8 24.3 %all-to-all-start.11 = ((bf16[4,64,1536]{2,1,0:T(8,128)(2,1)}), bf16[4,64,1536]{2,1,0:T(8,128)(2,1)}, u32[]{:S(2)}, u32[]{:S(2)}) async-start(bf16[4,64,1536]{2,1,0:T(8,128)(2,1)} %bitcast.422), calls=%async_computation.14 | async-start | bytes 1572864 | tf_op jit(solution)/shard_map/all_to_all | solution.py:163
  805.1 25.0 %all-to-all-start.12 = ((bf16[4,64,1536]{2,1,0:T(8,128)(2,1)}), bf16[4,64,1536]{2,1,0:T(8,128)(2,1)}, u32[]{:S(2)}, u32[]{:S(2)}) async-start(bf16[4,64,1536]{2,1,0:T(8,128)(2,1)} %bitcast.65), calls=%async_computation.16 | async-start | bytes 1572864 | tf_op jit(solution)/shard_map/all_to_all | solution.py:163
  816.4 18.2 %copy-start.60 = (u32[32]{0:T(128)S(1)}, u32[32]{0:T(128)}, u32[]{:S(2)}) copy-start(u32[32]{0:T(128)} %constant.107) | copy-start | bytes 388
  816.4 18.8 %copy-start.59 = (u32[32]{0:T(128)S(1)}, u32[32]{0:T(128)}, u32[]{:S(2)}) copy-start(u32[32]{0:T(128)} %constant.111) | copy-start | bytes 388
  830.1 78.8 %all-to-all-start.8 = ((bf16[4,128,2048]{2,1,0:T(8,128)(2,1)}), bf16[4,128,2048]{2,1,0:T(8,128)(2,1)}, u32[]{:S(2)}, u32[]{:S(2)}) async-start(bf16[4,128,2048]{2,1,0:T(8,128)(2,1)} %bitcast.412), calls=%async_computation.8 | async-start | bytes 4194304 | tf_op jit(solution)/shard_map/all_to_all | solution.py:145
  912.1 35.7 %copy-start.8 = (f32[128,2048]{0,1:T(8,128)S(1)}, f32[128,2048]{0,1:T(8,128)}, u32[]{:S(2)}) copy-start(f32[128,2048]{0,1:T(8,128)} %copy-done.7) | copy-start | bytes 3145732
  912.1 35.7 %copy-start.14 = (f32[128,2048]{0,1:T(8,128)S(1)}, f32[128,2048]{0,1:T(8,128)}, u32[]{:S(2)}) copy-start(f32[128,2048]{0,1:T(8,128)} %copy.340) | copy-start | bytes 3145732
  912.1 35.7 %copy-start.20 = (bf16[1,128,2048]{1,2,0:T(8,128)(2,1)S(1)}, bf16[1,128,2048]{1,2,0:T(8,128)(2,1)}, u32[]{:S(2)}) copy-start(bf16[1,128,2048]{1,2,0:T(8,128)(2,1)} %copy.338) | copy-start | bytes 1572868
  919.0 48.3 %all-to-all-start.9 = ((bf16[4,64,1536]{2,1,0:T(8,128)(2,1)}), bf16[4,64,1536]{2,1,0:T(8,128)(2,1)}, u32[]{:S(2)}, u32[]{:S(2)}) async-start(bf16[4,64,1536]{2,1,0:T(8,128)(2,1)} %bitcast.401), calls=%async_computation.10 | async-start | bytes 1572864 | tf_op jit(solution)/shard_map/all_to_all | solution.py:163
  (47 other events, 136.3 us)
Sparse Core Ops, SparseCore 0:
  10.2 63.4 all-gather.9
  75.6 48.4 all-gather.11
  135.1 35.2 all-gather.13
  172.8 45.5 all-gather.17
  277.2 60.8 all-gather.15
  339.9 43.7 all-gather.19
  385.3 46.2 all-gather.23
  433.4 43.7 all-gather.21
  563.6 44.0 all-gather.25
  610.9 60.4 reduce-scatter.6
  675.2 62.6 reduce-scatter.8
  741.1 61.7 reduce-scatter.10
  806.6 62.2 reduce-scatter.4

commit v2 on v1

v2 whole, which is shorter than its diff:
```python
import functools

import jax
import jax.numpy as jnp
from jax import lax
from jax.experimental import pallas as pl
from jax.experimental.pallas import tpu as pltpu
from jax.sharding import Mesh, PartitionSpec as P

epsilon = 1e-06
rotary_base = 1000000.0
masked_score = -1e30
parts = 4
bf16 = jnp.bfloat16
f32 = jnp.float32


def unit_rows(values):
    scale_row = lax.rsqrt(jnp.mean(values * values, axis=-1, keepdims=True) + epsilon)
    return values * scale_row, scale_row


def norm_back(weighted, unit, scale_row):
    inner_mean = jnp.mean(weighted * unit, axis=-1, keepdims=True)
    return scale_row * (weighted - unit * inner_mean)


def rope_tables(positions, width):
    half_width = width // 2
    frequency = rotary_base ** (-(jnp.arange(half_width, dtype=f32) * 2.0 / width))
    angles = positions.astype(f32)[:, None] * frequency[None, :]
    angles = jnp.concatenate([angles, angles], axis=-1)
    return jnp.cos(angles)[:, None, :], jnp.sin(angles)[:, None, :]


def rotate(values, cosine, sine_table):
    half_width = values.shape[-1] // 2
    turned = jnp.concatenate([-values[..., half_width:], values[..., :half_width]], axis=-1)
    return values * cosine + turned * sine_table


def rotate_back(grads, cosine, sine_table):
    half_width = grads.shape[-1] // 2
    shifted = grads * sine_table
    turned = jnp.concatenate([shifted[..., half_width:], -shifted[..., :half_width]], axis=-1)
    return grads * cosine + turned


def multiply(left, right):
    return jnp.dot(left, right, preferred_element_type=f32)


def multiply_trans(left, right):
    return lax.dot_general(left, right, (((1,), (1,)), ((), ())), preferred_element_type=f32)


def outer_rows(left, right):
    return lax.dot_general(left, right, (((0,), (0,)), ((), ())), preferred_element_type=f32)


def spread(pieces):
    return pieces.astype(f32).transpose(1, 0, 2).reshape(pieces.shape[1], -1)


class Links:
    def __init__(self, send_sems, recv_sems, local_sems):
        self.send_sems, self.recv_sems, self.local_sems = send_sems, recv_sems, local_sems
        self.count, self.local_count = 0, 0
        self.sent, self.kept = [], []

    def send(self, source, target, **device):
        index = self.count
        self.count += 1
        copy = pltpu.make_async_remote_copy(
            src_ref=source,
            dst_ref=target,
            send_sem=self.send_sems.at[index],
            recv_sem=self.recv_sems.at[index],
            device_id=device,
            device_id_type=pl.DeviceIdType.MESH,
        )
        copy.start()
        self.sent.append(copy)
        return copy

    def local(self, source, target):
        index = self.local_count
        self.local_count += 1
        copy = pltpu.make_async_copy(source, target, self.local_sems.at[index])
        copy.start()
        return copy

    def keep(self, source, target):
        self.kept.append(self.local(source, target))

    def finish(self):
        for copy in self.sent:
            copy.wait_send()
        for copy in self.kept:
            copy.wait()


class Place:
    def __init__(self, plane, cores):
        self.plane, self.cores = plane, cores
        self.z, self.p, self.c = (lax.axis_index(axis) for axis in ("z", "p", "c"))
        self.column = self.p * cores + self.c

    def along_z(self, step):
        return lax.rem(self.z + step, parts)

    def in_plane(self, step):
        return lax.rem(self.p + step, self.plane)

    def before(self, step):
        return lax.rem(self.p + self.plane - step, self.plane) * self.cores + self.c

    def siblings(self):
        return [lax.rem(self.c + step, self.cores) for step in range(1, self.cores)]


z_steps = (1, 3, 2)


class Fetch:
    def __init__(self, links, place, pieces, gathered):
        self.links, self.place, self.pieces, self.gathered = links, place, pieces, gathered

    def begin(self):
        links, place = self.links, self.place
        mine = self.gathered.at[place.z, place.column]
        self.first, self.own = [], []
        for shard, width, start, split in self.pieces:
            for step in z_steps:
                other = place.along_z(step)
                at = pl.multiple_of(other * width, 128) if split else 0
                self.first.append(
                    links.send(shard.at[:, pl.ds(at, width)], mine.at[:, pl.ds(start, width)], z=other)
                )
            at = pl.multiple_of(place.z * width, 128) if split else 0
            self.own.append(
                links.local(shard.at[:, pl.ds(at, width)], mine.at[:, pl.ds(start, width)])
            )

    def spread(self):
        links, place = self.links, self.place
        for copy in self.own:
            copy.wait()
        for copy in self.first:
            copy.wait_recv()
        block = self.gathered.at[:, place.column]
        self.second = [
            links.send(block, block, p=place.in_plane(step)) for step in range(1, place.plane)
        ]
        self.third = [links.send(block, block, c=other) for other in place.siblings()]

    def forward(self):
        links, place = self.links, self.place
        for step, copy in enumerate(self.second, 1):
            copy.wait_recv()
            block = self.gathered.at[:, place.before(step)]
            self.third += [links.send(block, block, c=other) for other in place.siblings()]

    def finish(self):
        for copy in self.third:
            copy.wait_recv()


def front_kernel(
    plane,
    cores,
    hidden,
    query_weight,
    key_weight,
    value_weight,
    out_weight,
    gate_weight,
    up_weight,
    down_weight,
    gain_block,
    grad_out,
    cosine,
    sine_turned,
    query_pos,
    key_pos,
    query_gain,
    key_gain,
    normed_out,
    projection_out,
    lin_out,
    queries_out,
    both_out,
    attended_out,
    out_columns_out,
    normed_mlp_out,
    residual_out,
    gate_out,
    up_out,
    down_out,
    grad_rows_out,
    stats_out,
    gains_out,
    hidden_all,
    normed,
    projection,
    lin,
    queries,
    both,
    attended_all,
    out_full,
    residual,
    normed_mlp,
    mixed,
    send_sems,
    recv_sems,
    local_sems,
):
    links = Links(send_sems, recv_sems, local_sems)
    place = Place(plane, cores)
    token_rows, width = hidden.shape
    tokens = parts * token_rows
    head = query_gain.shape[1]
    query_width = query_weight.shape[1] // parts
    key_width = key_weight.shape[1] // parts
    query_heads, key_heads = query_width // head, key_width // head
    group = query_heads // key_heads
    hidden_units = gate_weight.shape[1] // parts
    lin_width = query_width + 2 * key_width

    heads_fetch = Fetch(
        links,
        place,
        [
            (query_weight, query_width, 0, True),
            (key_weight, key_width, query_width, True),
            (value_weight, key_width, query_width + key_width, True),
            (gain_block, 128, lin_width, False),
        ],
        projection,
    )
    out_fetch = Fetch(links, place, [(out_weight, out_weight.shape[1], 0, False)], out_full)
    mlp_fetches = [
        Fetch(links, place, [(weight, hidden_units, 0, True)], target)
        for weight, target in ((gate_weight, gate_out), (up_weight, up_out), (down_weight, down_out))
    ]
    heads_fetch.begin()
    hidden_copies = [
        links.send(hidden, hidden_all.at[place.z], z=place.along_z(step)) for step in z_steps
    ]
    hidden_own = links.local(hidden, hidden_all.at[place.z])
    heads_fetch.spread()
    out_fetch.begin()
    for fetch in mlp_fetches:
        fetch.begin()
    hidden_own.wait()
    for copy in hidden_copies:
        copy.wait_recv()
    heads_fetch.forward()
    heads_fetch.finish()
    links.keep(projection, projection_out)

    gain_columns = projection[:, :, :, lin_width : lin_width + 128].reshape(width, 128)
    gain_rows = gain_columns.astype(f32).T
    gains_out[...] = gain_rows[:8]

    def norm_one(index, carry):
        values = hidden_all[index].astype(f32)
        scale = lax.rsqrt(jnp.mean(values * values, axis=-1, keepdims=True) + epsilon)
        rows = pl.ds(pl.multiple_of(index * token_rows, token_rows), token_rows)
        normed[rows] = (values * scale * gains_out[0:1]).astype(bf16)
        return carry

    lax.fori_loop(0, parts, norm_one, 0)
    links.keep(normed, normed_out)

    tile = 2 * head

    def project(index, carry):
        columns = pl.ds(pl.multiple_of(index * tile, tile), tile)
        weights = projection[:, :, :, columns].reshape(width, tile)
        lin[:, columns] = jnp.dot(normed[...], weights, preferred_element_type=f32)
        return carry

    lax.fori_loop(0, lin_width // tile, project, 0)
    own_both = both.at[place.p]

    def rope(values, gain):
        scale = lax.rsqrt(jnp.mean(values * values, axis=-1, keepdims=True) + epsilon)
        gained = values * scale * gain
        turned = pltpu.roll(gained, head // 2, 1)
        return (gained * cosine[...] + turned * sine_turned[...]).astype(bf16)

    for index in range(key_heads):
        columns = slice(query_width + index * head, query_width + (index + 1) * head)
        own_both[:, index * head : (index + 1) * head] = rope(lin[:, columns], key_gain[...])
    own_both[:, key_width:] = lin[:, query_width + key_width :].astype(bf16)
    both_copies = [
        links.send(own_both, own_both, p=place.in_plane(step)) for step in range(1, plane)
    ]
    for index in range(query_heads):
        columns = slice(index * head, (index + 1) * head)
        queries[index] = rope(lin[:, columns], query_gain[...])
    links.keep(lin.at[:, pl.ds(0, query_width + key_width)], lin_out)
    links.keep(queries, queries_out)
    out_fetch.spread()
    mlp_fetches[0].spread()
    for copy in both_copies:
        copy.wait_recv()
    links.keep(both, both_out)

    factor = head ** (-0.5) * 1.4426950408889634
    chunk = min(256, tokens)
    chunks_each = tokens // chunk
    lanes = group * tokens
    own_attended = attended_all.at[place.z]
    attended_copies = []
    for key_head in range(key_heads):
        block = queries[key_head * group : (key_head + 1) * group].reshape(lanes, head)
        positions = jnp.concatenate([query_pos[...]] * group, axis=1)
        mixed[...] = jnp.zeros_like(mixed)

        def attend_chunk(index, carry):
            best, summed = carry
            source, row = index // chunks_each, index % chunks_each
            rows = pl.ds(pl.multiple_of(row * chunk, chunk), chunk)
            keys = both[source, rows, pl.ds(key_head * head, head)]
            values = both[source, rows, pl.ds(key_width + key_head * head, head)]
            scores = multiply_trans(keys, block) * factor
            spot = pl.ds(pl.multiple_of(index * chunk, chunk), chunk)
            scores = jnp.where(key_pos[spot] <= positions, scores, masked_score)
            new_best = jnp.maximum(best, jnp.max(scores, axis=0, keepdims=True))
            weights = jnp.exp2(scores - new_best)
            shrink = jnp.exp2(best - new_best)
            summed = summed * shrink + jnp.sum(weights, axis=0, keepdims=True)
            mixed[...] = mixed[...] * shrink + outer_rows(values, weights.astype(bf16))
            return new_best, summed

        best, summed = lax.fori_loop(
            0,
            plane * chunks_each,
            attend_chunk,
            (jnp.full((1, lanes), masked_score, f32), jnp.zeros((1, lanes), f32)),
        )
        mixed_rows = (mixed[...] / summed).T
        stats = best + jnp.log2(summed)
        for member in range(group):
            index = key_head * group + member
            stats_out[index : index + 1] = stats[:, member * tokens : (member + 1) * tokens]
            own_attended[:, index * head : (index + 1) * head] = mixed_rows[
                member * tokens : (member + 1) * tokens
            ].astype(bf16)
        part = own_attended.at[:, pl.ds(key_head * group * head, group * head)]
        attended_copies += [links.send(part, part, z=place.along_z(step)) for step in z_steps]
        if key_head == 0:
            out_fetch.forward()
            mlp_fetches[1].spread()
    grad_copies = [
        links.send(grad_out, grad_rows_out.at[place.z], z=place.along_z(step)) for step in z_steps
    ]
    links.keep(grad_out, grad_rows_out.at[place.z])
    links.keep(own_attended, attended_out)
    mlp_fetches[2].spread()
    out_fetch.finish()
    links.keep(out_full, out_columns_out)
    for copy in attended_copies:
        copy.wait_recv()

    def add_out(index, carry):
        weights = out_full[index].reshape(width // parts, parts * query_width)
        columns = pl.ds(pl.multiple_of(index * (width // parts), 128), width // parts)
        total = hidden_all[:, :, columns].reshape(tokens, width // parts).astype(f32)
        for other in range(parts):
            total += multiply_trans(
                attended_all[other], weights[:, other * query_width : (other + 1) * query_width]
            )
        residual[:, columns] = total
        return carry

    lax.fori_loop(0, parts, add_out, 0)
    mlp_fetches[0].forward()

    def norm_two(index, carry):
        rows = pl.ds(pl.multiple_of(index * token_rows, token_rows), token_rows)
        values = residual[rows]
        scale = lax.rsqrt(jnp.mean(values * values, axis=-1, keepdims=True) + epsilon)
        normed_mlp[rows] = (values * scale * gains_out[1:2]).astype(bf16)
        return carry

    lax.fori_loop(0, parts, norm_two, 0)
    links.keep(normed_mlp, normed_mlp_out)
    own_rows = pl.ds(pl.multiple_of(place.z * token_rows, token_rows), token_rows)
    links.keep(residual.at[own_rows], residual_out)
    mlp_fetches[1].forward()
    mlp_fetches[2].forward()
    for copy in grad_copies:
        copy.wait_recv()
    for fetch in mlp_fetches:
        fetch.finish()
    links.finish()


def front(plane, cores, hidden, weights, gain_block, grad_out, tables, positions, head_gains):
    token_rows, width = hidden.shape
    tokens = parts * token_rows
    shard = weights[0].shape[0]
    head = head_gains[0].shape[1]
    query_width, key_width = weights[0].shape[1] // parts, weights[1].shape[1] // parts
    hidden_units = weights[4].shape[1] // parts
    lin_width = query_width + 2 * key_width
    query_heads = query_width // head
    group = query_width // key_width
    stacked = (parts, plane * cores, shard)
    copies = 3 * 7 + 3 * 3 + 3 * 2 + 5 * (2 * plane - 1) + plane + 8
    any_space, vmem = pl.BlockSpec(memory_space=pl.ANY), pl.BlockSpec(memory_space=pltpu.VMEM)
    outputs = [
        ((tokens, width), bf16),
        (stacked + (lin_width + 128,), bf16),
        ((tokens, query_width + key_width), f32),
        ((query_heads, tokens, head), bf16),
        ((plane, tokens, 2 * key_width), bf16),
        ((tokens, query_width), bf16),
        (stacked + (parts * query_width,), bf16),
        ((tokens, width), bf16),
        ((token_rows, width), f32),
        (stacked + (hidden_units,), bf16),
        (stacked + (hidden_units,), bf16),
        (stacked + (hidden_units,), bf16),
        ((parts, token_rows, width), bf16),
        ((8, tokens), f32),
        ((8, width), f32),
    ]
    return pl.pallas_call(
        functools.partial(front_kernel, plane, cores),
        out_shape=[jax.ShapeDtypeStruct(shape, kind) for shape, kind in outputs],
        in_specs=[any_space] * 10 + [vmem] * 6,
        out_specs=[any_space] * 13 + [vmem] * 2,
        scratch_shapes=[
            pltpu.VMEM((parts, token_rows, width), bf16),
            pltpu.VMEM((tokens, width), bf16),
            pltpu.VMEM(stacked + (lin_width + 128,), bf16),
            pltpu.VMEM((tokens, lin_width), f32),
            pltpu.VMEM((query_heads, tokens, head), bf16),
            pltpu.VMEM((plane, tokens, 2 * key_width), bf16),
            pltpu.VMEM((parts, tokens, query_width), bf16),
            pltpu.VMEM(stacked + (parts * query_width,), bf16),
            pltpu.VMEM((tokens, width), f32),
            pltpu.VMEM((tokens, width), bf16),
            pltpu.VMEM((head, group * tokens), f32),
            pltpu.SemaphoreType.DMA((copies,)),
            pltpu.SemaphoreType.DMA((copies,)),
            pltpu.SemaphoreType.DMA((32,)),
        ],
        compiler_params=pltpu.CompilerParams(
            has_side_effects=True, vmem_limit_bytes=60 * 1024 * 1024
        ),
        cost_estimate=pl.CostEstimate(flops=12 * 10**9, bytes_accessed=10**8, transcendentals=10**7),
    )(hidden, *weights, gain_block, grad_out, *tables, *positions, *head_gains)


def half_turn(values):
    return pltpu.roll(values, values.shape[1] // 2, 1)


def scatter_sends(links, place, piece, landed, token_rows, columns):
    copies = []
    for step in z_steps:
        other = place.along_z(step)
        rows = pl.ds(pl.multiple_of(other * token_rows, token_rows), token_rows)
        copies.append(
            links.send(piece.at[rows, columns], landed.at[place.z, :, columns], z=other)
        )
    return copies


def total_of(landed):
    total = landed[0].astype(f32)
    for index in range(1, parts):
        total += landed[index].astype(f32)
    return total


def mlp_kernel(
    plane,
    cores,
    normed_in,
    gate_in,
    up_in,
    down_in,
    grad_in,
    residual_in,
    gains,
    output,
    gate_grad,
    up_grad,
    down_grad,
    grad_residual,
    gain_sum,
    normed,
    normed_turned,
    grad_rows,
    grad_turned,
    gate,
    up,
    down,
    act,
    d_gate,
    d_up,
    part_in,
    part_out,
    landed_in,
    landed_out,
    residual,
    stage,
    stage_sems,
    send_sems,
    recv_sems,
    local_sems,
):
    links = Links(send_sems, recv_sems, local_sems)
    place = Place(plane, cores)
    tokens, width = normed.shape
    token_rows = tokens // parts
    units = act.shape[1]
    block = width // parts
    tile = 256
    loads = [
        links.local(normed_in, normed),
        links.local(gate_in, gate),
        links.local(up_in, up),
        links.local(grad_in, grad_rows),
        links.local(down_in, down),
        links.local(residual_in, residual),
    ]
    for copy in loads[:3]:
        copy.wait()

    for copy in loads[3:]:
        copy.wait()

    def hidden_tile(index, carry):
        columns = pl.ds(pl.multiple_of(index * tile, tile), tile)
        gate_lin = multiply(normed[...], gate[:, :, :, columns].reshape(width, tile))
        up_lin = multiply(normed[...], up[:, :, :, columns].reshape(width, tile))
        grad_act = multiply(
            grad_rows[...].reshape(tokens, width), down[:, :, :, columns].reshape(width, tile)
        )
        sigmoid = jax.nn.sigmoid(gate_lin)
        silu = gate_lin * sigmoid
        act[:, columns] = (silu * up_lin).astype(bf16)
        d_up[:, columns] = (grad_act * silu).astype(bf16)
        d_gate[:, columns] = (grad_act * up_lin * (sigmoid + silu * (1.0 - sigmoid))).astype(bf16)
        return carry

    lax.fori_loop(0, units // tile, hidden_tile, 0)
    in_copies, out_copies = [], []
    own_rows = pl.ds(pl.multiple_of(place.z * token_rows, token_rows), token_rows)
    for index in range(parts):
        columns = pl.ds(index * block, block)
        part_in[:, columns] = (
            multiply_trans(d_gate[...], gate[index].reshape(block, units))
            + multiply_trans(d_up[...], up[index].reshape(block, units))
        ).astype(bf16)
        in_copies += scatter_sends(links, place, part_in, landed_in, token_rows, columns)
    landed_in[place.z] = part_in[own_rows]
    for index in range(parts):
        columns = pl.ds(index * block, block)
        part_out[:, columns] = multiply_trans(
            act[...], down[index].reshape(block, units)
        ).astype(bf16)
        out_copies += scatter_sends(links, place, part_out, landed_out, token_rows, columns)
    landed_out[place.z] = part_out[own_rows]

    for index in range(parts):
        columns = slice(index * block, (index + 1) * block)
        normed_turned[columns] = normed[:, columns].T
        grad_turned[columns] = grad_rows[:, :, columns].reshape(tokens, block).T

    writes = []
    turn = 0
    for left, right, target in (
        (normed_turned, d_gate, gate_grad),
        (normed_turned, d_up, up_grad),
        (grad_turned, act, down_grad),
    ):
        for index in range(parts):
            slot = turn % 2
            if turn >= 2:
                writes[turn - 2].wait()

            def weight_tile(place_at, carry):
                columns = pl.ds(pl.multiple_of(place_at * tile, tile), tile)
                rows = left[index * block : (index + 1) * block]
                product = multiply(rows, right[:, columns]).astype(bf16)
                stage[slot, :, :, columns] = product.reshape(stage.shape[1], stage.shape[2], tile)
                return carry

            lax.fori_loop(0, units // tile, weight_tile, 0)
            copy = pltpu.make_async_copy(
                stage.at[slot], target.at[:, index], stage_sems.at[turn]
            )
            copy.start()
            writes.append(copy)
            turn += 1

    for copy in in_copies:
        copy.wait_recv()
    grad_normed = total_of(landed_in)
    values = residual[...]
    scale = lax.rsqrt(jnp.mean(values * values, axis=-1, keepdims=True) + epsilon)
    unit = values * scale
    gain_sum[0:1] = jnp.zeros((1, width), f32)
    gain_sum[1:2] = jnp.sum(grad_normed * unit, axis=0, keepdims=True)
    own_grad = grad_rows[place.z].astype(f32)
    grad_residual[...] = own_grad + norm_back(grad_normed * gains[1:2], unit, scale)
    for copy in out_copies:
        copy.wait_recv()
    output[...] = (residual[...] + total_of(landed_out)).astype(bf16)
    for copy in writes[-2:]:
        copy.wait()
    links.finish()


def mlp(plane, cores, normed, gate, up, down, grad_rows, residual, gains):
    tokens, width = normed.shape
    token_rows = tokens // parts
    units = gate.shape[3]
    shard = gate.shape[2]
    columns = plane * cores
    any_space, vmem = pl.BlockSpec(memory_space=pl.ANY), pl.BlockSpec(memory_space=pltpu.VMEM)
    grads = jax.ShapeDtypeStruct((columns, parts, shard, units), bf16)
    return pl.pallas_call(
        functools.partial(mlp_kernel, plane, cores),
        out_shape=[
            jax.ShapeDtypeStruct((token_rows, width), bf16),
            grads,
            grads,
            grads,
            jax.ShapeDtypeStruct((token_rows, width), f32),
            jax.ShapeDtypeStruct((2, width), f32),
        ],
        in_specs=[any_space] * 6 + [vmem],
        out_specs=[vmem] + [any_space] * 3 + [vmem] * 2,
        scratch_shapes=[
            pltpu.VMEM((tokens, width), bf16),
            pltpu.VMEM((width, tokens), bf16),
            pltpu.VMEM((parts, token_rows, width), bf16),
            pltpu.VMEM((width, tokens), bf16),
            pltpu.VMEM((parts, columns, shard, units), bf16),
            pltpu.VMEM((parts, columns, shard, units), bf16),
            pltpu.VMEM((parts, columns, shard, units), bf16),
            pltpu.VMEM((tokens, units), bf16),
            pltpu.VMEM((tokens, units), bf16),
            pltpu.VMEM((tokens, units), bf16),
            pltpu.VMEM((tokens, width), bf16),
            pltpu.VMEM((tokens, width), bf16),
            pltpu.VMEM((parts, token_rows, width), bf16),
            pltpu.VMEM((parts, token_rows, width), bf16),
            pltpu.VMEM((token_rows, width), f32),
            pltpu.VMEM((2, columns, shard, units), bf16),
            pltpu.SemaphoreType.DMA((12,)),
            pltpu.SemaphoreType.DMA((24,)),
            pltpu.SemaphoreType.DMA((24,)),
            pltpu.SemaphoreType.DMA((6,)),
        ],
        compiler_params=pltpu.CompilerParams(
            has_side_effects=True, vmem_limit_bytes=62 * 1024 * 1024
        ),
        cost_estimate=pl.CostEstimate(flops=3 * 10**10, bytes_accessed=10**8, transcendentals=10**6),
    )(normed, gate, up, down, grad_rows, residual, gains)


def back_kernel(
    plane,
    cores,
    projection_in,
    out_in,
    normed_in,
    lin_in,
    queries_in,
    both_in,
    attended_in,
    hidden,
    grad_residual,
    stats,
    gains,
    gain_sum,
    cosine,
    sine_turned,
    query_pos,
    key_pos,
    query_gain,
    key_gain,
    input_grad,
    weight_grads,
    head_sums,
    projection,
    out_columns,
    normed,
    lin,
    queries,
    both,
    attended,
    low_rows,
    grad_heads,
    delta,
    both_grads,
    both_landed,
    query_total,
    grad_lin,
    part,
    landed,
    stage,
    gain_stage,
    sums,
    stage_sems,
    send_sems,
    recv_sems,
    local_sems,
):
    links = Links(send_sems, recv_sems, local_sems)
    place = Place(plane, cores)
    tokens, width = normed.shape
    token_rows = tokens // parts
    block = width // parts
    head = query_gain.shape[1]
    query_heads = queries.shape[0]
    query_width = query_heads * head
    key_width = both.shape[2] // 2
    key_heads = key_width // head
    group = query_heads // key_heads
    lin_width = query_width + 2 * key_width

    low_rows[place.z] = grad_residual[...].astype(bf16)
    own_low = low_rows.at[place.z]
    low_copies = [links.send(own_low, own_low, z=place.along_z(step)) for step in z_steps]
    out_at = pl.ds(pl.multiple_of(place.z * query_width, 128), query_width)
    loads = [
        links.local(out_in.at[:, :, :, out_at], out_columns),
        links.local(attended_in, attended),
        links.local(queries_in, queries),
        links.local(both_in, both),
        links.local(lin_in, lin),
        links.local(projection_in, projection),
        links.local(normed_in, normed),
    ]
    for copy in loads:
        copy.wait()
    for copy in low_copies:
        copy.wait_recv()

    tile = group * head
    for index in range(key_heads):
        columns = slice(index * tile, (index + 1) * tile)
        grads = multiply(
            low_rows[...].reshape(tokens, width), out_columns[:, :, :, columns].reshape(width, tile)
        ).astype(bf16)
        for member in range(group):
            number = index * group + member
            own = grads[:, member * head : (member + 1) * head]
            grad_heads[number] = own
            mixed = attended[:, number * head : (number + 1) * head].astype(f32)
            delta[number : number + 1] = jnp.sum(
                (own.astype(f32) * mixed).T, axis=0, keepdims=True
            )

    factor = head ** (-0.5)
    score_factor = factor * 1.4426950408889634
    chunk = min(256, tokens)
    chunks_each = tokens // chunk
    lanes = group * tokens
    both_copies = []
    for key_head in range(key_heads):
        members = slice(key_head * group, (key_head + 1) * group)
        query_block = queries[members].reshape(lanes, head)
        grad_block = grad_heads[members].reshape(lanes, head)
        numbers = range(key_head * group, (key_head + 1) * group)
        stats_row = jnp.concatenate([stats[number : number + 1] for number in numbers], axis=1)
        delta_row = jnp.concatenate([delta[number : number + 1] for number in numbers], axis=1)
        positions = jnp.concatenate([query_pos[...]] * group, axis=1)
        query_total[...] = jnp.zeros_like(query_total)

        def back_chunk(index, carry):
            source, row = index // chunks_each, index % chunks_each
            rows = pl.ds(pl.multiple_of(row * chunk, chunk), chunk)
            keys = both[source, rows, pl.ds(key_head * head, head)]
            values = both[source, rows, pl.ds(key_width + key_head * head, head)]
            scores = multiply_trans(keys, query_block) * score_factor
            spot = pl.ds(pl.multiple_of(index * chunk, chunk), chunk)
            weights = jnp.where(
                key_pos[spot] <= positions, jnp.exp2(scores - stats_row), 0.0
            )
            grad_weights = multiply_trans(values, grad_block)
            grad_scores = (weights * (grad_weights - delta_row)).astype(bf16)
            query_total[...] += outer_rows(keys, grad_scores)
            both_grads[key_head, source, rows, pl.ds(0, head)] = (
                multiply(grad_scores, query_block) * factor
            ).astype(bf16)
            both_grads[key_head, source, rows, pl.ds(head, head)] = multiply(
                weights.astype(bf16), grad_block
            ).astype(bf16)
            return carry

        lax.fori_loop(0, plane * chunks_each, back_chunk, 0)
        both_landed[key_head, place.p] = both_grads[key_head, place.p]
        for step in range(1, plane):
            other = place.in_plane(step)
            both_copies.append(
                links.send(
                    both_grads.at[key_head, other], both_landed.at[key_head, place.p], p=other
                )
            )
        grad_queries = query_total[...].T * factor
        for member in range(group):
            number = key_head * group + member
            rows = slice(member * tokens, (member + 1) * tokens)
            own = grad_queries[rows]
            lin_rows = lin[:, number * head : (number + 1) * head]
            scale = lax.rsqrt(jnp.mean(lin_rows * lin_rows, axis=-1, keepdims=True) + epsilon)
            unit = lin_rows * scale
            turned = own * cosine[...] - half_turn(own) * sine_turned[...]
            gained = jnp.sum(turned * unit, axis=0, keepdims=True)
            if number == 0:
                sums[place.z, 0:1] = gained
            else:
                sums[place.z, 0:1] = sums[place.z, 0:1] + gained
            grad_lin[:, number * head : (number + 1) * head] = norm_back(
                turned * query_gain[...], unit, scale
            ).astype(bf16)

    writes = []

    def write_rows(left, right, start, index):
        turn = len(writes)
        slot = turn % 2
        if turn >= 2:
            writes[turn - 2].wait()
        size = right.shape[1]
        product = outer_rows(left, right).astype(bf16)
        stage[slot, :, :, 0:size] = product.reshape(stage.shape[1], stage.shape[2], size)
        copy = pltpu.make_async_copy(
            stage.at[slot, :, :, pl.ds(0, size)],
            weight_grads.at[:, index, :, pl.ds(start, size)],
            stage_sems.at[turn],
        )
        copy.start()
        writes.append(copy)

    for index in range(parts):
        left = low_rows[:, :, index * block : (index + 1) * block].reshape(tokens, block)
        write_rows(left, attended[...], lin_width, index)

    for copy in both_copies:
        copy.wait_recv()
    for key_head in range(key_heads):
        own = both_landed[key_head, 0].astype(f32)
        for source in range(1, plane):
            own += both_landed[key_head, source].astype(f32)
        at = query_width + key_width + key_head * head
        grad_lin[:, at : at + head] = own[:, head:].astype(bf16)
        own = own[:, :head]
        at = query_width + key_head * head
        lin_rows = lin[:, at : at + head]
        scale = lax.rsqrt(jnp.mean(lin_rows * lin_rows, axis=-1, keepdims=True) + epsilon)
        unit = lin_rows * scale
        turned = own * cosine[...] - half_turn(own) * sine_turned[...]
        gained = jnp.sum(turned * unit, axis=0, keepdims=True)
        if key_head == 0:
            sums[place.z, 1:2] = gained
        else:
            sums[place.z, 1:2] = sums[place.z, 1:2] + gained
        grad_lin[:, at : at + head] = norm_back(turned * key_gain[...], unit, scale).astype(bf16)
    head_sums[...] = sums[place.z]

    landed_copies = []
    for index in range(parts):
        columns = pl.ds(index * block, block)
        part[:, columns] = multiply_trans(
            grad_lin[...], projection[index, :, :, 0:lin_width].reshape(block, lin_width)
        ).astype(bf16)
        landed_copies += scatter_sends(links, place, part, landed, token_rows, columns)
    own_rows = pl.ds(pl.multiple_of(place.z * token_rows, token_rows), token_rows)
    landed[place.z] = part[own_rows]
    for index in range(parts):
        left = normed[:, index * block : (index + 1) * block]
        write_rows(left, grad_lin[...], 0, index)

    for copy in landed_copies:
        copy.wait_recv()
    grad_normed = total_of(landed)
    values = hidden[...].astype(f32)
    scale = lax.rsqrt(jnp.mean(values * values, axis=-1, keepdims=True) + epsilon)
    unit = values * scale
    gain_stage[...] = jnp.zeros_like(gain_stage)
    gain_stage[0:1] = jnp.sum(grad_normed * unit, axis=0, keepdims=True)
    gain_stage[1:2] = gain_sum[1:2]
    input_grad[...] = (
        grad_residual[...] + norm_back(grad_normed * gains[0:1], unit, scale)
    ).astype(bf16)
    gain_columns = gain_stage[...].T.astype(bf16)
    for index in range(parts):
        turn = len(writes)
        slot = turn % 2
        writes[turn - 2].wait()
        stage[slot, :, :, 0:128] = gain_columns[index * block : (index + 1) * block].reshape(
            stage.shape[1], stage.shape[2], 128
        )
        copy = pltpu.make_async_copy(
            stage.at[slot, :, :, pl.ds(0, 128)],
            weight_grads.at[:, index, :, pl.ds(lin_width + query_width, 128)],
            stage_sems.at[turn],
        )
        copy.start()
        writes.append(copy)
    for copy in writes[-2:]:
        copy.wait()
    links.finish()


def back(plane, cores, large, small):
    projection, out_full, normed, lin, queries, both, attended = large
    tokens, width = normed.shape
    token_rows = tokens // parts
    shard = projection.shape[2]
    columns = plane * cores
    query_heads, _, head = queries.shape
    query_width = query_heads * head
    key_width = both.shape[2] // 2
    key_heads = key_width // head
    lin_width = query_width + 2 * key_width
    group = query_heads // key_heads
    any_space, vmem = pl.BlockSpec(memory_space=pl.ANY), pl.BlockSpec(memory_space=pltpu.VMEM)
    copies = 3 + 2 * (plane - 1) + 12
    return pl.pallas_call(
        functools.partial(back_kernel, plane, cores),
        out_shape=[
            jax.ShapeDtypeStruct((token_rows, width), bf16),
            jax.ShapeDtypeStruct((columns, parts, shard, lin_width + query_width + 128), bf16),
            jax.ShapeDtypeStruct((8, head), f32),
        ],
        in_specs=[any_space] * 7 + [vmem] * 11,
        out_specs=[vmem, any_space, vmem],
        scratch_shapes=[
            pltpu.VMEM(projection.shape, bf16),
            pltpu.VMEM((parts, columns, shard, query_width), bf16),
            pltpu.VMEM((tokens, width), bf16),
            pltpu.VMEM(lin.shape, f32),
            pltpu.VMEM(queries.shape, bf16),
            pltpu.VMEM(both.shape, bf16),
            pltpu.VMEM(attended.shape, bf16),
            pltpu.VMEM((parts, token_rows, width), bf16),
            pltpu.VMEM(queries.shape, bf16),
            pltpu.VMEM((8, tokens), f32),
            pltpu.VMEM((key_heads, plane, tokens, 2 * head), bf16),
            pltpu.VMEM((key_heads, plane, tokens, 2 * head), bf16),
            pltpu.VMEM((head, group * tokens), f32),
            pltpu.VMEM((tokens, lin_width), bf16),
            pltpu.VMEM((tokens, width), bf16),
            pltpu.VMEM((parts, token_rows, width), bf16),
            pltpu.VMEM((2, columns, shard, lin_width), bf16),
            pltpu.VMEM((128, width), f32),
            pltpu.VMEM((parts, 8, head), f32),
            pltpu.SemaphoreType.DMA((12,)),
            pltpu.SemaphoreType.DMA((copies,)),
            pltpu.SemaphoreType.DMA((copies,)),
            pltpu.SemaphoreType.DMA((8,)),
        ],
        compiler_params=pltpu.CompilerParams(
            has_side_effects=True, vmem_limit_bytes=62 * 1024 * 1024
        ),
        cost_estimate=pl.CostEstimate(flops=10**10, bytes_accessed=10**8, transcendentals=10**7),
    )(*large, *small)


def make_local(plane, cores):
    def return_columns(grads):
        grads = grads.reshape(-1, grads.shape[3])
        summed = lax.psum_scatter(grads, ("p", "c"), scatter_dimension=0, tiled=True)
        pieces = summed.reshape(parts, summed.shape[0] // parts, summed.shape[1])
        return lax.all_to_all(pieces, "z", 0, 0, tiled=True)

    def local(
        hidden_in,
        block_map,
        query_weight,
        key_weight,
        value_weight,
        out_weight,
        gate_weight,
        up_weight,
        down_weight,
        attention_norm_gain,
        feedforward_gain,
        query_gain,
        key_gain,
        output_grad,
    ):
        shard = query_weight.shape[0]
        hidden_own, grad_own = hidden_in[0], output_grad[0]
        row_count, features = hidden_own.shape
        piece_rows = row_count // 2
        head_width = query_gain.shape[0]
        query_heads = query_weight.shape[1] // head_width // parts
        key_heads = key_weight.shape[1] // head_width // parts
        group_size = query_heads // key_heads
        query_width = query_heads * head_width
        key_width = key_heads * head_width
        hidden_units = gate_weight.shape[1] // parts
        p_index = lax.axis_index("p")
        tokens = parts * row_count

        blocks = block_map[0].reshape(parts, plane, 2)
        offsets = jnp.arange(piece_rows, dtype=jnp.int32)
        all_pos = blocks.transpose(1, 0, 2)[..., None] * piece_rows + offsets
        all_pos = all_pos.reshape(plane, tokens)
        query_pos = lax.dynamic_index_in_dim(all_pos, p_index, 0, keepdims=False)
        key_pos = all_pos.reshape(-1)
        cosine, sine_table = rope_tables(query_pos, head_width)
        sign = jnp.where(jnp.arange(head_width) < head_width // 2, -1.0, 1.0).astype(f32)
        query_gain_float = query_gain.astype(f32)
        key_gain_float = key_gain.astype(f32)
        gain_block = jnp.stack([attention_norm_gain, feedforward_gain], axis=1)
        gain_block = jnp.pad(gain_block, ((0, 0), (0, 126)))

        (
            normed,
            projection,
            lin,
            queries,
            both,
            attended_low,
            out_full,
            normed_mlp,
            own_residual,
            gate_columns,
            up_columns,
            down_columns,
            grad_rows,
            stats,
            gains,
        ) = front(
            plane,
            cores,
            hidden_own,
            (
                query_weight,
                key_weight,
                value_weight,
                out_weight,
                gate_weight,
                up_weight,
                down_weight,
            ),
            gain_block,
            grad_own,
            (cosine[:, 0], sine_table[:, 0] * sign),
            (query_pos[None], key_pos[:, None]),
            (query_gain_float[None], key_gain_float[None]),
        )
        output, gate_grads, up_grads, down_grads, grad_residual, gain_sum = mlp(
            plane,
            cores,
            normed_mlp,
            gate_columns,
            up_columns,
            down_columns,
            grad_rows,
            own_residual,
            gains,
        )
        down_pieces = return_columns(down_grads)
        gate_pieces = return_columns(gate_grads)
        up_pieces = return_columns(up_grads)
        input_grad, attention_grads, head_sums = back(
            plane,
            cores,
            (projection, out_full, normed, lin, queries, both, attended_low),
            (
                hidden_own,
                grad_residual,
                stats,
                gains,
                gain_sum,
                cosine[:, 0],
                sine_table[:, 0] * sign,
                query_pos[None],
                key_pos[:, None],
                query_gain_float[None],
                key_gain_float[None],
            ),
        )
        attention_pieces = return_columns(attention_grads)
        head_sums = lax.psum(head_sums[:2], ("z", "p", "c"))
        ends = [query_width, query_width + key_width, query_width + 2 * key_width]
        ends.append(ends[2] + query_width)
        gain_sums = jnp.sum(attention_pieces[:, :, ends[3] : ends[3] + 2].astype(f32), axis=0)
        return (
            output[None],
            input_grad[None],
            spread(attention_pieces[:, :, : ends[0]]),
            spread(attention_pieces[:, :, ends[0] : ends[1]]),
            spread(attention_pieces[:, :, ends[1] : ends[2]]),
            spread(attention_pieces[:, :, ends[2] : ends[3]]),
            spread(gate_pieces),
            spread(up_pieces),
            spread(down_pieces),
            gain_sums[:, 0],
            gain_sums[:, 1],
            head_sums[0],
            head_sums[1],
        )

    return local


def solution(mesh):
    ctx_count, core_count = mesh.shape["ctx"], mesh.shape["fsdp"]
    plane = ctx_count // parts
    fine_mesh = Mesh(mesh.devices.reshape(parts, plane, core_count), ("z", "p", "c"))
    token_spec = P("c", ("z", "p"), None)
    weight_spec = P(("z", "p", "c"), None)
    gain_spec = P(("z", "p", "c"))
    return jax.shard_map(
        make_local(plane, core_count),
        mesh=fine_mesh,
        in_specs=(
            (token_spec, P("c", None)) + (weight_spec,) * 7 + (gain_spec,) * 2 + (P(), P(), token_spec)
        ),
        out_specs=(token_spec,) * 2 + (weight_spec,) * 7 + (gain_spec,) * 2 + (P(), P()),
        check_vma=False,
    )
```

time: 990 us -> 723 us (0.73); the launches traced: 979 us -> 722 us
  Pallas kernels: 0 us -> 533 us
  waiting for transfers between devices: 373 us -> 99.6 us
  blocking collectives: 212 us -> 40.1 us
  matrix products: 161 us -> 0 us
  local copies, waits for them, and re-layouts: 97.1 us -> 13.5 us
  other arithmetic: 74.6 us -> 5.88 us
  starting transfers between devices: 45.4 us -> 16.4 us
    pallas_call x0 -> x3, Pallas kernels: none -> 533 us  [the longest x1 278 us: front(): pl.pallas_call(functools.partial(front_kernel, plane, cores), out_shape=[...]
    all_gather x9 -> x0, waiting for transfers between devices: 174 us -> none  [the longest x4 112 us: fetch_columns(): return lax.all_gather(pieces, ('p', 'c'), axis=0, tiled=True)]
    dot_general x43 -> x0, matrix products: 161 us -> none  [the longest x5 36.6 us: multiply(): return jnp.dot(left, right, preferred_element_type=f32)]
    all_to_all x6 -> x0, waiting for transfers between devices: 147 us -> none  [the longest x4 116 us: scatter_sum_z(): pieces = lax.all_to_all(pieces, 'z', 0, 0, tiled=True)]
    all_to_all x3 -> x0, blocking collectives: 115 us -> none  [fetch_columns(): pieces = lax.all_to_all(slices, 'z', 0, 0, tiled=True)]
    reduce_scatter x4, waiting for transfers between devices: 17.8 us -> 61.6 us  [return_columns(): lax.psum_scatter(grads, ('p', 'c'), scatter_dimension=0, tiled=True)]
    unnamed x2 -> x0, blocking collectives: 35.3 us -> none
    reduce_sum x17 -> x1, other arithmetic: 33.8 us -> 0.02 us  [local(): jnp.sum(attention_pieces[:, :, ends[3]:ends[3] + 2].astype(f32), axis=0)]
  transfers between devices with their start and end apart: 23 -> 8, of which waited for: 15 -> 4; matrix products, arithmetic and copies ran while one was open for 28% -> 1% of each run, Pallas kernels for 0% -> 19%
where the time goes in v2:
time: 723 us; the launch traced here: 722 us
  Pallas kernels  533 us (74%)
  waiting for transfers between devices  99.6 us (14%)
  blocking collectives  40.1 us (6%)
  starting transfers between devices  16.4 us (2%)
  between operations  13.9 us (2%)
  local copies, waits for them, and re-layouts  13.5 us (2%)
    pallas_call x1, Pallas kernels, front(): pl.pallas_call(functools.partial(front_kernel, plane, cores), out_shape=[...  278 us
    pallas_call x1, Pallas kernels, back(): pl.pallas_call(functools.partial(back_kernel, plane, cores), out_shape=[j...  134 us
    pallas_call x1, Pallas kernels, mlp(): pl.pallas_call(functools.partial(mlp_kernel, plane, cores), out_shape=[ja...  121 us
    reduce_scatter x4, waiting for transfers between devices, return_columns(): lax.psum_scatter(grads, ('p', 'c'), scatter_dimension=0, tiled=True)  61.6 us
    psum x1, blocking collectives, local(): head_sums = lax.psum(head_sums[:2], ('z', 'p', 'c'))  40.1 us
    all_to_all x4, waiting for transfers between devices, return_columns(): return lax.all_to_all(pieces, 'z', 0, 0, tiled=True)  36.6 us
    all_to_all x4, starting transfers between devices, return_columns(): return lax.all_to_all(pieces, 'z', 0, 0, tiled=True)  16.2 us
  transfers between devices with their start and end apart: 8, of which 4 were waited for; matrix products, arithmetic and copies ran while one was open for 1% of the time, Pallas kernels for 19%

profile of v2, /device:TPU:0, one launch (start us, length us, event | category | flops | bytes accessed | tf_op | source)
XLA Modules:
  0.0 722.3 jit_solution(5688972907821456794)
XLA Ops:
  7.2 0.0 reduce-scatter.11.cloned.1.call-start
  7.3 0.7 multiply_reduce_fusion
  7.9 0.1 add.53
  8.0 0.1 mul.43
  8.1 0.7 pad_maximum_fusion.1
  8.8 0.1 copy.60
  8.9 0.1 iota_add_fusion
  9.0 0.1 add.50
  9.1 0.1 add.51
  9.2 2.0 add.60.key_pos
  11.2 1.2 bitcast_convert_fusion
  12.4 0.6 pad.4.gain_block
  13.0 0.6 fusion.1
  13.6 0.1 broadcast_multiply_fusion
  13.7 1.8 sine_multiply_fusion
  15.5 278.4 %shard_map.237 = (bf16[512,2048]{1,0:T(8,128)(2,1)}, bf16[4,8,64,1152]{3,2,1,0:T(8,128)(2,1)}, f32[512,768]{1,0:T(8,128)}, bf16[4,512,128]{2,1,0:T(8,128)(2,1)},...) custom-call(bf16[128,2048]{1,0:T(8,128)(2,1)} %bitcast.78, ...), custom_call_target="tpu_custom_call" | custom-call | flops 12000000000 | bytes 100000000 | tf_op jit(solution)/shard_map/pallas_call | solution.py:432
  293.9 120.8 %shard_map.238 = (bf16[128,2048]{1,0:T(8,128)(2,1)}, bf16[8,4,64,1536]{3,2,1,0:T(8,128)(2,1)}, bf16[8,4,64,1536]{3,2,1,0:T(8,128)(2,1)}, bf16[8,4,64,1536]{3,2,1...) custom-call(bf16[512,2048]{1,0:T(8,128)(2,1)} %get-tuple-element.37.normed_in, ...), custom_call_target="tpu_custom_call" | custom-call | flops 30000001024 | bytes 100000000 | tf_op jit(solution)/shard_map/pallas_call | solution.py:631
  414.8 0.0 reduce-scatter.9.cloned.1.call-start
  414.8 0.7 reduce-scatter.9.cloned.1.call-update
  415.6 0.7 reduce-scatter.7.cloned.1.call-update
  416.3 0.0 reduce-scatter.5.cloned.1.call-start
  416.3 133.7 %shard_map.239 = (bf16[128,2048]{1,0:T(8,128)(2,1)}, bf16[8,4,64,1664]{3,2,1,0:T(8,128)(2,1)}, f32[8,128]{1,0:T(8,128)}) custom-call(bf16[4,8,64,1152]{3,2,1,0:T(8,128)(2,1)} %get-tuple-element.45.projection_in, bf16[4,8,64,2048]{3,2,1,0:T(8,128)(2,1)} %get-tuple-element.46.out_in, bf16[512,2048]{1,0:T(8,128)(2,1)} %get-tuple-element.47.normed_in, ...), custom_call_target="tpu_custom_call" | custom-call | flops 10000000000 | bytes 100000000 | tf_op jit(solution)/shard_map/pallas_call | solution.py:933
  550.1 3.5 all-to-all-start.3
  553.6 19.5 %all-to-all-done.3 = bf16[4,64,1536]{2,1,0:T(8,128)(2,1)S(1)} async-done(((bf16[4,64,1536]{2,1,0:T(8,128)(2,1)}), bf16[4,64,1536]{2,1,0:T(8,128)(2,1)S(1)}, u32[]{:S(2)}, u32[]{:S(2)}) %all-to-all-start.3) | async-done | bytes 786464 | tf_op jit(solution)/shard_map/all_to_all | solution.py:979
  573.1 3.5 all-to-all-start.2
  576.6 38.7 %reduce-scatter.7.cloned.1.call-done = bf16[256,1536]{1,0:T(8,128)(2,1)} async-done(((bf16[2048,1536]{1,0:T(8,128)(2,1)}), bf16[256,1536]{1,0:T(8,128)(2,1)}) %reduce-scatter.7.cloned.1.call-update) | async-done | bytes 786448 | tf_op jit(solution)/shard_map/reduce_scatter | solution.py:977
  615.3 4.6 all-to-all-start.1
  620.0 0.7 slice.37
  620.6 40.1 %psum.7 = f32[2,128]{1,0:T(2,128)S(1)} all-reduce(f32[2,128]{1,0:T(2,128)S(1)} %slice.37), channel_id=1, replica_groups=mesh['z'=4,'p'=4,'c'=2] {'z','p','c'}, use_global_device_ids=true, to_apply=%region_5.6 | all-reduce | flops 256 | bytes 2048 | tf_op jit(solution)/shard_map/psum | solution.py:1092
  660.7 0.5 slice_bitcast_fusion
  661.2 22.8 %reduce-scatter.5.cloned.1.call-done = bf16[256,1664]{1,0:T(8,128)(2,1)} async-done(((bf16[2048,1664]{1,0:T(8,128)(2,1)}), bf16[256,1664]{1,0:T(8,128)(2,1)}) %reduce-scatter.5.cloned.1.call-update) | async-done | bytes 851984 | tf_op jit(solution)/shard_map/reduce_scatter | solution.py:977
  684.0 4.6 all-to-all-start
  688.6 0.2 convert_bitcast_fusion.2
  688.8 1.3 copy.83
  690.1 0.2 convert_bitcast_fusion.1
  690.3 1.3 copy.84
  691.6 0.2 convert_bitcast_fusion
  691.7 1.3 copy.85
  693.0 17.1 %all-to-all-done = bf16[4,64,1664]{2,1,0:T(8,128)(2,1)S(1)} async-done(((bf16[4,64,1664]{2,1,0:T(8,128)(2,1)}), bf16[4,64,1664]{2,1,0:T(8,128)(2,1)S(1)}, u32[]{:S(2)}, u32[]{:S(2)}) %all-to-all-start) | async-done | bytes 852000 | tf_op jit(solution)/shard_map/all_to_all | solution.py:979
  710.2 0.1 copy.74
  710.3 0.5 slice_bitcast_fusion.2
  710.9 0.7 copy.81
  711.6 0.1 convert_bitcast_fusion.3
  711.7 0.8 copy.82
  712.6 0.7 copy.80
  713.3 0.8 copy.79
  714.1 0.8 copy.88
  714.9 0.8 copy.89
  (18 shorter events, 0.2 us)
Async XLA Ops:
  7.2 542.9 %reduce-scatter.11.cloned.1.call-start = ((), (), s32[]{:S(2)}) async-start(), calls=%async_computation.11 | async-start | bytes 7077888 | tf_op jit(solution)/shard_map/reduce_scatter | solution.py:977
  414.8 138.8 %reduce-scatter.9.cloned.1.call-start = ((), (), s32[]{:S(2)}) async-start(), calls=%async_computation.10 | async-start | bytes 7077888 | tf_op jit(solution)/shard_map/reduce_scatter | solution.py:977
  415.5 199.8 %reduce-scatter.7.cloned.1.call-start = ((), (), s32[]{:S(2)}) async-start(), calls=%async_computation.9 | async-start | bytes 7077888 | tf_op jit(solution)/shard_map/reduce_scatter | solution.py:977
  416.3 267.8 %reduce-scatter.5.cloned.1.call-start = ((), (), s32[]{:S(2)}) async-start(), calls=%async_computation.8 | async-start | bytes 7667712 | tf_op jit(solution)/shard_map/reduce_scatter | solution.py:977
  550.1 23.0 %all-to-all-start.3 = ((bf16[4,64,1536]{2,1,0:T(8,128)(2,1)}), bf16[4,64,1536]{2,1,0:T(8,128)(2,1)S(1)}, u32[]{:S(2)}, u32[]{:S(2)}) async-start(bf16[4,64,1536]{2,1,0:T(8,128)(2,1)} %bitcast.68), calls=%async_computation.7 | async-start | bytes 1572864 | tf_op jit(solution)/shard_map/all_to_all | solution.py:979
  573.1 42.2 %all-to-all-start.2 = ((bf16[4,64,1536]{2,1,0:T(8,128)(2,1)}), bf16[4,64,1536]{2,1,0:T(8,128)(2,1)S(1)}, u32[]{:S(2)}, u32[]{:S(2)}) async-start(bf16[4,64,1536]{2,1,0:T(8,128)(2,1)} %bitcast.67), calls=%async_computation.5 | async-start | bytes 1572864 | tf_op jit(solution)/shard_map/all_to_all | solution.py:979
  615.3 68.7 %all-to-all-start.1 = ((bf16[4,64,1536]{2,1,0:T(8,128)(2,1)}), bf16[4,64,1536]{2,1,0:T(8,128)(2,1)S(1)}, u32[]{:S(2)}, u32[]{:S(2)}) async-start(bf16[4,64,1536]{2,1,0:T(8,128)(2,1)} %bitcast.66), calls=%async_computation.3 | async-start | bytes 1572864 | tf_op jit(solution)/shard_map/all_to_all | solution.py:979
  684.0 26.1 %all-to-all-start = ((bf16[4,64,1664]{2,1,0:T(8,128)(2,1)}), bf16[4,64,1664]{2,1,0:T(8,128)(2,1)S(1)}, u32[]{:S(2)}, u32[]{:S(2)}) async-start(bf16[4,64,1664]{2,1,0:T(8,128)(2,1)} %bitcast.65), calls=%async_computation.1 | async-start | bytes 1703936 | tf_op jit(solution)/shard_map/all_to_all | solution.py:979
  711.6 2.5 copy-start
  711.7 3.2 copy-start.1
Sparse Core Ops, SparseCore 0:
  414.9 60.7 reduce-scatter.10
  479.5 70.7 reduce-scatter.8
  553.6 61.7 reduce-scatter.6
  619.0 64.9 reduce-scatter.4

commit v3 on v2

v3 whole, which is shorter than its diff:
```python
import functools

import jax
import jax.numpy as jnp
from jax import lax
from jax.experimental import pallas as pl
from jax.experimental.pallas import tpu as pltpu
from jax.sharding import Mesh, PartitionSpec as P

epsilon = 1e-06
rotary_base = 1000000.0
masked_score = -1e30
parts = 4
bf16 = jnp.bfloat16
f32 = jnp.float32


def unit_rows(values):
    scale_row = lax.rsqrt(jnp.mean(values * values, axis=-1, keepdims=True) + epsilon)
    return values * scale_row, scale_row


def norm_back(weighted, unit, scale_row):
    inner_mean = jnp.mean(weighted * unit, axis=-1, keepdims=True)
    return scale_row * (weighted - unit * inner_mean)


def rope_tables(positions, width):
    half_width = width // 2
    frequency = rotary_base ** (-(jnp.arange(half_width, dtype=f32) * 2.0 / width))
    angles = positions.astype(f32)[:, None] * frequency[None, :]
    angles = jnp.concatenate([angles, angles], axis=-1)
    return jnp.cos(angles)[:, None, :], jnp.sin(angles)[:, None, :]


def rotate(values, cosine, sine_table):
    half_width = values.shape[-1] // 2
    turned = jnp.concatenate([-values[..., half_width:], values[..., :half_width]], axis=-1)
    return values * cosine + turned * sine_table


def rotate_back(grads, cosine, sine_table):
    half_width = grads.shape[-1] // 2
    shifted = grads * sine_table
    turned = jnp.concatenate([shifted[..., half_width:], -shifted[..., :half_width]], axis=-1)
    return grads * cosine + turned


def multiply(left, right):
    return jnp.dot(left, right, preferred_element_type=f32)


def multiply_trans(left, right):
    return lax.dot_general(left, right, (((1,), (1,)), ((), ())), preferred_element_type=f32)


def outer_rows(left, right):
    return lax.dot_general(left, right, (((0,), (0,)), ((), ())), preferred_element_type=f32)


class Part:
    def __init__(self, ref, index=None):
        self.ref, self.index = ref, index

    def __getitem__(self, index):
        return Part(self.ref, index)

    def get(self):
        return self.ref if self.index is None else self.ref.at[self.index]


def at(ref):
    return Part(ref)


def found(ref):
    return ref.get() if isinstance(ref, Part) else ref


class Copy:
    def __init__(self, source, target, sems, device=None):
        self.source, self.target, self.sems, self.device = source, target, sems, device
        self.describe().start()

    def describe(self):
        source, target = found(self.source), found(self.target)
        sems = [array.at[index] for array, index in self.sems]
        if self.device is None:
            return pltpu.make_async_copy(source, target, sems[0])
        return pltpu.make_async_remote_copy(
            src_ref=source,
            dst_ref=target,
            send_sem=sems[0],
            recv_sem=sems[1],
            device_id=self.device,
            device_id_type=pl.DeviceIdType.MESH,
        )

    def wait(self):
        self.describe().wait()

    def wait_send(self):
        self.describe().wait_send()

    def wait_recv(self):
        self.describe().wait_recv()


class Links:
    def __init__(self, send_sems, recv_sems, local_sems):
        self.send_sems, self.recv_sems, self.local_sems = send_sems, recv_sems, local_sems
        self.count, self.local_count = 0, 0
        self.sent, self.kept = [], []

    def send(self, source, target, tracked=True, **device):
        index = self.count
        self.count += 1
        copy = Copy(source, target, [(self.send_sems, index), (self.recv_sems, index)], device)
        if tracked:
            self.sent.append(copy)
        return copy

    def local(self, source, target):
        index = self.local_count
        self.local_count += 1
        return Copy(source, target, [(self.local_sems, index)])

    def keep(self, source, target):
        self.kept.append(self.local(source, target))

    def finish(self):
        assert self.count <= self.send_sems.shape[0]
        assert self.local_count <= self.local_sems.shape[0]
        for copy in self.sent:
            copy.wait_send()
        for copy in self.kept:
            copy.wait()


class Place:
    def __init__(self, plane, cores, token_rows):
        self.plane, self.cores = plane, cores
        self.z, self.p, self.c = (lax.axis_index(axis) for axis in ("z", "p", "c"))
        self.column = self.p * cores + self.c
        self.other_core = lax.rem(self.c + 1, cores)
        self.z_others = [lax.rem(self.z + step, parts) for step in range(parts)]
        self.p_others = [lax.rem(self.p + step, plane) for step in range(plane)]
        self.columns_before = [
            lax.rem(self.p + plane - step, plane) * cores + self.c for step in range(plane)
        ]
        self.z_rows = [
            pl.ds(pl.multiple_of(other * token_rows, token_rows), token_rows)
            for other in self.z_others
        ]

    def along_z(self, step):
        return self.z_others[step]

    def in_plane(self, step):
        return self.p_others[step]

    def before(self, step):
        return self.columns_before[step]

    def siblings(self):
        return [self.other_core]


z_steps = (1, 3, 2)


class Fetch:
    def __init__(self, links, place, pieces, gathered):
        self.links, self.place, self.pieces, self.gathered = links, place, pieces, gathered

    def begin(self):
        links, place = self.links, self.place
        mine = self.gathered.at[place.z, place.column]
        self.first, self.own = [], []
        for shard, width, start, split in self.pieces:
            for step in z_steps:
                other = place.along_z(step)
                first = pl.multiple_of(other * width, 128) if split else 0
                self.first.append(
                    links.send(shard.at[:, pl.ds(first, width)], mine.at[:, pl.ds(start, width)], z=other)
                )
            first = pl.multiple_of(place.z * width, 128) if split else 0
            self.own.append(
                links.local(shard.at[:, pl.ds(first, width)], mine.at[:, pl.ds(start, width)])
            )

    def spread(self):
        links, place = self.links, self.place
        for copy in self.own:
            copy.wait()
        for copy in self.first:
            copy.wait_recv()
        block = self.gathered.at[:, place.column]
        self.second = [
            links.send(block, block, p=place.in_plane(step)) for step in range(1, place.plane)
        ]
        self.third = [links.send(block, block, c=other) for other in place.siblings()]

    def forward(self):
        links, place = self.links, self.place
        for step, copy in enumerate(self.second, 1):
            copy.wait_recv()
            block = self.gathered.at[:, place.before(step)]
            self.third += [links.send(block, block, c=other) for other in place.siblings()]

    def finish(self):
        for copy in self.third:
            copy.wait_recv()


def front_kernel(
    plane,
    cores,
    hidden,
    query_weight,
    key_weight,
    value_weight,
    out_weight,
    gate_weight,
    up_weight,
    down_weight,
    gain_block,
    grad_out,
    cosine,
    sine_turned,
    query_pos,
    key_pos,
    query_gain,
    key_gain,
    normed_out,
    projection_out,
    lin_out,
    queries_out,
    both_out,
    attended_out,
    out_columns_out,
    normed_mlp_out,
    residual_out,
    gate_out,
    up_out,
    down_out,
    grad_rows_out,
    stats_out,
    gains_out,
    hidden_all,
    normed,
    projection,
    lin,
    queries,
    both,
    attended_all,
    out_full,
    residual,
    normed_mlp,
    mixed,
    send_sems,
    recv_sems,
    local_sems,
):
    links = Links(send_sems, recv_sems, local_sems)
    token_rows, width = hidden.shape
    place = Place(plane, cores, token_rows)
    tokens = parts * token_rows
    head = query_gain.shape[1]
    query_width = query_weight.shape[1] // parts
    key_width = key_weight.shape[1] // parts
    query_heads, key_heads = query_width // head, key_width // head
    group = query_heads // key_heads
    hidden_units = gate_weight.shape[1] // parts
    lin_width = query_width + 2 * key_width

    heads_fetch = Fetch(
        links,
        place,
        [
            (query_weight, query_width, 0, True),
            (key_weight, key_width, query_width, True),
            (value_weight, key_width, query_width + key_width, True),
            (gain_block, 128, lin_width, False),
        ],
        projection,
    )
    out_fetch = Fetch(links, place, [(out_weight, out_weight.shape[1], 0, False)], out_full)
    mlp_fetches = [
        Fetch(links, place, [(weight, hidden_units, 0, True)], target)
        for weight, target in ((gate_weight, gate_out), (up_weight, up_out), (down_weight, down_out))
    ]
    heads_fetch.begin()
    hidden_copies = [
        links.send(hidden, hidden_all.at[place.z], z=place.along_z(step)) for step in z_steps
    ]
    hidden_own = links.local(hidden, hidden_all.at[place.z])
    heads_fetch.spread()
    out_fetch.begin()
    for fetch in mlp_fetches:
        fetch.begin()
    hidden_own.wait()
    for copy in hidden_copies:
        copy.wait_recv()
    heads_fetch.forward()
    heads_fetch.finish()
    links.keep(projection, projection_out)

    gain_columns = projection[:, :, :, lin_width : lin_width + 128].reshape(width, 128)
    gain_rows = gain_columns.astype(f32).T
    gains_out[...] = gain_rows[:8]

    def norm_one(index, carry):
        values = hidden_all[index].astype(f32)
        scale = lax.rsqrt(jnp.mean(values * values, axis=-1, keepdims=True) + epsilon)
        rows = pl.ds(pl.multiple_of(index * token_rows, token_rows), token_rows)
        normed[rows] = (values * scale * gains_out[0:1]).astype(bf16)
        return carry

    lax.fori_loop(0, parts, norm_one, 0)
    links.keep(normed, normed_out)

    tile = 2 * head

    def project(index, carry):
        columns = pl.ds(pl.multiple_of(index * tile, tile), tile)
        weights = projection[:, :, :, columns].reshape(width, tile)
        lin[:, columns] = jnp.dot(normed[...], weights, preferred_element_type=f32)
        return carry

    lax.fori_loop(0, lin_width // tile, project, 0)
    own_both = both.at[place.p]

    def rope(values, gain):
        scale = lax.rsqrt(jnp.mean(values * values, axis=-1, keepdims=True) + epsilon)
        gained = values * scale * gain
        turned = pltpu.roll(gained, head // 2, 1)
        return (gained * cosine[...] + turned * sine_turned[...]).astype(bf16)

    for index in range(key_heads):
        columns = slice(query_width + index * head, query_width + (index + 1) * head)
        own_both[:, index * head : (index + 1) * head] = rope(lin[:, columns], key_gain[...])
    own_both[:, key_width:] = lin[:, query_width + key_width :].astype(bf16)
    both_copies = [
        links.send(own_both, own_both, p=place.in_plane(step)) for step in range(1, plane)
    ]
    for index in range(query_heads):
        columns = slice(index * head, (index + 1) * head)
        queries[index] = rope(lin[:, columns], query_gain[...])
    links.keep(lin.at[:, pl.ds(0, query_width + key_width)], lin_out)
    links.keep(queries, queries_out)
    out_fetch.spread()
    mlp_fetches[0].spread()
    for copy in both_copies:
        copy.wait_recv()
    links.keep(both, both_out)

    factor = head ** (-0.5) * 1.4426950408889634
    chunk = min(256, tokens)
    chunks_each = tokens // chunk
    lanes = group * tokens
    own_attended = attended_all.at[place.z]
    attended_copies = []
    for key_head in range(key_heads):
        block = queries[key_head * group : (key_head + 1) * group].reshape(lanes, head)
        positions = jnp.concatenate([query_pos[...]] * group, axis=1)
        mixed[...] = jnp.zeros_like(mixed)

        def attend_chunk(index, carry):
            best, summed = carry
            source, row = index // chunks_each, index % chunks_each
            rows = pl.ds(pl.multiple_of(row * chunk, chunk), chunk)
            keys = both[source, rows, pl.ds(key_head * head, head)]
            values = both[source, rows, pl.ds(key_width + key_head * head, head)]
            scores = multiply_trans(keys, block) * factor
            spot = pl.ds(pl.multiple_of(index * chunk, chunk), chunk)
            scores = jnp.where(key_pos[spot] <= positions, scores, masked_score)
            new_best = jnp.maximum(best, jnp.max(scores, axis=0, keepdims=True))
            weights = jnp.exp2(scores - new_best)
            shrink = jnp.exp2(best - new_best)
            summed = summed * shrink + jnp.sum(weights, axis=0, keepdims=True)
            mixed[...] = mixed[...] * shrink + outer_rows(values, weights.astype(bf16))
            return new_best, summed

        best, summed = lax.fori_loop(
            0,
            plane * chunks_each,
            attend_chunk,
            (jnp.full((1, lanes), masked_score, f32), jnp.zeros((1, lanes), f32)),
        )
        mixed_rows = (mixed[...] / summed).T
        stats = best + jnp.log2(summed)
        for member in range(group):
            index = key_head * group + member
            stats_out[index : index + 1] = stats[:, member * tokens : (member + 1) * tokens]
            own_attended[:, index * head : (index + 1) * head] = mixed_rows[
                member * tokens : (member + 1) * tokens
            ].astype(bf16)
        part = own_attended.at[:, pl.ds(key_head * group * head, group * head)]
        attended_copies += [links.send(part, part, z=place.along_z(step)) for step in z_steps]
        if key_head == 0:
            out_fetch.forward()
            mlp_fetches[1].spread()
    grad_copies = [
        links.send(grad_out, grad_rows_out.at[place.z], z=place.along_z(step)) for step in z_steps
    ]
    links.keep(grad_out, grad_rows_out.at[place.z])
    links.keep(own_attended, attended_out)
    mlp_fetches[2].spread()
    out_fetch.finish()
    links.keep(out_full, out_columns_out)
    for copy in attended_copies:
        copy.wait_recv()

    def add_out(index, carry):
        weights = out_full[index].reshape(width // parts, parts * query_width)
        columns = pl.ds(pl.multiple_of(index * (width // parts), 128), width // parts)
        total = hidden_all[:, :, columns].reshape(tokens, width // parts).astype(f32)
        for other in range(parts):
            total += multiply_trans(
                attended_all[other], weights[:, other * query_width : (other + 1) * query_width]
            )
        residual[:, columns] = total
        return carry

    lax.fori_loop(0, parts, add_out, 0)
    mlp_fetches[0].forward()

    def norm_two(index, carry):
        rows = pl.ds(pl.multiple_of(index * token_rows, token_rows), token_rows)
        values = residual[rows]
        scale = lax.rsqrt(jnp.mean(values * values, axis=-1, keepdims=True) + epsilon)
        normed_mlp[rows] = (values * scale * gains_out[1:2]).astype(bf16)
        return carry

    lax.fori_loop(0, parts, norm_two, 0)
    links.keep(normed_mlp, normed_mlp_out)
    own_rows = place.z_rows[0]
    links.keep(residual.at[own_rows], residual_out)
    mlp_fetches[1].forward()
    mlp_fetches[2].forward()
    for copy in grad_copies:
        copy.wait_recv()
    for fetch in mlp_fetches:
        fetch.finish()
    links.finish()


def front(plane, cores, hidden, weights, gain_block, grad_out, tables, positions, head_gains):
    token_rows, width = hidden.shape
    tokens = parts * token_rows
    shard = weights[0].shape[0]
    head = head_gains[0].shape[1]
    query_width, key_width = weights[0].shape[1] // parts, weights[1].shape[1] // parts
    hidden_units = weights[4].shape[1] // parts
    lin_width = query_width + 2 * key_width
    query_heads = query_width // head
    group = query_width // key_width
    stacked = (parts, plane * cores, shard)
    copies = 3 * 7 + 3 * 3 + 3 * 2 + 5 * (2 * plane - 1) + plane + 8
    any_space, vmem = pl.BlockSpec(memory_space=pl.ANY), pl.BlockSpec(memory_space=pltpu.VMEM)
    outputs = [
        ((tokens, width), bf16),
        (stacked + (lin_width + 128,), bf16),
        ((tokens, query_width + key_width), f32),
        ((query_heads, tokens, head), bf16),
        ((plane, tokens, 2 * key_width), bf16),
        ((tokens, query_width), bf16),
        (stacked + (parts * query_width,), bf16),
        ((tokens, width), bf16),
        ((token_rows, width), f32),
        (stacked + (hidden_units,), bf16),
        (stacked + (hidden_units,), bf16),
        (stacked + (hidden_units,), bf16),
        ((parts, token_rows, width), bf16),
        ((8, tokens), f32),
        ((8, width), f32),
    ]
    return pl.pallas_call(
        functools.partial(front_kernel, plane, cores),
        out_shape=[jax.ShapeDtypeStruct(shape, kind) for shape, kind in outputs],
        in_specs=[any_space] * 10 + [vmem] * 6,
        out_specs=[any_space] * 13 + [vmem] * 2,
        scratch_shapes=[
            pltpu.VMEM((parts, token_rows, width), bf16),
            pltpu.VMEM((tokens, width), bf16),
            pltpu.VMEM(stacked + (lin_width + 128,), bf16),
            pltpu.VMEM((tokens, lin_width), f32),
            pltpu.VMEM((query_heads, tokens, head), bf16),
            pltpu.VMEM((plane, tokens, 2 * key_width), bf16),
            pltpu.VMEM((parts, tokens, query_width), bf16),
            pltpu.VMEM(stacked + (parts * query_width,), bf16),
            pltpu.VMEM((tokens, width), f32),
            pltpu.VMEM((tokens, width), bf16),
            pltpu.VMEM((head, group * tokens), f32),
            pltpu.SemaphoreType.DMA((copies,)),
            pltpu.SemaphoreType.DMA((copies,)),
            pltpu.SemaphoreType.DMA((32,)),
        ],
        compiler_params=pltpu.CompilerParams(
            has_side_effects=True, vmem_limit_bytes=60 * 1024 * 1024
        ),
        cost_estimate=pl.CostEstimate(flops=12 * 10**9, bytes_accessed=10**8, transcendentals=10**7),
    )(hidden, *weights, gain_block, grad_out, *tables, *positions, *head_gains)


def half_turn(values):
    return pltpu.roll(values, values.shape[1] // 2, 1)


def scatter_sends(links, place, piece, landed, token_rows, columns, tracked=True):
    copies = []
    for step in z_steps:
        other = place.along_z(step)
        rows = place.z_rows[step]
        copies.append(
            links.send(
                at(piece)[rows, columns], at(landed)[place.z, :, columns], tracked, z=other
            )
        )
    return copies


def total_of(landed):
    total = landed[0].astype(f32)
    for index in range(1, parts):
        total += landed[index].astype(f32)
    return total


class Returns:
    def __init__(self, links, place, ring, addend, ring_sems, buffers):
        self.links, self.place, self.ring, self.addend = links, place, ring, addend
        self.ring_sems = ring_sems
        self.from_sibling, self.halves, self.from_plane, self.sums, self.final = buffers
        self.pending = [[] for _ in range(ring.shape[0])]
        self.turn, self.used = 0, 0
        self.sibling_copies, self.plane_copies, self.z_copies = {}, {}, {}
        self.mine, self.own_final = {}, {}

    def slot(self):
        slot = self.turn % len(self.pending)
        self.turn += 1
        for wait in self.pending[slot]:
            wait()
        self.pending[slot] = []
        return slot

    def local(self, source, target):
        self.used += 1
        return Copy(source, target, [(self.ring_sems, self.used - 1)])

    def product(self, slot, left, half, right, start, index, added):
        size = right.shape[1]
        tile = 512 if size % 512 == 0 else 256

        def tile_of(step, carry):
            columns = pl.ds(pl.multiple_of(step * tile, tile), tile)
            target = pl.ds(pl.multiple_of(start + step * tile, 128), tile)
            rows = left[index, :, half]
            value = multiply(rows.reshape(-1, rows.shape[2]), right[:, columns])
            value = value.reshape(rows.shape[0], rows.shape[1], tile)
            if added is not None:
                value += self.addend[added, :, :, target].astype(f32)
            self.ring[slot, :, :, target] = value.astype(bf16)
            return carry

        lax.fori_loop(0, size // tile, tile_of, 0)

    def give(self, family, left, right, start=0):
        place, size = self.place, right.shape[1]
        other = place.other_core
        columns = pl.ds(start, size)
        for index in range(parts):
            slot = self.slot()
            self.product(slot, left, other, right, start, index, None)
            copy = self.links.send(
                at(self.ring)[slot, :, :, columns],
                at(self.from_sibling)[family, index, :, :, columns],
                tracked=False,
                c=other,
            )
            self.pending[slot].append(copy.wait_send)
            self.sibling_copies[family, start, index] = copy

    def take(self, family, left, right, start=0):
        size = right.shape[1]
        columns = pl.ds(start, size)
        kept = []
        for index in range(parts):
            slot = self.slot()
            self.sibling_copies[family, start, index].wait_recv()
            side = 0
            load = self.local(
                at(self.from_sibling)[family, index, :, :, columns],
                at(self.addend)[side, :, :, columns],
            )
            load.wait()
            self.product(slot, left, self.place.c, right, start, index, side)
            copy = self.local(
                at(self.ring)[slot, :, :, columns], at(self.halves)[family, index, :, :, columns]
            )
            kept.append(copy)
            self.pending[slot].append(lambda: None)
            if index >= 1:
                kept[index - 1].wait()
        kept[-1].wait()
        self.send_plane(family, columns)

    def send_plane(self, family, columns):
        links, place = self.links, self.place
        copies = []
        for step in range(1, place.plane):
            other = place.in_plane(step)
            copies.append(
                links.send(
                    at(self.halves)[family, :, other, :, columns],
                    at(self.from_plane)[family, place.p, :, :, columns],
                    p=other,
                )
            )
        self.plane_copies.setdefault(family, []).extend(copies)
        self.mine.setdefault(family, []).append(
            self.local(
                at(self.halves)[family, :, place.p, :, columns],
                at(self.from_plane)[family, place.p, :, :, columns],
            )
        )

    def along_z(self, family):
        links, place = self.links, self.place
        for copy in self.plane_copies[family]:
            copy.wait_recv()
        for copy in self.mine[family]:
            copy.wait()
        loads = []
        for index in range(parts):
            slot = self.slot()
            loads.append(
                (slot, self.local(at(self.from_plane)[family, :, index], at(self.ring)[slot]))
            )
        for index, (slot, load) in enumerate(loads):
            load.wait()
            total = self.ring[slot, 0].astype(f32)
            for source in range(1, place.plane):
                total += self.ring[slot, source].astype(f32)
            self.sums[family, index] = total.astype(bf16)
        copies = []
        for step in z_steps:
            other = place.along_z(step)
            copies.append(
                links.send(at(self.sums)[family, other], at(self.final)[family, place.z], z=other)
            )
        self.own_final[family] = self.local(
            at(self.sums)[family, place.z], at(self.final)[family, place.z]
        )
        self.z_copies[family] = copies

    def home(self, family, stage, stage_sems, targets):
        for copy in self.z_copies[family]:
            copy.wait_recv()
        self.own_final[family].wait()
        loads = []
        for index in range(parts):
            loaded = self.slot()
            loads.append(
                (loaded, self.local(at(self.final)[family, index], at(self.ring)[loaded, 0]))
            )
        for index in range(parts):
            slot = self.out_turn % stage.shape[0]
            for copy in self.out_pending[slot]:
                copy.wait()
            loaded, load = loads[index]
            load.wait()
            stage[slot] = self.ring[loaded, 0].astype(f32)
            self.out_pending[slot] = []
            for target, start, width in targets:
                copy = Copy(
                    at(stage)[slot, :, pl.ds(start, width)],
                    at(target)[:, pl.ds(index * width, width)],
                    [(stage_sems, self.out_used)],
                )
                self.out_used += 1
                self.out_pending[slot].append(copy)
            self.out_turn += 1

    out_turn = 0
    out_used = 0

    def finish(self):
        assert self.used <= self.ring_sems.shape[0]
        for waits in self.pending:
            for wait in waits:
                wait()
        for copies in self.out_pending:
            for copy in copies:
                copy.wait()


def rear_kernel(
    plane,
    cores,
    normed_mlp_in,
    gate_in,
    up_in,
    down_in,
    grad_in,
    residual_in,
    projection_in,
    out_in,
    normed_in,
    lin_in,
    queries_in,
    both_in,
    attended_in,
    hidden,
    stats,
    gains,
    cosine,
    sine_turned,
    query_pos,
    key_blocks,
    query_gain,
    key_gain,
    output,
    input_grad,
    query_grad,
    key_grad,
    value_grad,
    out_grad,
    gate_grad,
    up_grad,
    down_grad,
    small_sums,
    from_sibling,
    halves,
    from_plane,
    final,
    both_landed,
    normed,
    turned_left,
    turned_right,
    gate,
    up,
    down,
    part_in,
    landed_in,
    landed_out,
    residual,
    grad_residual,
    low_rows,
    sums,
    ring,
    addend,
    stage,
    gain_rows,
    messages,
    z_messages,
    plane_messages,
    core_messages,
    ring_sems,
    stage_sems,
    both_sems,
    send_sems,
    recv_sems,
    local_sems,
):
    links = Links(send_sems, recv_sems, local_sems)
    tokens, width = normed.shape
    token_rows = tokens // parts
    place = Place(plane, cores, token_rows)
    returns = Returns(
        links, place, ring, addend, ring_sems, (from_sibling, halves, from_plane, sums, final)
    )
    returns.out_pending = [[] for _ in range(stage.shape[0])]
    units = gate.shape[3]
    block = width // parts
    shard = gate.shape[2]
    head = query_gain.shape[1]
    query_heads = queries_in.shape[0]
    query_width = query_heads * head
    key_width = both_in.shape[2] // 2
    key_heads = key_width // head
    group = query_heads // key_heads
    lin_width = query_width + 2 * key_width
    own_rows = place.z_rows[0]
    part_out = normed
    split = (plane, cores, shard, tokens)

    low_copies, out_copies, landed_copies = [], [], []

    def feed_forward(grad_rows, act, d_gate, d_up):
        loads = [
            links.local(normed_mlp_in, normed),
            links.local(gate_in, gate),
            links.local(up_in, up),
            links.local(grad_in, grad_rows),
            links.local(down_in, down),
            links.local(residual_in, residual),
        ]
        for copy in loads:
            copy.wait()
        tile = 256

        def hidden_tile(index, carry):
            columns = pl.ds(pl.multiple_of(index * tile, tile), tile)
            gate_lin = multiply(normed[...], gate[:, :, :, columns].reshape(width, tile))
            up_lin = multiply(normed[...], up[:, :, :, columns].reshape(width, tile))
            grad_act = multiply(
                grad_rows[...].reshape(tokens, width), down[:, :, :, columns].reshape(width, tile)
            )
            sigmoid = jax.nn.sigmoid(gate_lin)
            silu = gate_lin * sigmoid
            act[:, columns] = (silu * up_lin).astype(bf16)
            d_up[:, columns] = (grad_act * silu).astype(bf16)
            d_gate[:, columns] = (
                grad_act * up_lin * (sigmoid + silu * (1.0 - sigmoid))
            ).astype(bf16)
            return carry

        lax.fori_loop(0, units // tile, hidden_tile, 0)
        in_copies = []
        for index in range(parts):
            columns = pl.ds(index * block, block)
            part_in[:, columns] = (
                multiply_trans(d_gate[...], gate[index].reshape(block, units))
                + multiply_trans(d_up[...], up[index].reshape(block, units))
            ).astype(bf16)
            in_copies += scatter_sends(
                links, place, part_in, landed_in, token_rows, columns, False
            )
        landed_in[place.z] = part_in[own_rows]
        for index in range(parts):
            columns = slice(index * block, (index + 1) * block)
            turned_left[index] = normed[:, columns].T.reshape(split)
            turned_right[index] = grad_rows[:, :, columns].reshape(tokens, block).T.reshape(split)
        returns.give(0, turned_left, d_gate)
        returns.give(1, turned_left, d_up)
        returns.take(0, turned_left, d_gate)
        returns.take(1, turned_left, d_up)
        for index in range(parts):
            columns = pl.ds(index * block, block)
            part_out[:, columns] = multiply_trans(
                act[...], down[index].reshape(block, units)
            ).astype(bf16)
        landed_out[place.z] = part_out[own_rows]

        for copy in in_copies:
            copy.wait_recv()
        grad_normed = total_of(landed_in)
        values = residual[...]
        scale = lax.rsqrt(jnp.mean(values * values, axis=-1, keepdims=True) + epsilon)
        unit = values * scale
        gain_rows[1:2] = jnp.sum(grad_normed * unit, axis=0, keepdims=True)
        own_grad = grad_rows[place.z].astype(f32)
        total = own_grad + norm_back(grad_normed * gains[1:2], unit, scale)
        grad_residual[...] = total
        low_rows[place.z] = total.astype(bf16)
        own_low = at(low_rows)[place.z]
        low_copies.extend(
            links.send(own_low, own_low, z=place.along_z(step)) for step in z_steps
        )
        out_copies.extend(
            scatter_sends(links, place, part_out, landed_out, token_rows, pl.ds(0, width))
        )
        returns.give(2, turned_right, act)
        returns.take(2, turned_right, act)
        for copy in in_copies:
            copy.wait_send()

    pl.run_scoped(
        feed_forward,
        pltpu.VMEM((parts, token_rows, width), bf16),
        pltpu.VMEM((tokens, units), bf16),
        pltpu.VMEM((tokens, units), bf16),
        pltpu.VMEM((tokens, units), bf16),
    )

    def attention(lin, queries, both, attended, grad_heads, delta, both_stage, both_total, query_total, grad_lin):
        out_at = pl.ds(pl.multiple_of(place.z * query_width, 128), query_width)
        out_columns = at(up)[:, :, :, pl.ds(0, query_width)]
        projection = at(gate)[:, :, :, pl.ds(0, lin_width)]
        loads = [
            links.local(at(out_in)[:, :, :, out_at], out_columns),
            links.local(attended_in, attended),
            links.local(queries_in, queries),
            links.local(both_in, both),
            links.local(lin_in, lin),
            links.local(at(projection_in)[:, :, :, pl.ds(0, lin_width)], projection),
            links.local(normed_in, part_in),
        ]
        for copy in loads:
            copy.wait()
        for index in range(parts):
            columns = slice(index * block, (index + 1) * block)
            turned_left[index] = part_in[:, columns].T.reshape(split)
        for copy in low_copies:
            copy.wait_recv()

        tile = group * head
        for index in range(key_heads):
            columns = slice(index * tile, (index + 1) * tile)
            grads = multiply(
                low_rows[...].reshape(tokens, width), up[:, :, :, columns].reshape(width, tile)
            ).astype(bf16)
            for member in range(group):
                number = index * group + member
                own = grads[:, member * head : (member + 1) * head]
                grad_heads[number] = own
                mixed = attended[:, number * head : (number + 1) * head].astype(f32)
                delta[number : number + 1] = jnp.sum(
                    (own.astype(f32) * mixed).T, axis=0, keepdims=True
                )

        factor = head ** (-0.5)
        score_factor = factor * 1.4426950408889634
        chunk = min(256, tokens)
        chunks_each = tokens // chunk
        lanes = group * tokens
        piece_rows = token_rows // 2
        both_copies, both_own = [], []
        for key_head in range(key_heads):
            members = slice(key_head * group, (key_head + 1) * group)
            query_block = queries[members].reshape(lanes, head)
            grad_block = grad_heads[members].reshape(lanes, head)
            numbers = range(key_head * group, (key_head + 1) * group)
            stats_row = jnp.concatenate([stats[number : number + 1] for number in numbers], axis=1)
            delta_row = jnp.concatenate([delta[number : number + 1] for number in numbers], axis=1)
            positions = jnp.concatenate([query_pos[...]] * group, axis=1)
            query_total[...] = jnp.zeros_like(query_total)

            def back_chunk(index, carry):
                source, row = index // chunks_each, index % chunks_each
                rows = pl.ds(pl.multiple_of(row * chunk, chunk), chunk)
                keys = both[source, rows, pl.ds(key_head * head, head)]
                values = both[source, rows, pl.ds(key_width + key_head * head, head)]
                scores = multiply_trans(keys, query_block) * score_factor
                spots = lax.broadcasted_iota(jnp.int32, (chunk, 1), 0)
                starts = jnp.zeros((chunk, 1), jnp.int32)
                for piece in range(chunk // piece_rows):
                    start = key_blocks[index * (chunk // piece_rows) + piece] * piece_rows
                    starts = jnp.where(spots >= piece * piece_rows, start - piece * piece_rows, starts)
                weights = jnp.where(
                    spots + starts <= positions, jnp.exp2(scores - stats_row), 0.0
                )
                grad_weights = multiply_trans(values, grad_block)
                grad_scores = (weights * (grad_weights - delta_row)).astype(bf16)
                query_total[...] += outer_rows(keys, grad_scores)
                both[source, rows, pl.ds(key_head * head, head)] = (
                    multiply(grad_scores, query_block) * factor
                ).astype(bf16)
                both[source, rows, pl.ds(key_width + key_head * head, head)] = multiply(
                    weights.astype(bf16), grad_block
                ).astype(bf16)
                return carry

            lax.fori_loop(0, plane * chunks_each, back_chunk, 0)
            for start in (key_head * head, key_width + key_head * head):
                columns = pl.ds(start, head)
                for step in range(1, plane):
                    other = place.in_plane(step)
                    both_copies.append(
                        links.send(
                            at(both)[other, :, columns],
                            at(both_landed)[place.p, :, columns],
                            tracked=False,
                            p=other,
                        )
                    )
                both_own.append(
                    links.local(
                        at(both)[place.p, :, columns], at(both_landed)[place.p, :, columns]
                    )
                )
            grad_queries = query_total[...].T * factor
            for member in range(group):
                number = key_head * group + member
                rows = slice(member * tokens, (member + 1) * tokens)
                own = grad_queries[rows]
                lin_rows = lin[:, number * head : (number + 1) * head]
                scale = lax.rsqrt(jnp.mean(lin_rows * lin_rows, axis=-1, keepdims=True) + epsilon)
                unit = lin_rows * scale
                turned = own * cosine[...] - half_turn(own) * sine_turned[...]
                gained = jnp.sum(turned * unit, axis=0, keepdims=True)
                if number == 0:
                    messages[0, 0:1, block : block + head] = gained
                else:
                    messages[0, 0:1, block : block + head] += gained
                grad_lin[:, number * head : (number + 1) * head] = norm_back(
                    turned * query_gain[...], unit, scale
                ).astype(bf16)

        for index in range(parts):
            columns = slice(index * block, (index + 1) * block)
            turned_right[index] = low_rows[:, :, columns].reshape(tokens, block).T.reshape(split)
        returns.give(3, turned_right, attended, lin_width)
        returns.take(3, turned_right, attended, lin_width)
        returns.along_z(0)

        for copy in both_copies:
            copy.wait_recv()
        for copy in both_own:
            copy.wait()

        def load_both(source):
            return Copy(
                at(both_landed)[source], at(both_stage)[source % 2], [(both_sems, source)]
            )

        load = load_both(0)
        for source in range(plane):
            load.wait()
            if source + 1 < plane:
                load = load_both(source + 1)
            landed = both_stage[source % 2].astype(f32)
            if source == 0:
                both_total[...] = landed
            else:
                both_total[...] += landed
        for key_head in range(key_heads):
            start = query_width + key_width + key_head * head
            grad_lin[:, start : start + head] = both_total[
                :, key_width + key_head * head : key_width + (key_head + 1) * head
            ].astype(bf16)
            own = both_total[:, key_head * head : (key_head + 1) * head]
            start = query_width + key_head * head
            lin_rows = lin[:, start : start + head]
            scale = lax.rsqrt(jnp.mean(lin_rows * lin_rows, axis=-1, keepdims=True) + epsilon)
            unit = lin_rows * scale
            turned = own * cosine[...] - half_turn(own) * sine_turned[...]
            gained = jnp.sum(turned * unit, axis=0, keepdims=True)
            if key_head == 0:
                messages[0, 1:2, block : block + head] = gained
            else:
                messages[0, 1:2, block : block + head] += gained
            grad_lin[:, start : start + head] = norm_back(turned * key_gain[...], unit, scale).astype(
                bf16
            )

        for index in range(parts):
            columns = pl.ds(index * block, block)
            part_in[:, columns] = multiply_trans(
                grad_lin[...], gate[index, :, :, 0:lin_width].reshape(block, lin_width)
            ).astype(bf16)
            landed_copies.extend(
                scatter_sends(links, place, part_in, landed_in, token_rows, columns)
            )
        landed_in[place.z] = part_in[own_rows]
        returns.give(3, turned_left, grad_lin)
        returns.take(3, turned_left, grad_lin)
        returns.along_z(1)
        returns.along_z(2)
        for copy in both_copies:
            copy.wait_send()

    pl.run_scoped(
        attention,
        pltpu.VMEM((tokens, query_width + key_width), f32),
        pltpu.VMEM((query_heads, tokens, head), bf16),
        pltpu.VMEM((plane, tokens, 2 * key_width), bf16),
        pltpu.VMEM((tokens, query_width), bf16),
        pltpu.VMEM((query_heads, tokens, head), bf16),
        pltpu.VMEM((8, tokens), f32),
        pltpu.VMEM((2, tokens, 2 * key_width), bf16),
        pltpu.VMEM((tokens, 2 * key_width), f32),
        pltpu.VMEM((head, group * tokens), f32),
        pltpu.VMEM((tokens, lin_width), bf16),
    )
    returns.along_z(3)

    for copy in landed_copies:
        copy.wait_recv()
    grad_normed = total_of(landed_in)
    values = hidden[...].astype(f32)
    scale = lax.rsqrt(jnp.mean(values * values, axis=-1, keepdims=True) + epsilon)
    unit = values * scale
    gain_rows[0:1] = jnp.sum(grad_normed * unit, axis=0, keepdims=True)
    input_grad[...] = (
        grad_residual[...] + norm_back(grad_normed * gains[0:1], unit, scale)
    ).astype(bf16)

    for index in range(1, parts):
        messages[index, :, block : block + head] = messages[0, :, block : block + head]
    for index in range(parts):
        messages[index, 0:2, 0:block] = gain_rows[:, index * block : (index + 1) * block]
    copies = [
        links.send(at(messages)[place.along_z(step)], at(z_messages)[place.z], z=place.along_z(step))
        for step in z_steps
    ]
    z_messages[place.z] = messages[place.z]
    for copy in out_copies:
        copy.wait_recv()
    output[...] = (residual[...] + total_of(landed_out)).astype(bf16)
    for copy in copies:
        copy.wait_recv()
    plane_messages[place.p] = (z_messages[0] + z_messages[1]) + (z_messages[2] + z_messages[3])
    copies = [
        links.send(
            at(plane_messages)[place.p], at(plane_messages)[place.p], p=place.in_plane(step)
        )
        for step in range(1, plane)
    ]
    returns.home(0, stage, stage_sems, [(gate_grad, 0, units)])
    for copy in copies:
        copy.wait_recv()
    total = plane_messages[0]
    for source in range(1, plane):
        total += plane_messages[source]
    core_messages[place.c] = total
    copies = [
        links.send(at(core_messages)[place.c], at(core_messages)[place.c], c=other)
        for other in place.siblings()
    ]
    returns.home(1, stage, stage_sems, [(up_grad, 0, units)])
    for copy in copies:
        copy.wait_recv()
    total = core_messages[0]
    for source in range(1, cores):
        total += core_messages[source]
    small_sums[...] = total
    returns.home(2, stage, stage_sems, [(down_grad, 0, units)])
    returns.home(
        3,
        stage,
        stage_sems,
        [
            (query_grad, 0, query_width),
            (key_grad, query_width, key_width),
            (value_grad, query_width + key_width, key_width),
            (out_grad, lin_width, query_width),
        ],
    )
    returns.finish()
    links.finish()


def rear(plane, cores, large, small):
    normed_mlp, gate = large[0], large[1]
    projection, lin, queries, both = large[6], large[9], large[10], large[11]
    tokens, width = normed_mlp.shape
    token_rows = tokens // parts
    _, columns, shard, units = gate.shape
    query_heads, _, head = queries.shape
    query_width = query_heads * head
    key_width = both.shape[2] // 2
    key_heads = key_width // head
    lin_width = query_width + 2 * key_width
    block = width // parts
    any_space, vmem = pl.BlockSpec(memory_space=pl.ANY), pl.BlockSpec(memory_space=pltpu.VMEM)
    copies = 16 + 12 + 6 + 12 + 20 + 10 * plane + 12 + 8
    wide = lin_width + query_width
    assert wide == units
    shapes = [
        ((token_rows, width), bf16),
        ((token_rows, width), bf16),
        ((shard, parts * query_width), f32),
        ((shard, parts * key_width), f32),
        ((shard, parts * key_width), f32),
        ((shard, parts * query_width), f32),
        ((shard, parts * units), f32),
        ((shard, parts * units), f32),
        ((shard, parts * units), f32),
        ((8, block + head), f32),
        ((4, parts, plane, shard, units), bf16),
        ((4, parts, plane, shard, units), bf16),
        ((4, plane, parts, shard, units), bf16),
        ((4, parts, shard, units), bf16),
        ((plane, tokens, 2 * key_width), bf16),
    ]
    turned = (parts, plane, cores, shard, tokens)
    message = (8, block + head)
    return pl.pallas_call(
        functools.partial(rear_kernel, plane, cores),
        out_shape=[jax.ShapeDtypeStruct(shape, kind) for shape, kind in shapes],
        in_specs=[any_space] * 13
        + [vmem] * 6
        + [pl.BlockSpec(memory_space=pltpu.SMEM)]
        + [vmem] * 2,
        out_specs=[vmem] * 2 + [any_space] * 7 + [vmem] + [any_space] * 5,
        scratch_shapes=[
            pltpu.VMEM((tokens, width), bf16),
            pltpu.VMEM(turned, bf16),
            pltpu.VMEM(turned, bf16),
            pltpu.VMEM(gate.shape, bf16),
            pltpu.VMEM(gate.shape, bf16),
            pltpu.VMEM(gate.shape, bf16),
            pltpu.VMEM((tokens, width), bf16),
            pltpu.VMEM((parts, token_rows, width), bf16),
            pltpu.VMEM((parts, token_rows, width), bf16),
            pltpu.VMEM((token_rows, width), f32),
            pltpu.VMEM((token_rows, width), f32),
            pltpu.VMEM((parts, token_rows, width), bf16),
            pltpu.VMEM((4, parts, shard, units), bf16),
            pltpu.VMEM((4, plane, shard, units), bf16),
            pltpu.VMEM((1, plane, shard, units), bf16),
            pltpu.VMEM((2, shard, units), f32),
            pltpu.VMEM((2, width), f32),
            pltpu.VMEM((parts,) + message, f32),
            pltpu.VMEM((parts,) + message, f32),
            pltpu.VMEM((plane,) + message, f32),
            pltpu.VMEM((cores,) + message, f32),
            pltpu.SemaphoreType.DMA((128,)),
            pltpu.SemaphoreType.DMA((32,)),
            pltpu.SemaphoreType.DMA((plane,)),
            pltpu.SemaphoreType.DMA((copies,)),
            pltpu.SemaphoreType.DMA((copies,)),
            pltpu.SemaphoreType.DMA((24,)),
        ],
        compiler_params=pltpu.CompilerParams(
            has_side_effects=True, vmem_limit_bytes=63 * 1024 * 1024
        ),
        cost_estimate=pl.CostEstimate(flops=4 * 10**10, bytes_accessed=10**8, transcendentals=10**7),
    )(*large, *small)


def make_local(plane, cores):
    def local(
        hidden_in,
        block_map,
        query_weight,
        key_weight,
        value_weight,
        out_weight,
        gate_weight,
        up_weight,
        down_weight,
        attention_norm_gain,
        feedforward_gain,
        query_gain,
        key_gain,
        output_grad,
    ):
        shard = query_weight.shape[0]
        hidden_own, grad_own = hidden_in[0], output_grad[0]
        row_count, features = hidden_own.shape
        piece_rows = row_count // 2
        head_width = query_gain.shape[0]
        p_index = lax.axis_index("p")
        tokens = parts * row_count

        blocks = block_map[0].reshape(parts, plane, 2)
        offsets = jnp.arange(piece_rows, dtype=jnp.int32)
        all_pos = blocks.transpose(1, 0, 2)[..., None] * piece_rows + offsets
        all_pos = all_pos.reshape(plane, tokens)
        query_pos = lax.dynamic_index_in_dim(all_pos, p_index, 0, keepdims=False)
        key_pos = all_pos.reshape(-1)
        cosine, sine_table = rope_tables(query_pos, head_width)
        sign = jnp.where(jnp.arange(head_width) < head_width // 2, -1.0, 1.0).astype(f32)
        query_gain_float = query_gain.astype(f32)
        key_gain_float = key_gain.astype(f32)
        gain_block = jnp.stack([attention_norm_gain, feedforward_gain], axis=1)
        gain_block = jnp.pad(gain_block, ((0, 0), (0, 126)))

        (
            normed,
            projection,
            lin,
            queries,
            both,
            attended_low,
            out_full,
            normed_mlp,
            own_residual,
            gate_columns,
            up_columns,
            down_columns,
            grad_rows,
            stats,
            gains,
        ) = front(
            plane,
            cores,
            hidden_own,
            (
                query_weight,
                key_weight,
                value_weight,
                out_weight,
                gate_weight,
                up_weight,
                down_weight,
            ),
            gain_block,
            grad_own,
            (cosine[:, 0], sine_table[:, 0] * sign),
            (query_pos[None], key_pos[:, None]),
            (query_gain_float[None], key_gain_float[None]),
        )
        results = rear(
            plane,
            cores,
            (
                normed_mlp,
                gate_columns,
                up_columns,
                down_columns,
                grad_rows,
                own_residual,
                projection,
                out_full,
                normed,
                lin,
                queries,
                both,
                attended_low,
            ),
            (
                hidden_own,
                stats,
                gains,
                cosine[:, 0],
                sine_table[:, 0] * sign,
                query_pos[None],
                blocks.transpose(1, 0, 2).reshape(-1),
                query_gain_float[None],
                key_gain_float[None],
            ),
        )
        output, input_grad = results[:2]
        small_sums = results[9]
        block = features // parts
        own_column = p_index * cores + lax.axis_index("c")
        own_gains = lax.dynamic_slice_in_dim(small_sums[:2, :block], own_column * shard, shard, 1)
        head_sums = small_sums[:2, block:]
        return (
            (output[None], input_grad[None])
            + tuple(results[2:9])
            + (own_gains[0], own_gains[1], head_sums[0], head_sums[1])
        )

    return local


def solution(mesh):
    ctx_count, core_count = mesh.shape["ctx"], mesh.shape["fsdp"]
    plane = ctx_count // parts
    fine_mesh = Mesh(mesh.devices.reshape(parts, plane, core_count), ("z", "p", "c"))
    token_spec = P("c", ("z", "p"), None)
    weight_spec = P(("z", "p", "c"), None)
    gain_spec = P(("z", "p", "c"))
    return jax.shard_map(
        make_local(plane, core_count),
        mesh=fine_mesh,
        in_specs=(
            (token_spec, P("c", None)) + (weight_spec,) * 7 + (gain_spec,) * 2 + (P(), P(), token_spec)
        ),
        out_specs=(token_spec,) * 2 + (weight_spec,) * 7 + (gain_spec,) * 2 + (P(), P()),
        check_vma=False,
    )
```

time: 723 us -> 602 us (0.83)
  waiting for transfers between devices: 99.6 us -> 0 us
  Pallas kernels: 533 us -> 576 us
  blocking collectives: 40.1 us -> 0 us
  starting transfers between devices: 16.4 us -> 0 us
  between operations: 13.9 us -> 0.73 us
    reduce_scatter x4 -> x0, waiting for transfers between devices: 61.6 us -> none  [return_columns(): lax.psum_scatter(grads, ('p', 'c'), scatter_dimension=0, tiled=True)]
    pallas_call x2 -> x1, Pallas kernels: 255 us -> 298 us  [rear(): pl.pallas_call(functools.partial(rear_kernel, plane, cores), out_shape=[j...]
    psum x1 -> x0, blocking collectives: 40.1 us -> none  [local(): head_sums = lax.psum(head_sums[:2], ('z', 'p', 'c'))]
    all_to_all x4 -> x0, waiting for transfers between devices: 36.6 us -> none  [return_columns(): return lax.all_to_all(pieces, 'z', 0, 0, tiled=True)]
    all_to_all x4 -> x0, starting transfers between devices: 16.2 us -> none  [return_columns(): return lax.all_to_all(pieces, 'z', 0, 0, tiled=True)]
    unnamed x7 -> x24, local copies, waits for them, and re-layouts: 1.71 us -> 11.7 us
  transfers between devices with their start and end apart: 8 -> 0, of which waited for: 4 -> 0; matrix products, arithmetic and copies ran while one was open for 1% -> 0% of each run, Pallas kernels for 19% -> 0%
where the time goes in v3:
time: 602 us; the launch traced here: 601 us
  Pallas kernels  576 us (96%)
  local copies, waits for them, and re-layouts  18.2 us (3%)
    pallas_call x1, Pallas kernels, rear(): pl.pallas_call(functools.partial(rear_kernel, plane, cores), out_shape=[j...  298 us
    pallas_call x1, Pallas kernels, front(): pl.pallas_call(functools.partial(front_kernel, plane, cores), out_shape=[...  278 us

profile of v3, /device:TPU:0, one launch (start us, length us, event | category | flops | bytes accessed | tf_op | source)
XLA Modules:
  0.0 601.0 jit_solution(4258061702870029756)
XLA Ops:
  0.7 0.5 broadcast.37
  1.2 1.3 reduce.3
  2.5 0.7 pad_maximum_fusion.1
  3.2 1.2 bitcast_convert_fusion
  4.4 0.1 add.49
  4.5 0.1 reshape_squeeze.3
  4.6 0.1 copy.41
  4.7 0.1 copy.42
  4.8 0.6 reshape.73.key_blocks
  5.4 0.1 copy.40
  5.5 0.6 pad.4.gain_block
  6.1 0.1 iota_add_fusion
  6.2 0.1 add.46
  6.3 0.1 add.47
  6.4 0.6 fusion.1
  7.0 0.1 broadcast_multiply_fusion
  7.1 1.8 sine_multiply_fusion
  9.0 2.0 add.58.key_pos
  10.9 278.4 %shard_map.237 = (bf16[512,2048]{1,0:T(8,128)(2,1)}, bf16[4,8,64,1152]{3,2,1,0:T(8,128)(2,1)}, f32[512,768]{1,0:T(8,128)}, bf16[4,512,128]{2,1,0:T(8,128)(2,1)},...) custom-call(bf16[128,2048]{1,0:T(8,128)(2,1)} %bitcast.29, ...), custom_call_target="tpu_custom_call" | custom-call | flops 12000000000 | bytes 100000000 | tf_op jit(solution)/shard_map/pallas_call | solution.py:479
  289.3 297.8 %shard_map.238 = (bf16[128,2048]{1,0:T(8,128)(2,1)}, bf16[128,2048]{1,0:T(8,128)(2,1)}, f32[64,2048]{1,0:T(8,128)}, f32[64,1024]{1,0:T(8,128)}, f32[64,1024]{1,0...) custom-call(bf16[512,2048]{1,0:T(8,128)(2,1)} %get-tuple-element.38., ...), custom_call_target="tpu_custom_call" | custom-call | flops 40000000000 | bytes 100000000 | tf_op jit(solution)/shard_map/pallas_call | solution.py:1172
  587.1 0.0 copy-start.4
  587.1 0.0 copy-start.6
  587.2 0.0 copy-start.5
  587.2 1.3 slice_bitcast_fusion
  588.5 0.7 slice.18
  589.2 0.1 constant_dynamic-slice_fusion
  589.2 0.5 slice_bitcast_fusion.2
  589.8 0.0 copy-start.3
  589.8 1.9 copy.55
  591.7 0.0 copy-start.2
  591.7 2.0 copy.56
  593.7 0.0 copy-done.4
  593.7 0.8 copy.57
  594.5 0.0 copy-done.6
  594.5 0.7 copy.58
  595.2 0.0 copy-done.5
  595.2 0.7 copy.59
  595.9 0.0 copy-done.3
  595.9 0.0 copy-start.1
  595.9 0.8 copy.60
  596.7 0.0 copy-done.2
  596.7 1.1 copy.61
  597.9 0.0 copy-done.1
  597.9 0.0 copy-start
  597.9 1.1 copy.62
  599.0 0.8 copy-done
  599.8 1.1 copy.63
  (5 shorter events, 0.0 us)
Async XLA Ops:
  587.1 6.6 %copy-start.4 = (f32[64,2048]{1,0:T(8,128)S(1)}, f32[64,2048]{1,0:T(8,128)}, u32[]{:S(2)}) copy-start(f32[64,2048]{1,0:T(8,128)} %get-tuple-element.88) | copy-start | bytes 1572868
  587.1 7.4 %copy-start.6 = (f32[64,1024]{1,0:T(8,128)S(1)}, f32[64,1024]{1,0:T(8,128)}, u32[]{:S(2)}) copy-start(f32[64,1024]{1,0:T(8,128)} %get-tuple-element.89) | copy-start | bytes 786436
  587.2 8.1 %copy-start.5 = (f32[64,1024]{1,0:T(8,128)S(1)}, f32[64,1024]{1,0:T(8,128)}, u32[]{:S(2)}) copy-start(f32[64,1024]{1,0:T(8,128)} %get-tuple-element.90) | copy-start | bytes 786436
  589.8 6.2 %copy-start.3 = (f32[64,2048]{1,0:T(8,128)S(1)}, f32[64,2048]{1,0:T(8,128)}, u32[]{:S(2)}) copy-start(f32[64,2048]{1,0:T(8,128)} %get-tuple-element.91) | copy-start | bytes 1572868
  591.7 5.0 copy-start.2
  595.9 1.9 copy-start.1
  597.9 2.0 copy-start

commit v4 on v3

--- a/solution.py
+++ b/solution.py
@@ -15,11 +15,6 @@
 f32 = jnp.float32
 
 
-def unit_rows(values):
-    scale_row = lax.rsqrt(jnp.mean(values * values, axis=-1, keepdims=True) + epsilon)
-    return values * scale_row, scale_row
-
-
 def norm_back(weighted, unit, scale_row):
     inner_mean = jnp.mean(weighted * unit, axis=-1, keepdims=True)
     return scale_row * (weighted - unit * inner_mean)
@@ -33,19 +28,6 @@
     return jnp.cos(angles)[:, None, :], jnp.sin(angles)[:, None, :]
 
 
-def rotate(values, cosine, sine_table):
-    half_width = values.shape[-1] // 2
-    turned = jnp.concatenate([-values[..., half_width:], values[..., :half_width]], axis=-1)
-    return values * cosine + turned * sine_table
-
-
-def rotate_back(grads, cosine, sine_table):
-    half_width = grads.shape[-1] // 2
-    shifted = grads * sine_table
-    turned = jnp.concatenate([shifted[..., half_width:], -shifted[..., :half_width]], axis=-1)
-    return grads * cosine + turned
-
-
 def multiply(left, right):
     return jnp.dot(left, right, preferred_element_type=f32)
 
@@ -78,9 +60,16 @@
 
 
 class Copy:
-    def __init__(self, source, target, sems, device=None):
-        self.source, self.target, self.sems, self.device = source, target, sems, device
-        self.describe().start()
+    def __init__(self, source, target, sems, device=None, when=None):
+        self.source, self.target, self.sems = source, target, sems
+        self.device, self.when = device, when
+        self.guarded(lambda: self.describe().start())
+
+    def guarded(self, action):
+        if self.when is None:
+            action()
+        else:
+            pl.when(self.when)(action)
 
     def describe(self):
         source, target = found(self.source), found(self.target)
@@ -100,7 +89,7 @@
         self.describe().wait()
 
     def wait_send(self):
-        self.describe().wait_send()
+        self.guarded(lambda: self.describe().wait_send())
 
     def wait_recv(self):
         self.describe().wait_recv()
@@ -112,10 +101,13 @@
         self.count, self.local_count = 0, 0
         self.sent, self.kept = [], []
 
-    def send(self, source, target, tracked=True, **device):
+    def send(self, source, target, tracked=True, when=None, lands=None, **device):
         index = self.count
         self.count += 1
-        copy = Copy(source, target, [(self.send_sems, index), (self.recv_sems, index)], device)
+        received = index if lands is None else lands.sems[1][1]
+        copy = Copy(
+            source, target, [(self.send_sems, index), (self.recv_sems, received)], device, when
+        )
         if tracked:
             self.sent.append(copy)
         return copy
@@ -135,6 +127,115 @@
             copy.wait_send()
         for copy in self.kept:
             copy.wait()
+
+
+class LineGather:
+    def __init__(self, links, place, source, block):
+        self.links, self.place, self.block = links, place, block
+        target = block(place.z)
+        self.far = links.send(source, target, z=place.along_z(2))
+        self.above = links.send(source, target, when=place.not_last, z=place.along_z(1))
+        self.below = links.send(source, target, when=place.not_first, z=place.along_z(3))
+
+    def relay(self):
+        links, place = self.links, self.place
+        self.far.wait_recv()
+        block = self.block(place.along_z(2))
+        self.relays = (
+            links.send(block, block, False, place.second, self.above, z=place.along_z(3)),
+            links.send(block, block, False, place.third, self.below, z=place.along_z(1)),
+        )
+
+    def wait(self):
+        self.above.wait_recv()
+        self.below.wait_recv()
+
+    def relayed(self):
+        for copy in self.relays:
+            copy.wait_send()
+
+
+class LineSum:
+    def __init__(self, links, place, part, landed, extra):
+        self.links, self.place = links, place
+        self.part, self.landed, self.extra = part, landed, extra
+        self.near, self.extras, self.far, self.columns = [], [], [], []
+
+    def start(self, columns, tracked=True):
+        links, place = self.links, self.place
+        target = at(self.landed)[place.z, :, columns]
+        rows = place.z_rows
+        above, below = at(self.part)[rows[1], columns], at(self.part)[rows[3], columns]
+        beyond = at(self.part)[rows[2], columns]
+        self.columns.append(columns)
+        self.far.append(links.send(beyond, target, tracked, place.at_end, z=place.along_z(2)))
+        self.near.append(
+            (
+                links.send(above, target, tracked, place.not_last, z=place.along_z(1)),
+                links.send(below, target, tracked, place.not_first, z=place.along_z(3)),
+            )
+        )
+        extra = at(self.extra)[:, columns]
+        self.extras.append(
+            (
+                links.send(below, extra, tracked, place.first, z=place.along_z(1)),
+                links.send(above, extra, tracked, place.last, z=place.along_z(3)),
+            )
+        )
+
+    def combine(self, tracked=True):
+        links, place = self.links, self.place
+
+        @pl.when(place.at_end)
+        def nothing_comes():
+            self.landed[place.opposite] = jnp.zeros(self.landed.shape[1:], bf16)
+
+        for columns, extras, far in zip(self.columns, self.extras, self.far):
+            rows = place.z_rows[2]
+
+            @pl.when(place.second)
+            def arrived():
+                extras[0].wait_recv()
+
+            @pl.when(place.third)
+            def arrived_too():
+                extras[1].wait_recv()
+
+            @pl.when(place.inside)
+            def add():
+                total = self.part[rows, columns].astype(f32) + self.extra[:, columns].astype(f32)
+                self.part[rows, columns] = total.astype(bf16)
+
+            self.near.append(
+                (
+                    links.send(
+                        at(self.part)[rows, columns],
+                        at(self.landed)[place.z, :, columns],
+                        tracked,
+                        place.inside,
+                        lands=far,
+                        z=place.along_z(2),
+                    ),
+                )
+            )
+
+    def wait(self):
+        place = self.place
+        for index, far in enumerate(self.far):
+            above, below = self.near[index]
+
+            @pl.when(place.not_first)
+            def from_below():
+                above.wait_recv()
+
+            @pl.when(place.not_last)
+            def from_above():
+                below.wait_recv()
+
+            far.wait_recv()
+
+    def sent(self):
+        return self.far + [copy for copies in self.near + self.extras for copy in copies]
 
 
 class Place:
@@ -148,6 +249,17 @@
         self.columns_before = [
             lax.rem(self.p + plane - step, plane) * cores + self.c for step in range(plane)
         ]
+        self.first, self.last = self.z == 0, self.z == parts - 1
+        self.second, self.third = self.z == 1, self.z == parts - 2
+        self.not_first, self.not_last = self.z != 0, self.z != parts - 1
+        self.at_end = jnp.logical_or(self.first, self.last)
+        self.inside = jnp.logical_not(self.at_end)
+        self.opposite = parts - 1 - self.z
+        self.relayed = plane == 4
+        if self.relayed:
+            self.flips = [self.p + 1 - 2 * lax.rem(self.p, 2), lax.rem(self.p + 2, 4)]
+            flipped = lax.rem(self.flips[0] + 2, 4)
+            self.flip_columns = [flip * cores + self.c for flip in self.flips + [flipped]]
         self.z_rows = [
             pl.ds(pl.multiple_of(other * token_rows, token_rows), token_rows)
             for other in self.z_others
@@ -170,43 +282,73 @@
 
 
 class Fetch:
-    def __init__(self, links, place, pieces, gathered):
+    def __init__(self, links, place, pieces, gathered, line_only=False):
         self.links, self.place, self.pieces, self.gathered = links, place, pieces, gathered
+        self.line_only = line_only
+        self.first, self.own = [], []
+
+    def mine(self, columns):
+        if self.line_only:
+            return at(self.gathered)[self.place.z, :, columns]
+        return at(self.gathered)[self.place.z, self.place.column, :, columns]
 
     def begin(self):
         links, place = self.links, self.place
-        mine = self.gathered.at[place.z, place.column]
-        self.first, self.own = [], []
+        mine = self.mine
         for shard, width, start, split in self.pieces:
             for step in z_steps:
                 other = place.along_z(step)
                 first = pl.multiple_of(other * width, 128) if split else 0
                 self.first.append(
-                    links.send(shard.at[:, pl.ds(first, width)], mine.at[:, pl.ds(start, width)], z=other)
+                    links.send(at(shard)[:, pl.ds(first, width)], mine(pl.ds(start, width)), z=other)
                 )
             first = pl.multiple_of(place.z * width, 128) if split else 0
             self.own.append(
-                links.local(shard.at[:, pl.ds(first, width)], mine.at[:, pl.ds(start, width)])
-            )
-
-    def spread(self):
-        links, place = self.links, self.place
+                links.local(at(shard)[:, pl.ds(first, width)], mine(pl.ds(start, width)))
+            )
+
+    def arrive(self):
         for copy in self.own:
             copy.wait()
         for copy in self.first:
             copy.wait_recv()
-        block = self.gathered.at[:, place.column]
-        self.second = [
-            links.send(block, block, p=place.in_plane(step)) for step in range(1, place.plane)
-        ]
+
+    def spread(self):
+        links, place = self.links, self.place
+        self.arrive()
+        block = at(self.gathered)[:, place.column]
+        if place.relayed:
+            self.second = [links.send(block, block, p=other) for other in place.flips]
+        else:
+            self.second = [
+                links.send(block, block, p=place.in_plane(step)) for step in range(1, place.plane)
+            ]
         self.third = [links.send(block, block, c=other) for other in place.siblings()]
+        self.halves = []
+
+    def pass_on(self, column):
+        block = at(self.gathered)[:, column]
+        self.third += [self.links.send(block, block, c=other) for other in self.place.siblings()]
 
     def forward(self):
         links, place = self.links, self.place
-        for step, copy in enumerate(self.second, 1):
-            copy.wait_recv()
-            block = self.gathered.at[:, place.before(step)]
-            self.third += [links.send(block, block, c=other) for other in place.siblings()]
+        if place.relayed:
+            for side, copy in enumerate(self.second):
+                copy.wait_recv()
+                column = place.flip_columns[side]
+                half = at(self.gathered)[pl.ds(side * (parts // 2), parts // 2), column]
+                self.halves.append(links.send(half, half, p=place.flips[1 - side]))
+                self.pass_on(column)
+        else:
+            for step, copy in enumerate(self.second, 1):
+                copy.wait_recv()
+                self.pass_on(place.before(step))
+
+    def close(self):
+        if self.place.relayed:
+            for copy in self.halves:
+                copy.wait_recv()
+            self.pass_on(self.place.flip_columns[2])
 
     def finish(self):
         for copy in self.third:
@@ -225,7 +367,6 @@
     up_weight,
     down_weight,
     gain_block,
-    grad_out,
     cosine,
     sine_turned,
     query_pos,
@@ -244,7 +385,6 @@
     gate_out,
     up_out,
     down_out,
-    grad_rows_out,
     stats_out,
     gains_out,
     hidden_all,
@@ -288,23 +428,24 @@
     out_fetch = Fetch(links, place, [(out_weight, out_weight.shape[1], 0, False)], out_full)
     mlp_fetches = [
         Fetch(links, place, [(weight, hidden_units, 0, True)], target)
-        for weight, target in ((gate_weight, gate_out), (up_weight, up_out), (down_weight, down_out))
+        for weight, target in ((gate_weight, gate_out), (up_weight, up_out))
     ]
+    down_fetch = Fetch(links, place, [(down_weight, hidden_units, 0, True)], down_out, True)
     heads_fetch.begin()
-    hidden_copies = [
-        links.send(hidden, hidden_all.at[place.z], z=place.along_z(step)) for step in z_steps
-    ]
+    out_fetch.begin()
+    heads_fetch.spread()
     hidden_own = links.local(hidden, hidden_all.at[place.z])
-    heads_fetch.spread()
-    out_fetch.begin()
-    for fetch in mlp_fetches:
-        fetch.begin()
-    hidden_own.wait()
-    for copy in hidden_copies:
-        copy.wait_recv()
+    hidden_gather = LineGather(links, place, hidden, lambda z: at(hidden_all)[z])
+    out_fetch.spread()
     heads_fetch.forward()
+    hidden_gather.relay()
+    heads_fetch.close()
     heads_fetch.finish()
     links.keep(projection, projection_out)
+    hidden_own.wait()
+    hidden_gather.wait()
+    for fetch in mlp_fetches + [down_fetch]:
+        fetch.begin()
 
     gain_columns = projection[:, :, :, lin_width : lin_width + 128].reshape(width, 128)
     gain_rows = gain_columns.astype(f32).T
@@ -349,18 +490,18 @@
         queries[index] = rope(lin[:, columns], query_gain[...])
     links.keep(lin.at[:, pl.ds(0, query_width + key_width)], lin_out)
     links.keep(queries, queries_out)
-    out_fetch.spread()
-    mlp_fetches[0].spread()
+    out_fetch.forward()
     for copy in both_copies:
         copy.wait_recv()
     links.keep(both, both_out)
+    mlp_fetches[0].spread()
 
     factor = head ** (-0.5) * 1.4426950408889634
     chunk = min(256, tokens)
     chunks_each = tokens // chunk
     lanes = group * tokens
     own_attended = attended_all.at[place.z]
-    attended_copies = []
+    attended_gathers = []
     for key_head in range(key_heads):
         block = queries[key_head * group : (key_head + 1) * group].reshape(lanes, head)
         positions = jnp.concatenate([query_pos[...]] * group, axis=1)
@@ -396,21 +537,28 @@
             own_attended[:, index * head : (index + 1) * head] = mixed_rows[
                 member * tokens : (member + 1) * tokens
             ].astype(bf16)
-        part = own_attended.at[:, pl.ds(key_head * group * head, group * head)]
-        attended_copies += [links.send(part, part, z=place.along_z(step)) for step in z_steps]
+        columns = pl.ds(key_head * group * head, group * head)
+        attended_gathers.append(
+            LineGather(
+                links,
+                place,
+                at(attended_all)[place.z, :, columns],
+                lambda z, columns=columns: at(attended_all)[z, :, columns],
+            )
+        )
         if key_head == 0:
-            out_fetch.forward()
-            mlp_fetches[1].spread()
-    grad_copies = [
-        links.send(grad_out, grad_rows_out.at[place.z], z=place.along_z(step)) for step in z_steps
-    ]
-    links.keep(grad_out, grad_rows_out.at[place.z])
+            out_fetch.close()
     links.keep(own_attended, attended_out)
-    mlp_fetches[2].spread()
+    mlp_fetches[0].forward()
+    mlp_fetches[1].spread()
+    for gather in attended_gathers:
+        gather.relay()
+    mlp_fetches[0].close()
     out_fetch.finish()
     links.keep(out_full, out_columns_out)
-    for copy in attended_copies:
-        copy.wait_recv()
+    mlp_fetches[1].forward()
+    for gather in attended_gathers:
+        gather.wait()
 
     def add_out(index, carry):
         weights = out_full[index].reshape(width // parts, parts * query_width)
@@ -424,7 +572,6 @@
         return carry
 
     lax.fori_loop(0, parts, add_out, 0)
-    mlp_fetches[0].forward()
 
     def norm_two(index, carry):
         rows = pl.ds(pl.multiple_of(index * token_rows, token_rows), token_rows)
@@ -437,16 +584,16 @@
     links.keep(normed_mlp, normed_mlp_out)
     own_rows = place.z_rows[0]
     links.keep(residual.at[own_rows], residual_out)
-    mlp_fetches[1].forward()
-    mlp_fetches[2].forward()
-    for copy in grad_copies:
-        copy.wait_recv()
+    mlp_fetches[1].close()
+    down_fetch.arrive()
     for fetch in mlp_fetches:
         fetch.finish()
+    for gather in [hidden_gather] + attended_gathers:
+        gather.relayed()
     links.finish()
 
 
-def front(plane, cores, hidden, weights, gain_block, grad_out, tables, positions, head_gains):
+def front(plane, cores, hidden, weights, gain_block, tables, positions, head_gains):
     token_rows, width = hidden.shape
     tokens = parts * token_rows
     shard = weights[0].shape[0]
@@ -457,7 +604,7 @@
     query_heads = query_width // head
     group = query_width // key_width
     stacked = (parts, plane * cores, shard)
-    copies = 3 * 7 + 3 * 3 + 3 * 2 + 5 * (2 * plane - 1) + plane + 8
+    copies = 24 + 5 * (2 * plane + 8) + plane + 24
     any_space, vmem = pl.BlockSpec(memory_space=pl.ANY), pl.BlockSpec(memory_space=pltpu.VMEM)
     outputs = [
         ((tokens, width), bf16),
@@ -471,16 +618,15 @@
         ((token_rows, width), f32),
         (stacked + (hidden_units,), bf16),
         (stacked + (hidden_units,), bf16),
-        (stacked + (hidden_units,), bf16),
-        ((parts, token_rows, width), bf16),
+        ((parts, shard, hidden_units), bf16),
         ((8, tokens), f32),
         ((8, width), f32),
     ]
     return pl.pallas_call(
         functools.partial(front_kernel, plane, cores),
         out_shape=[jax.ShapeDtypeStruct(shape, kind) for shape, kind in outputs],
-        in_specs=[any_space] * 10 + [vmem] * 6,
-        out_specs=[any_space] * 13 + [vmem] * 2,
+        in_specs=[any_space] * 9 + [vmem] * 6,
+        out_specs=[any_space] * 12 + [vmem] * 2,
         scratch_shapes=[
             pltpu.VMEM((parts, token_rows, width), bf16),
             pltpu.VMEM((tokens, width), bf16),
@@ -501,24 +647,11 @@
             has_side_effects=True, vmem_limit_bytes=60 * 1024 * 1024
         ),
         cost_estimate=pl.CostEstimate(flops=12 * 10**9, bytes_accessed=10**8, transcendentals=10**7),
-    )(hidden, *weights, gain_block, grad_out, *tables, *positions, *head_gains)
+    )(hidden, *weights, gain_block, *tables, *positions, *head_gains)
 
 
 def half_turn(values):
     return pltpu.roll(values, values.shape[1] // 2, 1)
-
-
-def scatter_sends(links, place, piece, landed, token_rows, columns, tracked=True):
-    copies = []
-    for step in z_steps:
-        other = place.along_z(step)
-        rows = place.z_rows[step]
-        copies.append(
-            links.send(
-                at(piece)[rows, columns], at(landed)[place.z, :, columns], tracked, z=other
-            )
-        )
-    return copies
 
 
 def total_of(landed):
@@ -586,40 +719,51 @@
     def take(self, family, left, right, start=0):
         size = right.shape[1]
         columns = pl.ds(start, size)
-        kept = []
+        loads, kept = [], []
+        slots = self.addend.shape[0]
+
+        def load(index):
+            self.sibling_copies[family, start, index].wait_recv()
+            loads.append(
+                self.local(
+                    at(self.from_sibling)[family, index, :, :, columns],
+                    at(self.addend)[index % slots, :, :, columns],
+                )
+            )
+
+        for index in range(slots):
+            load(index)
         for index in range(parts):
             slot = self.slot()
-            self.sibling_copies[family, start, index].wait_recv()
-            side = 0
-            load = self.local(
-                at(self.from_sibling)[family, index, :, :, columns],
-                at(self.addend)[side, :, :, columns],
-            )
-            load.wait()
-            self.product(slot, left, self.place.c, right, start, index, side)
-            copy = self.local(
-                at(self.ring)[slot, :, :, columns], at(self.halves)[family, index, :, :, columns]
-            )
-            kept.append(copy)
-            self.pending[slot].append(lambda: None)
-            if index >= 1:
-                kept[index - 1].wait()
-        kept[-1].wait()
+            loads[index].wait()
+            self.product(slot, left, self.place.c, right, start, index, index % slots)
+            if index + slots < parts:
+                load(index + slots)
+            kept.append(
+                self.local(
+                    at(self.ring)[slot, :, :, columns],
+                    at(self.halves)[family, index, :, :, columns],
+                )
+            )
+            self.pending[slot].append(kept[-1].wait)
+        for waits in self.pending:
+            for wait in waits:
+                wait()
+            waits.clear()
         self.send_plane(family, columns)
 
     def send_plane(self, family, columns):
         links, place = self.links, self.place
-        copies = []
+        sent = self.plane_copies.setdefault(family, [])
         for step in range(1, place.plane):
             other = place.in_plane(step)
-            copies.append(
+            sent.append(
                 links.send(
                     at(self.halves)[family, :, other, :, columns],
                     at(self.from_plane)[family, place.p, :, :, columns],
                     p=other,
                 )
             )
-        self.plane_copies.setdefault(family, []).extend(copies)
         self.mine.setdefault(family, []).append(
             self.local(
                 at(self.halves)[family, :, place.p, :, columns],
@@ -627,74 +771,57 @@
             )
         )
 
-    def along_z(self, family):
+    def along_z(self, family, columns):
         links, place = self.links, self.place
         for copy in self.plane_copies[family]:
             copy.wait_recv()
         for copy in self.mine[family]:
             copy.wait()
+        sources = place.plane
         loads = []
         for index in range(parts):
             slot = self.slot()
             loads.append(
-                (slot, self.local(at(self.from_plane)[family, :, index], at(self.ring)[slot]))
+                (
+                    slot,
+                    self.local(
+                        at(self.from_plane)[family, pl.ds(0, sources), index, :, columns],
+                        at(self.ring)[slot, pl.ds(0, sources), :, columns],
+                    ),
+                )
             )
         for index, (slot, load) in enumerate(loads):
             load.wait()
-            total = self.ring[slot, 0].astype(f32)
-            for source in range(1, place.plane):
-                total += self.ring[slot, source].astype(f32)
-            self.sums[family, index] = total.astype(bf16)
+            total = self.ring[slot, 0, :, columns].astype(f32)
+            for source in range(1, sources):
+                total += self.ring[slot, source, :, columns].astype(f32)
+            self.sums[family, index, :, columns] = total.astype(bf16)
         copies = []
         for step in z_steps:
             other = place.along_z(step)
             copies.append(
-                links.send(at(self.sums)[family, other], at(self.final)[family, place.z], z=other)
+                links.send(
+                    at(self.sums)[family, other, :, columns],
+                    at(self.final)[family, place.z, :, columns],
+                    z=other,
+                )
             )
         self.own_final[family] = self.local(
-            at(self.sums)[family, place.z], at(self.final)[family, place.z]
+            at(self.sums)[family, place.z, :, columns],
+            at(self.final)[family, place.z, :, columns],
         )
         self.z_copies[family] = copies
 
-    def home(self, family, stage, stage_sems, targets):
+    def home(self, family):
         for copy in self.z_copies[family]:
             copy.wait_recv()
         self.own_final[family].wait()
-        loads = []
-        for index in range(parts):
-            loaded = self.slot()
-            loads.append(
-                (loaded, self.local(at(self.final)[family, index], at(self.ring)[loaded, 0]))
-            )
-        for index in range(parts):
-            slot = self.out_turn % stage.shape[0]
-            for copy in self.out_pending[slot]:
-                copy.wait()
-            loaded, load = loads[index]
-            load.wait()
-            stage[slot] = self.ring[loaded, 0].astype(f32)
-            self.out_pending[slot] = []
-            for target, start, width in targets:
-                copy = Copy(
-                    at(stage)[slot, :, pl.ds(start, width)],
-                    at(target)[:, pl.ds(index * width, width)],
-                    [(stage_sems, self.out_used)],
-                )
-                self.out_used += 1
-                self.out_pending[slot].append(copy)
-            self.out_turn += 1
-
-    out_turn = 0
-    out_used = 0
 
     def finish(self):
         assert self.used <= self.ring_sems.shape[0]
         for waits in self.pending:
             for wait in waits:
                 wait()
-        for copies in self.out_pending:
-            for copy in copies:
-                copy.wait()
 
 
 def rear_kernel(
@@ -704,7 +831,6 @@
     gate_in,
     up_in,
     down_in,
-    grad_in,
     residual_in,
     projection_in,
     out_in,
@@ -714,6 +840,7 @@
     both_in,
     attended_in,
     hidden,
+    grad_out,
     stats,
     gains,
     cosine,
@@ -724,13 +851,6 @@
     key_gain,
     output,
     input_grad,
-    query_grad,
-    key_grad,
-    value_grad,
-    out_grad,
-    gate_grad,
-    up_grad,
-    down_grad,
     small_sums,
     from_sibling,
     halves,
@@ -746,20 +866,20 @@
     part_in,
     landed_in,
     landed_out,
+    extra_in,
+    extra_out,
     residual,
     grad_residual,
     low_rows,
     sums,
     ring,
     addend,
-    stage,
     gain_rows,
     messages,
     z_messages,
     plane_messages,
     core_messages,
     ring_sems,
-    stage_sems,
     both_sems,
     send_sems,
     recv_sems,
@@ -772,7 +892,6 @@
     returns = Returns(
         links, place, ring, addend, ring_sems, (from_sibling, halves, from_plane, sums, final)
     )
-    returns.out_pending = [[] for _ in range(stage.shape[0])]
     units = gate.shape[3]
     block = width // parts
     shard = gate.shape[2]
@@ -787,18 +906,25 @@
     part_out = normed
     split = (plane, cores, shard, tokens)
 
-    low_copies, out_copies, landed_copies = [], [], []
-
-    def feed_forward(grad_rows, act, d_gate, d_up):
+    gathers = []
+    all_units = pl.ds(0, units)
+    out_sum = LineSum(links, place, part_out, landed_out, extra_out)
+    back_sum = LineSum(links, place, part_in, landed_in, extra_in)
+
+    def feed_forward(act, d_gate, d_up):
+        own_down = links.local(down_in, at(down)[:, place.column])
         loads = [
             links.local(normed_mlp_in, normed),
             links.local(gate_in, gate),
             links.local(up_in, up),
-            links.local(grad_in, grad_rows),
-            links.local(down_in, down),
             links.local(residual_in, residual),
         ]
-        for copy in loads:
+        low_rows[place.z] = grad_out[...]
+        gathers.append(LineGather(links, place, grad_out, lambda z: at(low_rows)[z]))
+        own_down.wait()
+        down_fetch = Fetch(links, place, [], down)
+        down_fetch.spread()
+        for copy in loads[:3]:
             copy.wait()
         tile = 256
 
@@ -806,71 +932,81 @@
             columns = pl.ds(pl.multiple_of(index * tile, tile), tile)
             gate_lin = multiply(normed[...], gate[:, :, :, columns].reshape(width, tile))
             up_lin = multiply(normed[...], up[:, :, :, columns].reshape(width, tile))
-            grad_act = multiply(
-                grad_rows[...].reshape(tokens, width), down[:, :, :, columns].reshape(width, tile)
-            )
             sigmoid = jax.nn.sigmoid(gate_lin)
             silu = gate_lin * sigmoid
             act[:, columns] = (silu * up_lin).astype(bf16)
-            d_up[:, columns] = (grad_act * silu).astype(bf16)
-            d_gate[:, columns] = (
-                grad_act * up_lin * (sigmoid + silu * (1.0 - sigmoid))
+            d_up[:, columns] = silu.astype(bf16)
+            d_gate[:, columns] = (up_lin * (sigmoid + silu * (1.0 - sigmoid))).astype(bf16)
+            return carry
+
+        lax.fori_loop(0, units // tile, hidden_tile, 0)
+        gathers[0].relay()
+        down_fetch.forward()
+        for copy in loads[3:]:
+            copy.wait()
+        for index in range(parts):
+            columns = slice(index * block, (index + 1) * block)
+            turned_left[index] = normed[:, columns].T.reshape(split)
+        down_fetch.close()
+        down_fetch.finish()
+        for index in range(parts):
+            columns = pl.ds(index * block, block)
+            part_out[:, columns] = multiply_trans(
+                act[...], down[index].reshape(block, units)
             ).astype(bf16)
+        landed_out[place.z] = part_out[own_rows]
+        gathers[0].wait()
+
+        def grad_tile(index, carry):
+            columns = pl.ds(pl.multiple_of(index * tile, tile), tile)
+            grad_act = multiply(
+                low_rows[...].reshape(tokens, width), down[:, :, :, columns].reshape(width, tile)
+            )
+            d_up[:, columns] = (grad_act * d_up[:, columns].astype(f32)).astype(bf16)
+            d_gate[:, columns] = (grad_act * d_gate[:, columns].astype(f32)).astype(bf16)
             return carry
 
-        lax.fori_loop(0, units // tile, hidden_tile, 0)
-        in_copies = []
+        lax.fori_loop(0, units // tile, grad_tile, 0)
+        gathers[0].relayed()
+        for index in range(parts):
+            columns = slice(index * block, (index + 1) * block)
+            turned_right[index] = low_rows[:, :, columns].reshape(tokens, block).T.reshape(split)
+        in_sum = LineSum(links, place, part_in, landed_in, extra_in)
         for index in range(parts):
             columns = pl.ds(index * block, block)
             part_in[:, columns] = (
                 multiply_trans(d_gate[...], gate[index].reshape(block, units))
                 + multiply_trans(d_up[...], up[index].reshape(block, units))
             ).astype(bf16)
-            in_copies += scatter_sends(
-                links, place, part_in, landed_in, token_rows, columns, False
-            )
+            in_sum.start(columns, False)
         landed_in[place.z] = part_in[own_rows]
-        for index in range(parts):
-            columns = slice(index * block, (index + 1) * block)
-            turned_left[index] = normed[:, columns].T.reshape(split)
-            turned_right[index] = grad_rows[:, :, columns].reshape(tokens, block).T.reshape(split)
         returns.give(0, turned_left, d_gate)
         returns.give(1, turned_left, d_up)
+        in_sum.combine(False)
         returns.take(0, turned_left, d_gate)
-        returns.take(1, turned_left, d_up)
-        for index in range(parts):
-            columns = pl.ds(index * block, block)
-            part_out[:, columns] = multiply_trans(
-                act[...], down[index].reshape(block, units)
-            ).astype(bf16)
-        landed_out[place.z] = part_out[own_rows]
-
-        for copy in in_copies:
-            copy.wait_recv()
+
+        in_sum.wait()
         grad_normed = total_of(landed_in)
         values = residual[...]
         scale = lax.rsqrt(jnp.mean(values * values, axis=-1, keepdims=True) + epsilon)
         unit = values * scale
         gain_rows[1:2] = jnp.sum(grad_normed * unit, axis=0, keepdims=True)
-        own_grad = grad_rows[place.z].astype(f32)
+        own_grad = grad_out[...].astype(f32)
         total = own_grad + norm_back(grad_normed * gains[1:2], unit, scale)
         grad_residual[...] = total
         low_rows[place.z] = total.astype(bf16)
-        own_low = at(low_rows)[place.z]
-        low_copies.extend(
-            links.send(own_low, own_low, z=place.along_z(step)) for step in z_steps
+        gathers.append(
+            LineGather(links, place, at(low_rows)[place.z], lambda z: at(low_rows)[z])
         )
-        out_copies.extend(
-            scatter_sends(links, place, part_out, landed_out, token_rows, pl.ds(0, width))
-        )
+        returns.take(1, turned_left, d_up)
+        gathers[1].relay()
         returns.give(2, turned_right, act)
         returns.take(2, turned_right, act)
-        for copy in in_copies:
+        for copy in in_sum.sent():
             copy.wait_send()
 
     pl.run_scoped(
         feed_forward,
-        pltpu.VMEM((parts, token_rows, width), bf16),
         pltpu.VMEM((tokens, units), bf16),
         pltpu.VMEM((tokens, units), bf16),
         pltpu.VMEM((tokens, units), bf16),
@@ -894,8 +1030,8 @@
         for index in range(parts):
             columns = slice(index * block, (index + 1) * block)
             turned_left[index] = part_in[:, columns].T.reshape(split)
-        for copy in low_copies:
-            copy.wait_recv()
+        gathers[1].wait()
+        out_sum.start(pl.ds(0, width))
 
         tile = group * head
         for index in range(key_heads):
@@ -972,6 +1108,8 @@
                         at(both)[place.p, :, columns], at(both_landed)[place.p, :, columns]
                     )
                 )
+            if key_head == 0:
+                out_sum.combine()
             grad_queries = query_total[...].T * factor
             for member in range(group):
                 number = key_head * group + member
@@ -993,9 +1131,13 @@
         for index in range(parts):
             columns = slice(index * block, (index + 1) * block)
             turned_right[index] = low_rows[:, :, columns].reshape(tokens, block).T.reshape(split)
-        returns.give(3, turned_right, attended, lin_width)
-        returns.take(3, turned_right, attended, lin_width)
-        returns.along_z(0)
+        returns.give(3, turned_right, attended, query_width)
+        query_lin = at(grad_lin)[:, pl.ds(0, query_width)].get()
+        returns.give(3, turned_left, query_lin)
+        returns.take(3, turned_right, attended, query_width)
+        returns.along_z(0, all_units)
+        returns.take(3, turned_left, query_lin)
+        returns.along_z(1, all_units)
 
         for copy in both_copies:
             copy.wait_recv()
@@ -1042,14 +1184,13 @@
             part_in[:, columns] = multiply_trans(
                 grad_lin[...], gate[index, :, :, 0:lin_width].reshape(block, lin_width)
             ).astype(bf16)
-            landed_copies.extend(
-                scatter_sends(links, place, part_in, landed_in, token_rows, columns)
-            )
+            back_sum.start(columns)
         landed_in[place.z] = part_in[own_rows]
-        returns.give(3, turned_left, grad_lin)
-        returns.take(3, turned_left, grad_lin)
-        returns.along_z(1)
-        returns.along_z(2)
+        both_lin = at(grad_lin)[:, pl.ds(query_width, 2 * key_width)].get()
+        returns.give(4, turned_left, both_lin)
+        back_sum.combine()
+        returns.take(4, turned_left, both_lin)
+        returns.along_z(2, all_units)
         for copy in both_copies:
             copy.wait_send()
 
@@ -1066,10 +1207,7 @@
         pltpu.VMEM((head, group * tokens), f32),
         pltpu.VMEM((tokens, lin_width), bf16),
     )
-    returns.along_z(3)
-
-    for copy in landed_copies:
-        copy.wait_recv()
+    back_sum.wait()
     grad_normed = total_of(landed_in)
     values = hidden[...].astype(f32)
     scale = lax.rsqrt(jnp.mean(values * values, axis=-1, keepdims=True) + epsilon)
@@ -1088,8 +1226,7 @@
         for step in z_steps
     ]
     z_messages[place.z] = messages[place.z]
-    for copy in out_copies:
-        copy.wait_recv()
+    out_sum.wait()
     output[...] = (residual[...] + total_of(landed_out)).astype(bf16)
     for copy in copies:
         copy.wait_recv()
@@ -1100,7 +1237,8 @@
         )
         for step in range(1, plane)
     ]
-    returns.home(0, stage, stage_sems, [(gate_grad, 0, units)])
+    returns.along_z(3, pl.ds(0, 2 * query_width))
+    returns.along_z(4, pl.ds(0, 2 * key_width))
     for copy in copies:
         copy.wait_recv()
     total = plane_messages[0]
@@ -1111,32 +1249,22 @@
         links.send(at(core_messages)[place.c], at(core_messages)[place.c], c=other)
         for other in place.siblings()
     ]
-    returns.home(1, stage, stage_sems, [(up_grad, 0, units)])
     for copy in copies:
         copy.wait_recv()
     total = core_messages[0]
     for source in range(1, cores):
         total += core_messages[source]
     small_sums[...] = total
-    returns.home(2, stage, stage_sems, [(down_grad, 0, units)])
-    returns.home(
-        3,
-        stage,
-        stage_sems,
-        [
-            (query_grad, 0, query_width),
-            (key_grad, query_width, key_width),
-            (value_grad, query_width + key_width, key_width),
-            (out_grad, lin_width, query_width),
-        ],
-    )
+    for family in range(5):
+        returns.home(family)
+    gathers[1].relayed()
     returns.finish()
     links.finish()
 
 
 def rear(plane, cores, large, small):
     normed_mlp, gate = large[0], large[1]
-    projection, lin, queries, both = large[6], large[9], large[10], large[11]
+    projection, lin, queries, both = large[5], large[8], large[9], large[10]
     tokens, width = normed_mlp.shape
     token_rows = tokens // parts
     _, columns, shard, units = gate.shape
@@ -1147,24 +1275,16 @@
     lin_width = query_width + 2 * key_width
     block = width // parts
     any_space, vmem = pl.BlockSpec(memory_space=pl.ANY), pl.BlockSpec(memory_space=pltpu.VMEM)
-    copies = 16 + 12 + 6 + 12 + 20 + 10 * plane + 12 + 8
-    wide = lin_width + query_width
-    assert wide == units
+    copies = 120 + 10 + 6 + 24 + 24 + 16 * plane + 48 + 16
+    assert 2 * max(query_width, key_width) <= units
     shapes = [
         ((token_rows, width), bf16),
         ((token_rows, width), bf16),
-        ((shard, parts * query_width), f32),
-        ((shard, parts * key_width), f32),
-        ((shard, parts * key_width), f32),
-        ((shard, parts * query_width), f32),
-        ((shard, parts * units), f32),
-        ((shard, parts * units), f32),
-        ((shard, parts * units), f32),
         ((8, block + head), f32),
-        ((4, parts, plane, shard, units), bf16),
-        ((4, parts, plane, shard, units), bf16),
-        ((4, plane, parts, shard, units), bf16),
-        ((4, parts, shard, units), bf16),
+        ((5, parts, plane, shard, units), bf16),
+        ((5, parts, plane, shard, units), bf16),
+        ((5, plane, parts, shard, units), bf16),
+        ((5, parts, shard, units), bf16),
         ((plane, tokens, 2 * key_width), bf16),
     ]
     turned = (parts, plane, cores, shard, tokens)
@@ -1172,11 +1292,11 @@
     return pl.pallas_call(
         functools.partial(rear_kernel, plane, cores),
         out_shape=[jax.ShapeDtypeStruct(shape, kind) for shape, kind in shapes],
-        in_specs=[any_space] * 13
-        + [vmem] * 6
+        in_specs=[any_space] * 12
+        + [vmem] * 7
         + [pl.BlockSpec(memory_space=pltpu.SMEM)]
         + [vmem] * 2,
-        out_specs=[vmem] * 2 + [any_space] * 7 + [vmem] + [any_space] * 5,
+        out_specs=[vmem] * 3 + [any_space] * 5,
         scratch_shapes=[
             pltpu.VMEM((tokens, width), bf16),
             pltpu.VMEM(turned, bf16),
@@ -1187,20 +1307,20 @@
             pltpu.VMEM((tokens, width), bf16),
             pltpu.VMEM((parts, token_rows, width), bf16),
             pltpu.VMEM((parts, token_rows, width), bf16),
+            pltpu.VMEM((token_rows, width), bf16),
+            pltpu.VMEM((token_rows, width), bf16),
             pltpu.VMEM((token_rows, width), f32),
             pltpu.VMEM((token_rows, width), f32),
             pltpu.VMEM((parts, token_rows, width), bf16),
-            pltpu.VMEM((4, parts, shard, units), bf16),
+            pltpu.VMEM((5, parts, shard, units), bf16),
             pltpu.VMEM((4, plane, shard, units), bf16),
-            pltpu.VMEM((1, plane, shard, units), bf16),
-            pltpu.VMEM((2, shard, units), f32),
+            pltpu.VMEM((parts if plane == 4 else 1, plane, shard, units), bf16),
             pltpu.VMEM((2, width), f32),
             pltpu.VMEM((parts,) + message, f32),
             pltpu.VMEM((parts,) + message, f32),
             pltpu.VMEM((plane,) + message, f32),
             pltpu.VMEM((cores,) + message, f32),
-            pltpu.SemaphoreType.DMA((128,)),
-            pltpu.SemaphoreType.DMA((32,)),
+            pltpu.SemaphoreType.DMA((160,)),
             pltpu.SemaphoreType.DMA((plane,)),
             pltpu.SemaphoreType.DMA((copies,)),
             pltpu.SemaphoreType.DMA((copies,)),
@@ -1264,7 +1384,6 @@
             gate_columns,
             up_columns,
             down_columns,
-            grad_rows,
             stats,
             gains,
         ) = front(
@@ -1281,7 +1400,6 @@
                 down_weight,
             ),
             gain_block,
-            grad_own,
             (cosine[:, 0], sine_table[:, 0] * sign),
             (query_pos[None], key_pos[:, None]),
             (query_gain_float[None], key_gain_float[None]),
@@ -1294,7 +1412,6 @@
                 gate_columns,
                 up_columns,
                 down_columns,
-                grad_rows,
                 own_residual,
                 projection,
                 out_full,
@@ -1306,6 +1423,7 @@
             ),
             (
                 hidden_own,
+                grad_own,
                 stats,
                 gains,
                 cosine[:, 0],
@@ -1317,14 +1435,29 @@
             ),
         )
         output, input_grad = results[:2]
-        small_sums = results[9]
+        small_sums, final = results[2], results[6]
+
+        def home(family, start, count):
+            columns = final[family, :, :, start : start + count].transpose(1, 0, 2)
+            return columns.astype(f32).reshape(shard, parts * count)
+
+        units = gate_weight.shape[1] // parts
+        query_width, key_width = query_weight.shape[1] // parts, key_weight.shape[1] // parts
         block = features // parts
         own_column = p_index * cores + lax.axis_index("c")
         own_gains = lax.dynamic_slice_in_dim(small_sums[:2, :block], own_column * shard, shard, 1)
         head_sums = small_sums[:2, block:]
         return (
             (output[None], input_grad[None])
-            + tuple(results[2:9])
+            + (
+                home(3, 0, query_width),
+                home(4, 0, key_width),
+                home(4, key_width, key_width),
+                home(3, query_width, query_width),
+                home(0, 0, units),
+                home(1, 0, units),
+                home(2, 0, units),
+            )
             + (own_gains[0], own_gains[1], head_sums[0], head_sums[1])
         )
 

time: 602 us -> 523 us (0.87)
  Pallas kernels: 576 us -> 491 us
    pallas_call x1, Pallas kernels: 278 us -> 191 us  [front(): pl.pallas_call(functools.partial(front_kernel, plane, cores), out_shape=[...]
    unnamed x24 -> x9, local copies, waits for them, and re-layouts: 11.7 us -> 2.11 us
    reshape x0 -> x7, local copies, waits for them, and re-layouts: none -> 6.94 us  [home(): return columns.astype(f32).reshape(shard, parts * count)]
where the time goes in v4:
time: 523 us; the launch traced here: 517 us
  Pallas kernels  491 us (94%)
  local copies, waits for them, and re-layouts  15.5 us (3%)
  other arithmetic  9.08 us (2%)
    pallas_call x1, Pallas kernels, rear(): pl.pallas_call(functools.partial(rear_kernel, plane, cores), out_shape=[j...  300 us
    pallas_call x1, Pallas kernels, front(): pl.pallas_call(functools.partial(front_kernel, plane, cores), out_shape=[...  191 us

profile of v4, /device:TPU:0, one launch (start us, length us, event | category | flops | bytes accessed | tf_op | source)
XLA Modules:
  0.0 516.7 jit_solution(17962602409413508599)
XLA Ops:
  0.7 0.5 broadcast.37
  1.2 1.3 reduce.3
  2.5 0.7 pad_maximum_fusion.1
  3.2 1.2 bitcast_convert_fusion
  4.4 0.1 add.49
  4.5 0.1 reshape_squeeze.3
  4.6 0.1 copy.55
  4.7 0.1 copy.56
  4.8 0.6 reshape.129.key_blocks
  5.4 0.1 copy.54
  5.5 0.6 pad.4.gain_block
  6.1 0.1 iota_add_fusion
  6.2 0.1 add.46
  6.3 0.1 add.47
  6.4 0.6 fusion.1
  7.0 0.1 broadcast_multiply_fusion
  7.1 1.8 sine_multiply_fusion
  9.0 2.0 add.58.key_pos
  10.9 191.0 %shard_map.237 = (bf16[512,2048]{1,0:T(8,128)(2,1)}, bf16[4,8,64,1152]{3,2,1,0:T(8,128)(2,1)}, f32[512,768]{1,0:T(8,128)}, bf16[4,512,128]{2,1,0:T(8,128)(2,1)},...) custom-call(bf16[128,2048]{1,0:T(8,128)(2,1)} %bitcast.84, ...), custom_call_target="tpu_custom_call" | custom-call | flops 12000000000 | bytes 100000000 | tf_op jit(solution)/shard_map/pallas_call | solution.py:625
  202.0 300.0 %shard_map.238 = (bf16[128,2048]{1,0:T(8,128)(2,1)}, bf16[128,2048]{1,0:T(8,128)(2,1)}, f32[8,640]{1,0:T(8,128)}, bf16[5,4,4,64,1536]{4,3,2,1,0:T(8,128)(2,1)}, ...) custom-call(bf16[512,2048]{1,0:T(8,128)(2,1)} %get-tuple-element.31., ...), custom_call_target="tpu_custom_call" | custom-call | flops 40000000000 | bytes 100000000 | tf_op jit(solution)/shard_map/pallas_call | solution.py:1292
  502.0 1.3 slice_bitcast_fusion
  503.3 0.7 slice.46
  504.0 0.1 constant_dynamic-slice_fusion
  504.1 0.5 slice_bitcast_fusion.2
  504.6 1.0 convert_bitcast_fusion.5
  505.6 0.7 copy.69
  506.4 0.0 copy-start
  506.4 0.7 copy.68
  507.1 1.6 convert_bitcast_fusion.3
  508.7 0.8 copy.70
  509.5 0.8 copy.67
  510.4 0.0 copy-done
  510.4 0.6 convert_bitcast_fusion
  511.0 1.3 copy.73
  512.3 1.3 copy.72
  513.6 0.0 copy-start.2
  513.6 0.0 copy-start.1
  513.6 1.3 copy.71
  514.8 0.0 copy-done.2
  514.8 0.8 copy.76
  515.6 0.0 copy-done.1
  515.6 0.8 copy.77
  (5 shorter events, 0.0 us)
Async XLA Ops:
  506.4 4.0 copy-start
  513.6 1.3 copy-start.2
  513.6 2.1 copy-start.1

commit v5 on v4

--- a/solution.py
+++ b/solution.py
@@ -355,6 +355,16 @@
             copy.wait_recv()
 
 
+def key_positions(key_blocks, index, chunk, piece_rows):
+    pieces = chunk // piece_rows
+    spots = lax.broadcasted_iota(jnp.int32, (chunk, 1), 0)
+    starts = jnp.zeros((chunk, 1), jnp.int32)
+    for piece in range(pieces):
+        start = key_blocks[index * pieces + piece] * piece_rows - piece * piece_rows
+        starts = jnp.where(spots >= piece * piece_rows, start, starts)
+    return spots + starts
+
+
 def front_kernel(
     plane,
     cores,
@@ -367,10 +377,11 @@
     up_weight,
     down_weight,
     gain_block,
+    grad_out,
     cosine,
     sine_turned,
     query_pos,
-    key_pos,
+    key_blocks,
     query_gain,
     key_gain,
     normed_out,
@@ -385,6 +396,7 @@
     gate_out,
     up_out,
     down_out,
+    grad_half_out,
     stats_out,
     gains_out,
     hidden_all,
@@ -425,18 +437,18 @@
         ],
         projection,
     )
-    out_fetch = Fetch(links, place, [(out_weight, out_weight.shape[1], 0, False)], out_full)
+    out_fetch = Fetch(links, place, [], out_full)
     mlp_fetches = [
         Fetch(links, place, [(weight, hidden_units, 0, True)], target)
         for weight, target in ((gate_weight, gate_out), (up_weight, up_out))
     ]
     down_fetch = Fetch(links, place, [(down_weight, hidden_units, 0, True)], down_out, True)
     heads_fetch.begin()
-    out_fetch.begin()
+    mlp_fetches[0].begin()
     heads_fetch.spread()
     hidden_own = links.local(hidden, hidden_all.at[place.z])
     hidden_gather = LineGather(links, place, hidden, lambda z: at(hidden_all)[z])
-    out_fetch.spread()
+    mlp_fetches[0].spread()
     heads_fetch.forward()
     hidden_gather.relay()
     heads_fetch.close()
@@ -444,7 +456,11 @@
     links.keep(projection, projection_out)
     hidden_own.wait()
     hidden_gather.wait()
-    for fetch in mlp_fetches + [down_fetch]:
+    out_fetch.own.append(links.local(out_weight, at(out_full)[place.z, place.column]))
+    out_gather = LineGather(
+        links, place, out_weight, lambda z: at(out_full)[z, place.column]
+    )
+    for fetch in (mlp_fetches[1], down_fetch):
         fetch.begin()
 
     gain_columns = projection[:, :, :, lin_width : lin_width + 128].reshape(width, 128)
@@ -490,11 +506,11 @@
         queries[index] = rope(lin[:, columns], query_gain[...])
     links.keep(lin.at[:, pl.ds(0, query_width + key_width)], lin_out)
     links.keep(queries, queries_out)
-    out_fetch.forward()
+    mlp_fetches[0].forward()
     for copy in both_copies:
         copy.wait_recv()
     links.keep(both, both_out)
-    mlp_fetches[0].spread()
+    out_gather.relay()
 
     factor = head ** (-0.5) * 1.4426950408889634
     chunk = min(256, tokens)
@@ -514,8 +530,8 @@
             keys = both[source, rows, pl.ds(key_head * head, head)]
             values = both[source, rows, pl.ds(key_width + key_head * head, head)]
             scores = multiply_trans(keys, block) * factor
-            spot = pl.ds(pl.multiple_of(index * chunk, chunk), chunk)
-            scores = jnp.where(key_pos[spot] <= positions, scores, masked_score)
+            allowed = key_positions(key_blocks, index, chunk, token_rows // 2) <= positions
+            scores = jnp.where(allowed, scores, masked_score)
             new_best = jnp.maximum(best, jnp.max(scores, axis=0, keepdims=True))
             weights = jnp.exp2(scores - new_best)
             shrink = jnp.exp2(best - new_best)
@@ -547,18 +563,25 @@
             )
         )
         if key_head == 0:
-            out_fetch.close()
+            mlp_fetches[0].close()
+            out_gather.wait()
+            out_fetch.spread()
     links.keep(own_attended, attended_out)
-    mlp_fetches[0].forward()
+    out_fetch.forward()
     mlp_fetches[1].spread()
     for gather in attended_gathers:
         gather.relay()
-    mlp_fetches[0].close()
+    out_fetch.close()
     out_fetch.finish()
     links.keep(out_full, out_columns_out)
     mlp_fetches[1].forward()
     for gather in attended_gathers:
         gather.wait()
+    half = pl.ds(0, width // 2)
+    links.keep(at(grad_out)[:, half], at(grad_half_out)[place.z])
+    grad_gather = LineGather(
+        links, place, at(grad_out)[:, half], lambda z: at(grad_half_out)[z]
+    )
 
     def add_out(index, carry):
         weights = out_full[index].reshape(width // parts, parts * query_width)
@@ -584,16 +607,18 @@
     links.keep(normed_mlp, normed_mlp_out)
     own_rows = place.z_rows[0]
     links.keep(residual.at[own_rows], residual_out)
+    grad_gather.relay()
     mlp_fetches[1].close()
     down_fetch.arrive()
+    grad_gather.wait()
     for fetch in mlp_fetches:
         fetch.finish()
-    for gather in [hidden_gather] + attended_gathers:
+    for gather in [hidden_gather, out_gather, grad_gather] + attended_gathers:
         gather.relayed()
     links.finish()
 
 
-def front(plane, cores, hidden, weights, gain_block, tables, positions, head_gains):
+def front(plane, cores, hidden, weights, gain_block, grad_out, tables, positions, head_gains):
     token_rows, width = hidden.shape
     tokens = parts * token_rows
     shard = weights[0].shape[0]
@@ -619,14 +644,18 @@
         (stacked + (hidden_units,), bf16),
         (stacked + (hidden_units,), bf16),
         ((parts, shard, hidden_units), bf16),
+        ((parts, token_rows, width // 2), bf16),
         ((8, tokens), f32),
         ((8, width), f32),
     ]
     return pl.pallas_call(
         functools.partial(front_kernel, plane, cores),
         out_shape=[jax.ShapeDtypeStruct(shape, kind) for shape, kind in outputs],
-        in_specs=[any_space] * 9 + [vmem] * 6,
-        out_specs=[any_space] * 12 + [vmem] * 2,
+        in_specs=[any_space] * 10
+        + [vmem] * 3
+        + [pl.BlockSpec(memory_space=pltpu.SMEM)]
+        + [vmem] * 2,
+        out_specs=[any_space] * 13 + [vmem] * 2,
         scratch_shapes=[
             pltpu.VMEM((parts, token_rows, width), bf16),
             pltpu.VMEM((tokens, width), bf16),
@@ -647,7 +676,7 @@
             has_side_effects=True, vmem_limit_bytes=60 * 1024 * 1024
         ),
         cost_estimate=pl.CostEstimate(flops=12 * 10**9, bytes_accessed=10**8, transcendentals=10**7),
-    )(hidden, *weights, gain_block, *tables, *positions, *head_gains)
+    )(hidden, *weights, gain_block, grad_out, *tables, *positions, *head_gains)
 
 
 def half_turn(values):
@@ -716,7 +745,7 @@
             self.pending[slot].append(copy.wait_send)
             self.sibling_copies[family, start, index] = copy
 
-    def take(self, family, left, right, start=0):
+    def take(self, family, left, right, start=0, send=True):
         size = right.shape[1]
         columns = pl.ds(start, size)
         loads, kept = [], []
@@ -750,7 +779,8 @@
             for wait in waits:
                 wait()
             waits.clear()
-        self.send_plane(family, columns)
+        if send:
+            self.send_plane(family, columns)
 
     def send_plane(self, family, columns):
         links, place = self.links, self.place
@@ -831,6 +861,7 @@
     gate_in,
     up_in,
     down_in,
+    grad_half_in,
     residual_in,
     projection_in,
     out_in,
@@ -918,9 +949,13 @@
             links.local(gate_in, gate),
             links.local(up_in, up),
             links.local(residual_in, residual),
+            links.local(grad_half_in, at(low_rows)[:, :, pl.ds(0, width // 2)]),
         ]
-        low_rows[place.z] = grad_out[...]
-        gathers.append(LineGather(links, place, grad_out, lambda z: at(low_rows)[z]))
+        half = pl.ds(width // 2, width // 2)
+        low_rows[place.z, :, half] = grad_out[:, half]
+        gathers.append(
+            LineGather(links, place, at(grad_out)[:, half], lambda z: at(low_rows)[z, :, half])
+        )
         own_down.wait()
         down_fetch = Fetch(links, place, [], down)
         down_fetch.spread()
@@ -939,8 +974,10 @@
             d_gate[:, columns] = (up_lin * (sigmoid + silu * (1.0 - sigmoid))).astype(bf16)
             return carry
 
-        lax.fori_loop(0, units // tile, hidden_tile, 0)
+        middle = units // tile // 2
+        lax.fori_loop(0, middle, hidden_tile, 0)
         gathers[0].relay()
+        lax.fori_loop(middle, units // tile, hidden_tile, 0)
         down_fetch.forward()
         for copy in loads[3:]:
             copy.wait()
@@ -1001,7 +1038,7 @@
         returns.take(1, turned_left, d_up)
         gathers[1].relay()
         returns.give(2, turned_right, act)
-        returns.take(2, turned_right, act)
+        returns.take(2, turned_right, act, send=False)
         for copy in in_sum.sent():
             copy.wait_send()
 
@@ -1071,13 +1108,9 @@
                 keys = both[source, rows, pl.ds(key_head * head, head)]
                 values = both[source, rows, pl.ds(key_width + key_head * head, head)]
                 scores = multiply_trans(keys, query_block) * score_factor
-                spots = lax.broadcasted_iota(jnp.int32, (chunk, 1), 0)
-                starts = jnp.zeros((chunk, 1), jnp.int32)
-                for piece in range(chunk // piece_rows):
-                    start = key_blocks[index * (chunk // piece_rows) + piece] * piece_rows
-                    starts = jnp.where(spots >= piece * piece_rows, start - piece * piece_rows, starts)
+                places = key_positions(key_blocks, index, chunk, piece_rows)
                 weights = jnp.where(
-                    spots + starts <= positions, jnp.exp2(scores - stats_row), 0.0
+                    places <= positions, jnp.exp2(scores - stats_row), 0.0
                 )
                 grad_weights = multiply_trans(values, grad_block)
                 grad_scores = (weights * (grad_weights - delta_row)).astype(bf16)
@@ -1134,15 +1167,17 @@
         returns.give(3, turned_right, attended, query_width)
         query_lin = at(grad_lin)[:, pl.ds(0, query_width)].get()
         returns.give(3, turned_left, query_lin)
-        returns.take(3, turned_right, attended, query_width)
+        returns.take(3, turned_right, attended, query_width, send=False)
         returns.along_z(0, all_units)
-        returns.take(3, turned_left, query_lin)
-        returns.along_z(1, all_units)
+        returns.take(3, turned_left, query_lin, send=False)
 
         for copy in both_copies:
             copy.wait_recv()
         for copy in both_own:
             copy.wait()
+        returns.send_plane(2, all_units)
+        returns.send_plane(3, pl.ds(query_width, query_width))
+        returns.send_plane(3, pl.ds(0, query_width))
 
         def load_both(source):
             return Copy(
@@ -1188,9 +1223,9 @@
         landed_in[place.z] = part_in[own_rows]
         both_lin = at(grad_lin)[:, pl.ds(query_width, 2 * key_width)].get()
         returns.give(4, turned_left, both_lin)
+        returns.along_z(1, all_units)
         back_sum.combine()
         returns.take(4, turned_left, both_lin)
-        returns.along_z(2, all_units)
         for copy in both_copies:
             copy.wait_send()
 
@@ -1226,6 +1261,7 @@
         for step in z_steps
     ]
     z_messages[place.z] = messages[place.z]
+    returns.along_z(2, all_units)
     out_sum.wait()
     output[...] = (residual[...] + total_of(landed_out)).astype(bf16)
     for copy in copies:
@@ -1264,7 +1300,7 @@
 
 def rear(plane, cores, large, small):
     normed_mlp, gate = large[0], large[1]
-    projection, lin, queries, both = large[5], large[8], large[9], large[10]
+    projection, lin, queries, both = large[6], large[9], large[10], large[11]
     tokens, width = normed_mlp.shape
     token_rows = tokens // parts
     _, columns, shard, units = gate.shape
@@ -1292,7 +1328,7 @@
     return pl.pallas_call(
         functools.partial(rear_kernel, plane, cores),
         out_shape=[jax.ShapeDtypeStruct(shape, kind) for shape, kind in shapes],
-        in_specs=[any_space] * 12
+        in_specs=[any_space] * 13
         + [vmem] * 7
         + [pl.BlockSpec(memory_space=pltpu.SMEM)]
         + [vmem] * 2,
@@ -1363,7 +1399,7 @@
         all_pos = blocks.transpose(1, 0, 2)[..., None] * piece_rows + offsets
         all_pos = all_pos.reshape(plane, tokens)
         query_pos = lax.dynamic_index_in_dim(all_pos, p_index, 0, keepdims=False)
-        key_pos = all_pos.reshape(-1)
+        key_blocks = blocks.transpose(1, 0, 2).reshape(-1)
         cosine, sine_table = rope_tables(query_pos, head_width)
         sign = jnp.where(jnp.arange(head_width) < head_width // 2, -1.0, 1.0).astype(f32)
         query_gain_float = query_gain.astype(f32)
@@ -1384,6 +1420,7 @@
             gate_columns,
             up_columns,
             down_columns,
+            grad_half,
             stats,
             gains,
         ) = front(
@@ -1400,8 +1437,9 @@
                 down_weight,
             ),
             gain_block,
+            grad_own,
             (cosine[:, 0], sine_table[:, 0] * sign),
-            (query_pos[None], key_pos[:, None]),
+            (query_pos[None], key_blocks),
             (query_gain_float[None], key_gain_float[None]),
         )
         results = rear(
@@ -1412,6 +1450,7 @@
                 gate_columns,
                 up_columns,
                 down_columns,
+                grad_half,
                 own_residual,
                 projection,
                 out_full,
@@ -1429,7 +1468,7 @@
                 cosine[:, 0],
                 sine_table[:, 0] * sign,
                 query_pos[None],
-                blocks.transpose(1, 0, 2).reshape(-1),
+                key_blocks,
                 query_gain_float[None],
                 key_gain_float[None],
             ),

time: 523 us -> 511 us (0.977)
  Pallas kernels: 491 us -> 482 us
    pallas_call x1, Pallas kernels: 300 us -> 291 us  [rear(): pl.pallas_call(functools.partial(rear_kernel, plane, cores), out_shape=[j...]
where the time goes in v5:
time: 511 us; the launch traced here: 505 us
  Pallas kernels  482 us (94%)
  local copies, waits for them, and re-layouts  13.5 us (3%)
  other arithmetic  9 us (2%)
    pallas_call x1, Pallas kernels, rear(): pl.pallas_call(functools.partial(rear_kernel, plane, cores), out_shape=[j...  291 us
    pallas_call x1, Pallas kernels, front(): pl.pallas_call(functools.partial(front_kernel, plane, cores), out_shape=[...  190 us

profile of v5, /device:TPU:0, one launch (start us, length us, event | category | flops | bytes accessed | tf_op | source)
XLA Modules:
  0.0 505.0 jit_solution(8503477581015810367)
XLA Ops:
  0.7 0.5 broadcast.33
  1.2 1.3 reduce.3
  2.5 0.7 pad_maximum_fusion.1
  3.2 1.2 bitcast_convert_fusion
  4.4 0.1 add.35
  4.5 0.1 reshape_squeeze.3
  4.6 0.1 copy.53
  4.7 0.1 copy.54
  4.8 0.1 add.32
  4.9 0.1 add.33
  5.0 0.6 fusion.1
  5.6 0.6 reshape.107.key_blocks
  6.2 0.1 copy.52
  6.3 0.6 pad.4.gain_block
  6.9 0.1 broadcast_multiply_fusion
  7.0 1.8 sine_multiply_fusion
  8.9 190.3 %shard_map.237 = (bf16[512,2048]{1,0:T(8,128)(2,1)}, bf16[4,8,64,1152]{3,2,1,0:T(8,128)(2,1)}, f32[512,768]{1,0:T(8,128)}, bf16[4,512,128]{2,1,0:T(8,128)(2,1)},...) custom-call(bf16[128,2048]{1,0:T(8,128)(2,1)} %bitcast.84, ...), custom_call_target="tpu_custom_call" | custom-call | flops 12000000000 | bytes 100000000 | tf_op jit(solution)/shard_map/pallas_call | solution.py:651
  199.2 291.2 %shard_map.238 = (bf16[128,2048]{1,0:T(8,128)(2,1)}, bf16[128,2048]{1,0:T(8,128)(2,1)}, f32[8,640]{1,0:T(8,128)}, bf16[5,4,4,64,1536]{4,3,2,1,0:T(8,128)(2,1)}, ...) custom-call(bf16[512,2048]{1,0:T(8,128)(2,1)} %get-tuple-element.32., ...), custom_call_target="tpu_custom_call" | custom-call | flops 40000000000 | bytes 100000000 | tf_op jit(solution)/shard_map/pallas_call | solution.py:1328
  490.4 1.3 slice_bitcast_fusion
  491.7 0.7 slice.46
  492.4 0.1 constant_dynamic-slice_fusion
  492.4 0.5 slice_bitcast_fusion.2
  493.0 1.0 convert_bitcast_fusion.5
  494.0 0.7 copy.66
  494.7 0.0 copy-start
  494.7 0.7 copy.65
  495.4 1.6 convert_bitcast_fusion.3
  497.0 0.8 copy.67
  497.9 0.8 copy.64
  498.7 0.0 copy-done
  498.7 0.6 convert_bitcast_fusion
  499.4 1.3 copy.70
  500.6 1.3 copy.69
  501.9 0.0 copy-start.2
  501.9 0.0 copy-start.1
  501.9 1.3 copy.68
  503.2 0.0 copy-done.2
  503.2 0.8 copy.73
  504.0 0.0 copy-done.1
  504.0 0.8 copy.74
  (5 shorter events, 0.0 us)
Async XLA Ops:
  494.7 4.0 copy-start
  501.9 1.3 copy-start.2
  501.9 2.1 copy-start.1

commit v6 on v5

--- a/solution.py
+++ b/solution.py
@@ -1396,16 +1396,17 @@
 
         blocks = block_map[0].reshape(parts, plane, 2)
         offsets = jnp.arange(piece_rows, dtype=jnp.int32)
-        all_pos = blocks.transpose(1, 0, 2)[..., None] * piece_rows + offsets
-        all_pos = all_pos.reshape(plane, tokens)
-        query_pos = lax.dynamic_index_in_dim(all_pos, p_index, 0, keepdims=False)
+        own_blocks = lax.dynamic_slice_in_dim(blocks, p_index, 1, 1)
+        query_pos = (own_blocks.reshape(-1, 1) * piece_rows + offsets).reshape(tokens)
         key_blocks = blocks.transpose(1, 0, 2).reshape(-1)
         cosine, sine_table = rope_tables(query_pos, head_width)
         sign = jnp.where(jnp.arange(head_width) < head_width // 2, -1.0, 1.0).astype(f32)
         query_gain_float = query_gain.astype(f32)
         key_gain_float = key_gain.astype(f32)
-        gain_block = jnp.stack([attention_norm_gain, feedforward_gain], axis=1)
-        gain_block = jnp.pad(gain_block, ((0, 0), (0, 126)))
+        lanes = lax.broadcasted_iota(jnp.int32, (shard, 128), 1)
+        gain_block = jnp.where(
+            lanes == 0, attention_norm_gain[:, None], feedforward_gain[:, None]
+        )
 
         (
             normed,

time: 511 us -> 511 us (level)
  no operation moved by 1% of the time
where the time goes in v6:
time: 511 us; the launch traced here: 505 us
  Pallas kernels  481 us (94%)
  local copies, waits for them, and re-layouts  13.2 us (3%)
  other arithmetic  9.19 us (2%)
    pallas_call x1, Pallas kernels, rear(): pl.pallas_call(functools.partial(rear_kernel, plane, cores), out_shape=[j...  291 us
    pallas_call x1, Pallas kernels, front(): pl.pallas_call(functools.partial(front_kernel, plane, cores), out_shape=[...  190 us

profile of v6, /device:TPU:0, one launch (start us, length us, event | category | flops | bytes accessed | tf_op | source)
XLA Modules:
  0.0 504.8 jit_solution(8694877352931062557)
XLA Ops:
  0.7 0.5 broadcast.51
  1.2 1.3 reduce.7
  2.5 1.2 bitcast_convert_fusion
  3.7 0.1 reshape_squeeze.3
  3.8 0.1 mul.46
  3.9 0.1 iota_add_fusion
  4.0 0.7 add.42.query_pos
  4.6 0.1 convert_element_type.62
  4.7 0.6 reshape.145.key_blocks
  5.3 1.4 broadcast_select_fusion.gain_block
  6.7 0.1 broadcast_multiply_fusion
  6.8 1.8 sine_multiply_fusion
  8.7 190.3 %shard_map.237 = (bf16[512,2048]{1,0:T(8,128)(2,1)}, bf16[4,8,64,1152]{3,2,1,0:T(8,128)(2,1)}, f32[512,768]{1,0:T(8,128)}, bf16[4,512,128]{2,1,0:T(8,128)(2,1)},...) custom-call(bf16[128,2048]{1,0:T(8,128)(2,1)} %bitcast.78, ...), custom_call_target="tpu_custom_call" | custom-call | flops 12000000000 | bytes 100000000 | tf_op jit(solution)/shard_map/pallas_call | solution.py:651
  199.0 291.2 %shard_map.238 = (bf16[128,2048]{1,0:T(8,128)(2,1)}, bf16[128,2048]{1,0:T(8,128)(2,1)}, f32[8,640]{1,0:T(8,128)}, bf16[5,4,4,64,1536]{4,3,2,1,0:T(8,128)(2,1)}, ...) custom-call(bf16[512,2048]{1,0:T(8,128)(2,1)} %get-tuple-element.32., ...), custom_call_target="tpu_custom_call" | custom-call | flops 40000000000 | bytes 100000000 | tf_op jit(solution)/shard_map/pallas_call | solution.py:1328
  490.2 1.3 slice_bitcast_fusion
  491.4 0.7 slice.46
  492.2 0.1 constant_dynamic-slice_fusion
  492.2 0.5 slice_bitcast_fusion.2
  492.8 1.0 convert_bitcast_fusion.5
  493.8 0.7 copy.38
  494.5 0.0 copy-start
  494.5 0.7 copy.37
  495.2 1.6 convert_bitcast_fusion.3
  496.8 0.8 copy.39
  497.7 0.8 copy.36
  498.5 0.0 copy-done
  498.5 0.6 convert_bitcast_fusion
  499.2 1.3 copy.42
  500.4 1.3 copy.41
  501.7 0.0 copy-start.2
  501.7 0.0 copy-start.1
  501.7 1.3 copy.40
  503.0 0.0 copy-done.2
  503.0 0.8 copy.45
  503.8 0.0 copy-done.1
  503.8 0.8 copy.46
  (5 shorter events, 0.1 us)
Async XLA Ops:
  494.5 4.0 copy-start
  501.7 1.3 copy-start.2
  501.7 2.1 copy-start.1
